TPU v7x, 32 devices: a whole 2x2x4 slice. The times are simulated.
32 devices in a mesh: gx: 4 (over y, x), gy: 4 (over z), gz: 2 (over core).
Axes of the slice: x: 2, y: 2, z: 4, core: 2. Of those that a mesh axis runs over, the one named last changes fastest.
Arguments:
- u_now: float32 [3, 64, 64, 256], P(None, 'gx', 'gy', 'gz'), may hold values from -6 to 6
- u_prev: float32 [3, 64, 64, 256], P(None, 'gx', 'gy', 'gz'), may hold values from -6 to 6
- panels: bfloat16 [4, 2, 64, 48, 256], P('gx', 'gz', 'gy'), may hold values from -6 to 6
- panel_owner: int32 [4, 2, 64, 1], P('gx', 'gz'), may hold values from 0 to 3; in each aligned block of 16 rows (0 to 15, 16 to 31, ..., all dimensions but the last counted through in order) at most 8 rows name the same one
- panel_block: int32 [4, 2, 64], P('gx', 'gz'), may hold values from 0 to 2047
- coupling: float32 [3, 16, 16], replicated, may hold values from -1.5 to 1.5
- layer_depth: int32 [256], P('gz'), may hold values from 0 to 7, never falling along the last dimension, each value on 1 to 64 neighbouring positions
- layer_speed: float32 [8], replicated, may hold values from 0.04 to 0.3
- lateral: float32 [64, 64, 256], P('gx', 'gy', 'gz'), may hold values from 0.5 to 1
Outputs:
- u_final: float32 [3, 64, 64, 256], P(None, 'gx', 'gy', 'gz')
- u_before: float32 [3, 64, 64, 256], P(None, 'gx', 'gy', 'gz')
Inputs may be any that keep to these rules, and one draw needn't show every extreme that they name: `panel_owner`: among the 16 panels of one device (an aligned block of rows) at most 8 have the same owner; in each draw some owner receives exactly 8 from some device. `layer_depth`: layers never decrease with depth; each layer spans 1 to 64 depths.
All inputs are finite; a program needn't handle non-finite values.
Results may differ from a plain program's by a relative error of at most 0.00038.
Values may be sent and summed in bfloat16 or wider, within the bound.
No kernel may reach another device: no remote copies, remote signals or barrier semaphores. Data moves between devices by JAX's collectives and lax.ppermute only.
A program may use at most 64 MiB of HBM per device.

v0:
```python
import jax
import jax.numpy as jnp
from jax import lax
from jax.sharding import PartitionSpec as P

NSTEP = 4


def extended(shard, sides, width):
    for axis, dim in sides:
        peers, length = (lax.axis_size(axis), shard.shape[dim])
        up = [(i, (i + 1) % peers) for i in range(peers - 1)]
        down = [(j, i) for i, j in up]
        last = lax.slice_in_dim(shard, length - width, length, axis=dim)
        leading = lax.slice_in_dim(shard, 0, width, axis=dim)
        before = lax.ppermute(last, axis, up)
        after = lax.ppermute(leading, axis, down)
        shard = jnp.concatenate([before, shard, after], axis=dim)
    return shard


def wave_table(count):
    half = count // 2
    freq = 2.0 * jnp.pi * (jnp.arange(half, dtype=jnp.float32) + 0.5) / count
    times = 37.0 + jnp.arange(NSTEP, dtype=jnp.float32)
    phase = freq[:, None] * times[None, :]
    table = jnp.concatenate([jnp.cos(phase), jnp.sin(phase)], axis=0) / jnp.sqrt(jnp.float32(half))
    return table.astype(jnp.bfloat16)


def trim_rim(field, width):
    return field[..., width:-width, width:-width, width:-width]


def neighbours(padded, center):
    beside = padded[:, 2:, 1:-1, 1:-1] + padded[:, :-2, 1:-1, 1:-1]
    beside = beside + padded[:, 1:-1, 2:, 1:-1] + padded[:, 1:-1, :-2, 1:-1]
    beside = beside + padded[:, 1:-1, 1:-1, 2:] + padded[:, 1:-1, 1:-1, :-2]
    return beside - 6.0 * center


def per_device(
    u_now, u_prev, panels, panel_owner, panel_block, coupling, layer_depth, layer_speed, lateral
):
    width_gy = lax.axis_size("gy")
    mine = lax.axis_index("gy")
    per_dev = panels.shape[2]
    block_len = coupling.shape[1]
    spectral = panels.shape[4]
    capacity = max(2, 2 * per_dev // width_gy)
    comps, size_x, size_y, size_z = u_now.shape
    zblocks = size_z // block_len
    nblocks = size_x * size_y * zblocks
    table = wave_table(spectral)
    owners = panel_owner.reshape(width_gy, per_dev)
    blocks = panel_block.reshape(width_gy, per_dev)
    target = jnp.arange(width_gy, dtype=jnp.int32)
    hits = (owners[:, :, None] == target[None, None, :]).astype(jnp.int32)
    earlier = jnp.cumsum(hits, axis=1) - hits
    ranks = jnp.sum(earlier * hits, axis=2)
    slot_ids = jnp.arange(capacity, dtype=jnp.int32)
    my_owner = lax.dynamic_index_in_dim(owners, mine, 0, keepdims=False)
    my_rank = lax.dynamic_index_in_dim(ranks, mine, 0, keepdims=False)
    send_pick = (my_owner[None, None, :] == target[:, None, None]) & (
        my_rank[None, None, :] == slot_ids[None, :, None]
    )
    send_pick = send_pick.reshape(width_gy * capacity, per_dev)
    recv_pick = (
        (owners[:, None, :] == mine) & (ranks[:, None, :] == slot_ids[None, :, None])
    ).astype(jnp.int32)
    slot_block = jnp.sum(recv_pick * blocks[:, None, :], axis=2).reshape(-1)
    slot_valid = jnp.sum(recv_pick, axis=2).reshape(-1)
    free = jnp.einsum(
        "skt,tn->skn",
        panels.reshape(per_dev, 3 * block_len, spectral),
        table,
        preferred_element_type=jnp.float32,
    )
    free = free.reshape(-1, 3, block_len, NSTEP)
    force = jnp.einsum("cij,scjn->scin", coupling, free, precision=lax.Precision.HIGHEST)
    own = force.reshape(force.shape[0], 3 * block_len * NSTEP)
    outgoing = jnp.dot(send_pick.astype(jnp.float32), own, precision=lax.Precision.HIGHEST)
    outgoing = outgoing.reshape(width_gy, capacity, 3 * block_len * NSTEP)
    forces = lax.all_to_all(outgoing, "gy", split_axis=0, concat_axis=0, tiled=True)
    placing = (
        (slot_block[:, None] == jnp.arange(nblocks, dtype=jnp.int32)[None, :])
        & (slot_valid[:, None] > 0)
    ).astype(jnp.float32)
    gathered = jnp.einsum(
        "sb,sf->bf",
        placing,
        forces.reshape(width_gy * capacity, -1),
        precision=lax.Precision.HIGHEST,
    )
    gathered = gathered.reshape(size_x, size_y, zblocks, 3, block_len, NSTEP)
    drive_all = jnp.transpose(gathered, (5, 3, 0, 1, 2, 4)).reshape(
        NSTEP, 3, size_x, size_y, size_z
    )
    layers = jnp.arange(layer_speed.shape[0], dtype=jnp.int32)
    speed_z = jnp.sum(
        (layer_depth[None, :] == layers[:, None]).astype(jnp.float32) * layer_speed[:, None], axis=0
    )
    rate = lateral * speed_z[None, None, :]
    stacked = jnp.concatenate(
        [u_now, u_prev, rate[None], drive_all.reshape(NSTEP * 3, size_x, size_y, size_z)], axis=0
    )
    wide = extended(stacked, (("gx", 1), ("gy", 2), ("gz", 3)), NSTEP)
    current = wide[0:3]
    older = wide[3:6]
    rate_wide = wide[6]
    drive_wide = wide[7:].reshape(
        NSTEP, 3, size_x + 2 * NSTEP, size_y + 2 * NSTEP, size_z + 2 * NSTEP
    )
    for step in range(NSTEP):
        inner = trim_rim(current, 1)
        laplace = neighbours(current, inner)
        u_next = (
            2.0 * inner
            - trim_rim(older, 1)
            + trim_rim(rate_wide, step + 1)[None] * laplace
            + trim_rim(drive_wide[step], step + 1)
        )
        older = inner
        current = u_next
    u_now = current
    u_prev = older
    return (u_now, u_prev)


def solution(mesh):
    in_specs = (
        P(None, "gx", "gy", "gz"),
        P(None, "gx", "gy", "gz"),
        P("gx", "gz", "gy", None, None),
        P("gx", "gz", None, None),
        P("gx", "gz", None),
        P(),
        P("gz"),
        P(),
        P("gx", "gy", "gz"),
    )
    out_specs = (P(None, "gx", "gy", "gz"), P(None, "gx", "gy", "gz"))
    return jax.shard_map(
        per_device, mesh=mesh, in_specs=in_specs, out_specs=out_specs, check_vma=False
    )
```

profile of v0, /device:TPU:12, one launch (start us, length us, event | category | flops | bytes accessed | tf_op | source)
XLA Modules:
  0.0 178.4 jit_solution(4613944878309893126)
XLA Ops:
  0.6 0.0 copy-start
  0.7 0.5 broadcast.125
  1.2 1.3 reduce.7
  2.5 0.1 broadcast_in_dim_reshape.2
  2.6 0.1 fusion.22
  2.7 0.2 select_reduce_fusion
  2.9 0.1 multiply_cosine_fusion
  3.1 0.0 copy-done
  3.1 0.3 convolution_bitcast_fusion.2
  3.3 0.1 reshape.155
  3.5 1.0 convolution_bitcast_fusion.1
  4.5 0.1 copy.34
  4.6 0.8 fusion.25
  5.4 5.3 %all-to-all-start = ((f32[4,8,192]{2,1,0:T(8,128)}), f32[4,8,192]{2,1,0:T(8,128)S(1)}, u32[]{:S(2)}, u32[]{:S(2)}) async-start(f32[4,8,192]{2,1,0:T(8,128)} %fusion.25), calls=%async_computation | async-start | bytes 65536 | tf_op jit(solution)/shard_map/all_to_all | solution.py:84
  10.8 1.3 reduce.6
  12.1 0.1 mul.136
  12.2 0.2 convert_reduce_fusion
  12.4 0.8 select_reduce_fusion.2
  13.2 0.9 multiply_bitcast_fusion
  14.1 0.1 eq.138
  14.2 0.1 gt.16
  14.3 0.9 all-to-all-done
  15.1 0.1 copy.36
  15.2 8.0 %convolution_bitcast_fusion = f32[4,3,16,16,8,16]{5,3,0,1,4,2:T(8,128)} fusion(s32[16,16,8]{1,2,0:T(8,128)S(1)} %multiply_add_fusion, s32[32]{0:T(128)S(1)} %eq.138, pred[32]{0:T(512)(128)(4,1)S(1)} %gt.16, f32[3,16,4,32,1,1]{3,2,1,0,5,4:T(4,128)S(1)} %bitcast.47), kind=kOutput, calls=%fused_computation.2 | convolution fusion | flops 151126016 | bytes 1605792 | tf_op jit(solution)/shard_map/sb,sf->bf/dot_general | solution.py:89
  23.3 16.3 %copy.38 = f32[4,3,16,16,8,16]{5,4,3,2,1,0:T(8,128)} copy(f32[4,3,16,16,8,16]{5,3,0,1,4,2:T(8,128)} %convolution_bitcast_fusion) | data formatting | bytes 3145728 | tf_op jit(solution)/shard_map/transpose | solution.py:96
  39.6 8.0 %reshape_reshape.3 = f32[12,16,16,128]{3,2,1,0:T(8,128)S(1)} reshape(f32[4,3,16,16,8,16]{5,4,3,2,1,0:T(8,128)} %copy.38) | data formatting | bytes 3145728 | tf_op jit(solution)/shard_map/reshape;reshape | solution.py:105
  47.6 0.0 copy-done.2
  47.6 0.0 copy-done.3
  47.6 0.1 pad_maximum_fusion.11
  47.7 3.3 %collective-permute-start.1 = (f32[19,4,16,128]{3,2,1,0:T(8,128)S(1)}, f32[19,4,16,128]{3,2,1,0:T(8,128)S(1)}, u32[]{:S(2)}, u32[]{:S(2)}) collective-permute-start(f32[19,4,16,128]{3,2,1,0:T(8,128)S(1)} %get-tuple-element.11), channel_id=1, source_target_pairs={{8,0},{16,8},{24,16},{9,1},{17,9},{25,17},{10,2},{18,10},{26,18},{... | collective-permute-start | bytes 1867784 | tf_op jit(solution)/shard_map/ppermute | solution.py:17
  51.1 2.7 %collective-permute-start = (f32[19,4,16,128]{3,2,1,0:T(8,128)S(1)}, f32[19,4,16,128]{3,2,1,0:T(8,128)S(1)}, u32[]{:S(2)}, u32[]{:S(2)}) collective-permute-start(f32[19,4,16,128]{3,2,1,0:T(8,128)S(1)} %get-tuple-element.10), channel_id=1, source_target_pairs={{0,8},{8,16},{16,24},{1,9},{9,17},{17,25},{2,10},{10,18},{18,26},{... | collective-permute-start | bytes 1867784 | tf_op jit(solution)/shard_map/ppermute | solution.py:16
  53.8 11.7 %collective-permute-done.1 = f32[19,4,16,128]{3,2,1,0:T(8,128)S(1)} collective-permute-done((f32[19,4,16,128]{3,2,1,0:T(8,128)S(1)}, f32[19,4,16,128]{3,2,1,0:T(8,128)S(1)}, u32[]{:S(2)}, u32[]{:S(2)}) %collective-permute-start.1) | collective-permute-done | bytes 622624 | tf_op jit(solution)/shard_map/ppermute | solution.py:17
  65.5 11.7 %collective-permute-done = f32[19,4,16,128]{3,2,1,0:T(8,128)S(1)} collective-permute-done((f32[19,4,16,128]{3,2,1,0:T(8,128)S(1)}, f32[19,4,16,128]{3,2,1,0:T(8,128)S(1)}, u32[]{:S(2)}, u32[]{:S(2)}) %collective-permute-start) | collective-permute-done | bytes 622624 | tf_op jit(solution)/shard_map/ppermute | solution.py:16
  77.2 0.5 pad_maximum_fusion.7
  77.8 3.2 %collective-permute-start.3 = (f32[19,24,4,128]{3,2,1,0:T(4,128)S(1)}, f32[19,24,4,128]{3,2,1,0:T(4,128)S(1)}, u32[]{:S(2)}, u32[]{:S(2)}) collective-permute-start(f32[19,24,4,128]{3,2,1,0:T(4,128)S(1)} %get-tuple-element.9), channel_id=1, source_target_pairs={{2,0},{4,2},{6,4},{3,1},{5,3},{7,5},{10,8},{12,10},{14,12},{11,9},... | collective-permute-start | bytes 2801672 | tf_op jit(solution)/shard_map/ppermute | solution.py:17
  81.0 2.7 %collective-permute-start.2 = (f32[19,24,4,128]{3,2,1,0:T(4,128)S(1)}, f32[19,24,4,128]{3,2,1,0:T(4,128)S(1)}, u32[]{:S(2)}, u32[]{:S(2)}) collective-permute-start(f32[19,24,4,128]{3,2,1,0:T(4,128)S(1)} %get-tuple-element.8), channel_id=1, source_target_pairs={{0,2},{2,4},{4,6},{1,3},{3,5},{5,7},{8,10},{10,12},{12,14},{9,11},... | collective-permute-start | bytes 2801672 | tf_op jit(solution)/shard_map/ppermute | solution.py:16
  83.6 16.7 %collective-permute-done.3 = f32[19,24,4,128]{3,2,1,0:T(4,128)S(1)} collective-permute-done((f32[19,24,4,128]{3,2,1,0:T(4,128)S(1)}, f32[19,24,4,128]{3,2,1,0:T(4,128)S(1)}, u32[]{:S(2)}, u32[]{:S(2)}) %collective-permute-start.3) | collective-permute-done | bytes 933920 | tf_op jit(solution)/shard_map/ppermute | solution.py:17
  100.4 2.3 %collective-permute-done.2 = f32[19,24,4,128]{3,2,1,0:T(4,128)S(1)} collective-permute-done((f32[19,24,4,128]{3,2,1,0:T(4,128)S(1)}, f32[19,24,4,128]{3,2,1,0:T(4,128)S(1)}, u32[]{:S(2)}, u32[]{:S(2)}) %collective-permute-start.2) | collective-permute-done | bytes 933920 | tf_op jit(solution)/shard_map/ppermute | solution.py:16
  102.7 0.0 copy-done.4
  102.7 1.0 copy-done.6
  103.7 3.1 %pad_maximum_fusion.1 = f32[19,24,24,128]{3,2,1,0:T(8,128)S(1)} fusion(f32[19,24,4,128]{3,2,1,0:T(4,128)S(1)} %collective-permute-done.3, f32[19,4,16,128]{3,2,1,0:T(8,128)S(1)} %collective-permute-done.1, f32[12,16,16,128]{3,2,1,0:T(8,128)S(1)} %reshape_reshape.3, f32[1,16,16,128]{3,2,1,0:T(8,128)S(1)} %multiply_bitcast_fusion, ...), kind=kLoop, calls=%fused_computation.1 | loop fusion | flops 9805824 | bytes 11206656 | tf_op jit(solution)/shard_map/concatenate | solution.py:18
  106.8 0.0 copy-done.5
  106.8 6.2 %fusion.35 = (f32[19,24,24,4]{3,2,1,0:T(8,128)}, f32[19,24,24,4]{3,2,1,0:T(8,128)}) fusion(f32[19,24,24,128]{3,2,1,0:T(8,128)S(1)} %pad_maximum_fusion.1), kind=kLoop, calls=%fused_computation.97 | loop fusion | bytes 700416 | tf_op jit(solution)/shard_map/slice | solution.py:14
  112.9 5.9 %copy.40 = f32[19,24,24,4]{2,1,3,0:T(8,128)} copy(f32[19,24,24,4]{3,2,1,0:T(8,128)} %get-tuple-element.7) | data formatting | bytes 350208 | tf_op jit(solution)/shard_map/slice | solution.py:15
  118.8 1.3 collective-permute-start.5
  120.1 5.9 %copy.39 = f32[19,24,24,4]{2,1,3,0:T(8,128)} copy(f32[19,24,24,4]{3,2,1,0:T(8,128)} %get-tuple-element.6) | data formatting | bytes 350208 | tf_op jit(solution)/shard_map/slice | solution.py:14
  126.0 5.2 %collective-permute-start.4 = (f32[19,24,24,4]{2,1,3,0:T(8,128)}, f32[19,24,24,4]{2,1,3,0:T(8,128)}, u32[]{:S(2)}, u32[]{:S(2)}) collective-permute-start(f32[19,24,24,4]{2,1,3,0:T(8,128)} %copy.39), channel_id=1, source_target_pairs={{0,1},{2,3},{4,5},{6,7},{8,9},{10,11},{12,13},{14,15},{16,17},{18,... | collective-permute-start | bytes 525320 | tf_op jit(solution)/shard_map/ppermute | solution.py:16
  131.1 0.0 slice-done
  131.2 3.1 %copy.43 = f32[1,3,16,16,8,16]{5,4,3,2,1,0:T(8,128)} copy(f32[1,3,16,16,8,16]{5,3,0,1,4,2:T(8,128)S(1)} %slice-done) | data formatting | bytes 786432 | tf_op jit(solution)/shard_map/slice | solution.py:32
  134.2 2.4 %slice.225 = f32[3,16,16,128]{3,2,1,0:T(8,128)S(1)} reshape(f32[1,3,16,16,8,16]{5,4,3,2,1,0:T(8,128)} %copy.43) | data formatting | bytes 786432 | tf_op jit(solution)/shard_map/slice | solution.py:32
  136.6 0.0 collective-permute-done.5
  136.6 5.4 %copy.42 = f32[19,24,24,4]{3,2,1,0:T(8,128)} copy(f32[19,24,24,4]{2,1,3,0:T(8,128)} %collective-permute-done.5) | data formatting | bytes 350208 | tf_op jit(solution)/shard_map/ppermute | solution.py:17
  142.0 0.0 collective-permute-done.4
  142.0 5.4 %copy.41 = f32[19,24,24,4]{3,2,1,0:T(8,128)} copy(f32[19,24,24,4]{2,1,3,0:T(8,128)} %collective-permute-done.4) | data formatting | bytes 350208 | tf_op jit(solution)/shard_map/ppermute | solution.py:16
  147.4 19.1 %pad_maximum_fusion = f32[19,24,24,136]{3,2,1,0:T(8,128)S(1)} fusion(f32[19,24,24,4]{3,2,1,0:T(8,128)} %copy.42, f32[19,24,4,128]{3,2,1,0:T(4,128)} %copy-done.5, f32[19,4,16,128]{3,2,1,0:T(8,128)S(1)} %collective-permute-done.1, f32[12,16,16,128]{3,2,1,0:T(8,128)S(1)} %reshape_reshape.3, f32[1,16,16,128]{3,2,1,0:T(8,128)S(1)} %multiply_bitcast_fusion, ...), kind=kLoop, calls=%fused_computation | loop fusion | flops 13395456 | bytes 11907072 | tf_op jit(solution)/shard_map/concatenate | solution.py:18
  166.6 0.2 slice.231
  166.9 0.2 slice.241
  167.1 0.2 slice.251
  167.3 0.1 slice.261
  167.4 3.4 %slice_add_fusion = f32[3,22,22,134]{3,2,1,0:T(8,128)S(1)} fusion(f32[19,24,24,136]{3,2,1,0:T(8,128)S(1)} %pad_maximum_fusion, f32[22,22,134]{2,1,0:T(8,128)S(1)} %slice.231), kind=kLoop, calls=%fused_computation.3 | loop fusion | flops 2334816 | bytes 8042144 | tf_op jit(solution)/shard_map/add | solution.py:118
  170.8 3.1 %slice_add_fusion.6 = f32[3,20,20,132]{3,2,1,0:T(8,128)S(1)} fusion(f32[19,24,24,136]{3,2,1,0:T(8,128)S(1)} %pad_maximum_fusion, f32[3,22,22,134]{3,2,1,0:T(8,128)S(1)} %slice_add_fusion, f32[20,20,132]{2,1,0:T(8,128)S(1)} %slice.241), kind=kLoop, calls=%fused_computation.13 | loop fusion | flops 1900800 | bytes 6547200 | tf_op jit(solution)/shard_map/add | solution.py:118
  173.9 0.0 copy-start.1
  173.9 2.8 %slice_add_fusion.12 = f32[3,18,18,130]{3,2,1,0:T(8,128)S(1)} fusion(f32[19,24,24,136]{3,2,1,0:T(8,128)S(1)} %pad_maximum_fusion, f32[3,20,20,132]{3,2,1,0:T(8,128)S(1)} %slice_add_fusion.6, f32[3,22,22,134]{3,2,1,0:T(8,128)S(1)} %slice_add_fusion, f32[18,18,130]{2,1,0:T(8,128)S(1)} %slice.251), kind=kLoop, calls=%fused_computation.23 | loop fusion | flops 1516320 | bytes 5222880 | tf_op jit(solution)/shard_map/add | solution.py:118
  176.8 1.6 fusion.18
  (17 shorter events, 0.2 us)
Async XLA Ops:
  0.6 2.4 %copy-start = (bf16[1,1,16,48,256]{4,3,2,1,0:T(8,128)(2,1)S(1)}, bf16[1,1,16,48,256]{4,3,2,1,0:T(8,128)(2,1)}, u32[]{:S(2)}) copy-start(bf16[1,1,16,48,256]{4,3,2,1,0:T(8,128)(2,1)} %param.11) | copy-start | bytes 1179652
  5.4 9.7 %all-to-all-start = ((f32[4,8,192]{2,1,0:T(8,128)}), f32[4,8,192]{2,1,0:T(8,128)S(1)}, u32[]{:S(2)}, u32[]{:S(2)}) async-start(f32[4,8,192]{2,1,0:T(8,128)} %fusion.25), calls=%async_computation | async-start | bytes 65536 | tf_op jit(solution)/shard_map/all_to_all | solution.py:84
  39.6 8.0 %copy-start.2 = (f32[3,16,16,128]{3,2,1,0:T(8,128)S(1)}, f32[3,16,16,128]{3,2,1,0:T(8,128)}, u32[]{:S(2)}) copy-start(f32[3,16,16,128]{3,2,1,0:T(8,128)} %param.10) | copy-start | bytes 1179652
  39.6 8.0 %copy-start.3 = (f32[3,16,16,128]{3,2,1,0:T(8,128)S(1)}, f32[3,16,16,128]{3,2,1,0:T(8,128)}, u32[]{:S(2)}) copy-start(f32[3,16,16,128]{3,2,1,0:T(8,128)} %param.9) | copy-start | bytes 1179652
  47.7 17.8 %collective-permute-start.1 = (f32[19,4,16,128]{3,2,1,0:T(8,128)S(1)}, f32[19,4,16,128]{3,2,1,0:T(8,128)S(1)}, u32[]{:S(2)}, u32[]{:S(2)}) collective-permute-start(f32[19,4,16,128]{3,2,1,0:T(8,128)S(1)} %get-tuple-element.11), channel_id=1, source_target_pairs={{8,0},{16,8},{24,16},{9,1},{17,9},{25,17},{10,2},{18,10},{26,18},{... | collective-permute-start | bytes 1867784 | tf_op jit(solution)/shard_map/ppermute | solution.py:17
  51.1 26.2 %collective-permute-start = (f32[19,4,16,128]{3,2,1,0:T(8,128)S(1)}, f32[19,4,16,128]{3,2,1,0:T(8,128)S(1)}, u32[]{:S(2)}, u32[]{:S(2)}) collective-permute-start(f32[19,4,16,128]{3,2,1,0:T(8,128)S(1)} %get-tuple-element.10), channel_id=1, source_target_pairs={{0,8},{8,16},{16,24},{1,9},{9,17},{17,25},{2,10},{10,18},{18,26},{... | collective-permute-start | bytes 1867784 | tf_op jit(solution)/shard_map/ppermute | solution.py:16
  77.2 25.4 %copy-start.4 = (f32[19,4,16,128]{3,2,1,0:T(8,128)}, f32[19,4,16,128]{3,2,1,0:T(8,128)S(1)}, u32[]{:S(2)}) copy-start(f32[19,4,16,128]{3,2,1,0:T(8,128)S(1)} %collective-permute-done) | copy-start | bytes 1867780
  77.8 22.6 %collective-permute-start.3 = (f32[19,24,4,128]{3,2,1,0:T(4,128)S(1)}, f32[19,24,4,128]{3,2,1,0:T(4,128)S(1)}, u32[]{:S(2)}, u32[]{:S(2)}) collective-permute-start(f32[19,24,4,128]{3,2,1,0:T(4,128)S(1)} %get-tuple-element.9), channel_id=1, source_target_pairs={{2,0},{4,2},{6,4},{3,1},{5,3},{7,5},{10,8},{12,10},{14,12},{11,9},... | collective-permute-start | bytes 2801672 | tf_op jit(solution)/shard_map/ppermute | solution.py:17
  81.0 21.7 %collective-permute-start.2 = (f32[19,24,4,128]{3,2,1,0:T(4,128)S(1)}, f32[19,24,4,128]{3,2,1,0:T(4,128)S(1)}, u32[]{:S(2)}, u32[]{:S(2)}) collective-permute-start(f32[19,24,4,128]{3,2,1,0:T(4,128)S(1)} %get-tuple-element.8), channel_id=1, source_target_pairs={{0,2},{2,4},{4,6},{1,3},{3,5},{5,7},{8,10},{10,12},{12,14},{9,11},... | collective-permute-start | bytes 2801672 | tf_op jit(solution)/shard_map/ppermute | solution.py:16
  100.3 6.4 %copy-start.5 = (f32[19,24,4,128]{3,2,1,0:T(4,128)}, f32[19,24,4,128]{3,2,1,0:T(4,128)S(1)}, u32[]{:S(2)}) copy-start(f32[19,24,4,128]{3,2,1,0:T(4,128)S(1)} %collective-permute-done.3) | copy-start | bytes 2801668
  102.7 1.0 copy-start.6
  118.8 17.8 %collective-permute-start.5 = (f32[19,24,24,4]{2,1,3,0:T(8,128)}, f32[19,24,24,4]{2,1,3,0:T(8,128)}, u32[]{:S(2)}, u32[]{:S(2)}) collective-permute-start(f32[19,24,24,4]{2,1,3,0:T(8,128)} %copy.40), channel_id=1, source_target_pairs={{1,0},{3,2},{5,4},{7,6},{9,8},{11,10},{13,12},{15,14},{17,16},{19,... | collective-permute-start | bytes 525320 | tf_op jit(solution)/shard_map/ppermute | solution.py:17
  126.0 5.2 %slice-start = ((f32[4,3,16,16,8,16]{5,3,0,1,4,2:T(8,128)}), f32[1,3,16,16,8,16]{5,3,0,1,4,2:T(8,128)S(1)}, s32[]{:S(2)}) async-start(f32[4,3,16,16,8,16]{5,3,0,1,4,2:T(8,128)} %convolution_bitcast_fusion), calls=%async_computation.1 | async-start | bytes 6291456 | tf_op jit(solution)/shard_map/slice | solution.py:32
  126.0 16.1 %collective-permute-start.4 = (f32[19,24,24,4]{2,1,3,0:T(8,128)}, f32[19,24,24,4]{2,1,3,0:T(8,128)}, u32[]{:S(2)}, u32[]{:S(2)}) collective-permute-start(f32[19,24,24,4]{2,1,3,0:T(8,128)} %copy.39), channel_id=1, source_target_pairs={{0,1},{2,3},{4,5},{6,7},{8,9},{10,11},{12,13},{14,15},{16,17},{18,... | collective-permute-start | bytes 525320 | tf_op jit(solution)/shard_map/ppermute | solution.py:16
  173.9 4.5 %copy-start.1 = (bf16[1,1,16,48,256]{4,3,2,1,0:T(8,128)(2,1)S(1)}, bf16[1,1,16,48,256]{4,3,2,1,0:T(8,128)(2,1)}, u32[]{:S(2)}) copy-start(bf16[1,1,16,48,256]{4,3,2,1,0:T(8,128)(2,1)} %param.11) | copy-start | bytes 1179652
where the time goes:
time: 179 us; the launch traced here: 178 us
  local copies, waits for them, and re-layouts  61.5 us (34%)
  waiting for transfers between devices  43.4 us (24%)
  other arithmetic  38.8 us (22%)
  starting transfers between devices  23.7 us (13%)
  matrix products  10.1 us (6%)
    ppermute x3, waiting for transfers between devices, extended(): after = lax.ppermute(leading, axis, down)  28.5 us
    concatenate x2, other arithmetic, extended(): shard = jnp.concatenate([before, shard, after], axis=dim)  22.2 us
    transpose x1, local copies, waits for them, and re-layouts, per_device(): jnp.transpose(gathered, (5, 3, 0, 1, 2, 4))  16.3 us
    ppermute x3, waiting for transfers between devices, extended(): before = lax.ppermute(last, axis, up)  14 us
    slice x2, local copies, waits for them, and re-layouts, extended(): last = lax.slice_in_dim(shard, length - width, length, axis=dim)  12 us
    add x4, other arithmetic, per_device(): 2.0 * inner - trim_rim(older, 1)  11 us
    ppermute x3, starting transfers between devices, extended(): before = lax.ppermute(last, axis, up)  10.5 us
    dot_general x1, matrix products, per_device(): jnp.einsum('sb,sf->bf', placing, forces.reshape(width_gy * capacity, -1),...  8.03 us
  transfers between devices with their start and end apart: 7, of which 5 were waited for; matrix products, arithmetic and copies ran while one was open for 11% of the time, Pallas kernels for 0%

commit v1 on v0

v1 whole, which is shorter than its diff:
```python
import functools

import jax
import jax.numpy as jnp
import ml_dtypes
import numpy as np
from jax import lax
from jax.experimental import pallas as pl
from jax.experimental.pallas import tpu as pltpu
from jax.sharding import PartitionSpec as P

NSTEP = 4
HALO = 8
F32 = jnp.float32
BF16 = jnp.bfloat16


def wave_table(count, per_step):
    half = count // 2
    freq = np.float32(2.0 * np.pi) * (np.arange(half, dtype=np.float32) + np.float32(0.5)) / np.float32(count)
    times = np.float32(37.0) + np.arange(NSTEP, dtype=np.float32)
    phase = freq[:, None] * times[None, :]
    table = np.concatenate([np.cos(phase), np.sin(phase)], axis=0) / np.sqrt(np.float32(half))
    wide = np.repeat(table.astype(ml_dtypes.bfloat16), per_step, axis=1)
    return np.pad(wide, ((0, 0), (0, -wide.shape[1] % 128)))


def shift_of(size):
    assert size & (size - 1) == 0
    return size.bit_length() - 1


def iota(shape, dim):
    return lax.broadcasted_iota(jnp.int32, shape, dim)


def spin(value, amount, axis):
    return pltpu.roll(value, amount % value.shape[axis], axis)


def across(z0, z1):
    lanes = z0.shape[-1]
    lane = iota(z0.shape, z0.ndim - 1)
    first, last = lane == 0, lane == lanes - 1
    ax = z0.ndim - 1
    down0, down1 = spin(z0, 1, ax), spin(z1, 1, ax)
    up0, up1 = spin(z0, -1, ax), spin(z1, -1, ax)
    sum0 = jnp.where(first, 0.0, down0) + jnp.where(last, up1, up0)
    sum1 = jnp.where(first, down0, down1) + jnp.where(last, 0.0, up1)
    return sum0, sum1


def inplane(z0, z1):
    ax = z0.ndim - 2
    sum0, sum1 = across(z0, z1)
    sum0 = sum0 + (spin(z0, 1, ax) + spin(z0, -1, ax)) - 6.0 * z0
    sum1 = sum1 + (spin(z1, 1, ax) + spin(z1, -1, ax)) - 6.0 * z1
    return sum0, sum1


def speed_row(ints_ref, speed_ref):
    depth = ints_ref[0:1, :]
    row = jnp.zeros(depth.shape, F32)
    for layer in range(speed_ref.shape[0]):
        row = jnp.where(depth == layer, speed_ref[layer], row)
    return row


def force_kernel(panels_ref, coupling_ref, table_ref, force_ref):
    count, rows, spectral = panels_ref.shape
    comps, block = 3, rows // 3
    lanes = table_ref.shape[1]
    free = jnp.dot(
        panels_ref[...].reshape(count * rows, spectral), table_ref[...], preferred_element_type=F32
    )
    weights = coupling_ref[...].reshape(rows, block)
    stacked = jnp.concatenate([weights] * NSTEP + [jnp.zeros((lanes - NSTEP * rows, block), F32)], axis=0)
    pick = ((iota((rows, block), 0) & (block - 1)) == iota((rows, block), 1)).astype(F32)
    spread = lax.dot_general(
        pick, stacked, (((1,), (1,)), ((), ())), precision=lax.Precision.HIGHEST, preferred_element_type=F32
    )
    comp_row = iota((rows, lanes), 0) >> shift_of(block)
    comp_lane = iota((rows, lanes), 1) >> shift_of(block)
    same = comp_lane == comp_row
    for step in range(1, NSTEP):
        same = same | (comp_lane == comp_row + step * comps)
    spread = jnp.where(same, spread, 0.0)
    force_ref[...] = jnp.sum(free.reshape(count, rows, lanes) * spread[None], axis=1)


def pack_kernel(
    scal_ref, speed_ref, un_ref, up_ref, lat_ref, uno_ref, upo_ref, lato_ref, ints_ref, intso_ref,
    force_ref, forceo_ref, out_ref, pair_ref,
):
    mine = scal_ref[2]
    high = lax.rem(scal_ref[1] + mine, 2) == 0
    comps, size_x, size_y, size_z = un_ref.shape
    tiles = comps * size_x
    shape = (size_x, HALO, size_z)
    sub = iota(shape, 1)

    def fill(side):
        base = size_y - HALO if side else 0
        for z_at, un, up, lat, ints in (
            (mine, un_ref, up_ref, lat_ref, ints_ref),
            (1 - mine, uno_ref, upo_ref, lato_ref, intso_ref),
        ):
            rate = lat[:, base:base + HALO, :] * speed_row(ints, speed_ref)[None]
            for c in range(comps):
                now = un[c, :, base:base + HALO, :]
                old = spin(up[c, :, base:base + HALO, :], HALO // 2, 1)
                keep = sub >= HALO // 2 if side else sub < HALO // 2
                row = HALO - 1 - c if side else c
                tile = jnp.where(keep, now, old)
                tile = jnp.where(sub == (0 if side else HALO - 1), rate[:, row:row + 1, :], tile)
                out_ref[pl.ds(z_at * tiles + c * size_x, size_x)] = tile

    @pl.when(high)
    def _():
        fill(True)

    @pl.when(jnp.logical_not(high))
    def _():
        fill(False)

    count, lanes = force_ref.shape
    for z_at, force in ((mine, force_ref), (1 - mine, forceo_ref)):
        pair_ref[z_at] = force[...]
        for part in range(lanes // size_z):
            for piece in range(count // HALO):
                at = 2 * tiles + (z_at * (lanes // size_z) + part) * (count // HALO) + piece
                out_ref[at] = force[piece * HALO:(piece + 1) * HALO, part * size_z:(part + 1) * size_z]


def place_forces(scal_ref, sets, all_ref):
    if len(sets) == 1:
        return sets[0]
    own_ref, side_ref, sideo_ref, far_ref, faro_ref = sets
    o, mine = scal_ref[1], scal_ref[2]
    count, lanes = own_ref.shape[1:]
    beside, opposite, mirror = o + 1 - 2 * lax.rem(o, 2), lax.rem(o + 2, 4), 3 - o
    size_z = side_ref.shape[-1]
    tiles = side_ref.shape[0] - 2 * (lanes // size_z) * (count // HALO)
    here = mine == 0

    def spot(j):
        return pl.ds(pl.multiple_of(j * count, count), count)

    for ref, j in ((side_ref, jnp.where(here, beside, mirror)), (sideo_ref, jnp.where(here, mirror, beside))):
        for z in range(2):
            for part in range(lanes // size_z):
                at = tiles + (z * (lanes // size_z) + part) * (count // HALO)
                all_ref[z, spot(j), part * size_z:(part + 1) * size_z] = ref[
                    at:at + count // HALO
                ].reshape(count, size_z)
    for ref, j in (
        (far_ref, jnp.where(here, opposite, mirror)),
        (faro_ref, jnp.where(here, mirror, opposite)),
        (own_ref, o),
    ):
        for z in range(2):
            all_ref[z, spot(j), :] = ref[z]
    return all_ref


def panel_keys(ints_ref, o, panels, rows, size_x, size_y, zblocks):
    owner = jnp.concatenate([ints_ref[1 + i:2 + i, :] for i in range(-(-2 * panels // 128))], axis=1)
    half = 1 + owner.shape[1] // 128
    block = jnp.concatenate([ints_ref[half + i:half + 1 + i, :] for i in range(-(-2 * panels // 128))], axis=1)
    depth = block & (zblocks - 1)
    y = (block >> shift_of(zblocks)) & (size_y - 1)
    x = block >> (shift_of(zblocks) + shift_of(size_y))
    key = x * rows
    reach = NSTEP - 1
    row = jnp.where(owner == o, y, -1)
    row = jnp.where((owner == o + 1) & (y < reach), y + size_y, row)
    row = jnp.where((owner == o - 1) & (y >= size_y - reach), y + rows - size_y, row)
    return jnp.where(row < 0, -1, key + row), depth


def spread_forces(force, depth, size_z, block, steps):
    high = force.astype(BF16).astype(F32)
    both = jnp.concatenate([high, force - high], axis=0)
    rows = both.shape[0]
    lane = iota((rows, size_z), 1) >> shift_of(block)
    base = (
        (iota((size_z, size_z), 0) & (block - 1)) == (iota((size_z, size_z), 1) & (block - 1))
    ).astype(BF16)
    at = (iota((size_z, rows), 0) >> shift_of(block)) == depth
    at = jnp.transpose(at.astype(F32))
    per_tile = size_z // block
    out = []
    for q in range(steps * 3):
        part = both[:, (q // per_tile) * size_z:(q // per_tile + 1) * size_z]
        part = jnp.where(lane == q % per_tile, part, 0.0).astype(BF16)
        wide = jnp.dot(part, base, preferred_element_type=F32)
        out.append((wide * at).astype(BF16))
    return jnp.concatenate(out, axis=1)


def halo_tiles(high, low):
    sub = iota(high.shape, high.ndim - 2)
    upper = sub < HALO // 2
    now = jnp.where(upper, high, low)
    old = spin(jnp.where(upper, low, high), HALO // 2, high.ndim - 2)
    return now, old


def halo_rate(highs, lows):
    sub = iota(highs[0].shape, highs[0].ndim - 2)
    tile = jnp.zeros(highs[0].shape, F32)
    ends = slice(HALO - 1, HALO), slice(0, 1)
    for c in range(3):
        tile = jnp.where(sub == c, highs[c][..., ends[0], :], tile)
        tile = jnp.where(sub == HALO - 1 - c, lows[c][..., ends[1], :], tile)
    return tile


def sides(scal_ref, side_ref, sideo_ref, at):
    o, mine = scal_ref[1], scal_ref[2]
    high = lax.rem(o + mine, 2) == 0
    one, two = side_ref[at], sideo_ref[at]
    upper = jnp.where(o < scal_ref[4] - 1, jnp.where(high, one, two), 0.0)
    lower = jnp.where(o > 0, jnp.where(high, two, one), 0.0)
    return upper, lower


def face_kernel(
    scal_ref, speed_ref, un_ref, up_ref, lat_ref, uno_ref, upo_ref, lato_ref, ints_ref, intso_ref,
    side_ref, sideo_ref, *rest,
):
    *sets, out_ref, all_ref = rest
    comps, size_x, size_y, size_z = un_ref.shape
    rows = size_y + HALO
    tiles = comps * size_x
    a, o, mine = scal_ref[0], scal_ref[1], scal_ref[2]
    high = lax.rem(a + mine, 2) == 0
    forces = place_forces(scal_ref, sets, all_ref)
    panels = forces.shape[1]
    own = mine == 0
    now, old, rate, drive = {}, {}, {}, {}
    for z in range(2):
        keys, depth = panel_keys_of(z, own, ints_ref, intso_ref, o, panels, rows, size_x, size_y, size_z)
        wide = spread_forces(forces[z], depth, size_z, size_z // (size_z // 16), NSTEP - 1)
        first = jnp.where(high, size_x - NSTEP + 1, 0)
        node = iota(((NSTEP - 1) * rows, keys.shape[1]), 0) + first * rows
        hit = (node == keys).astype(F32).astype(BF16)
        got = jnp.dot(hit, wide, preferred_element_type=F32)
        got = got.reshape(NSTEP - 1, rows, wide.shape[1])
        for d in range(1, NSTEP):
            for n in range(NSTEP - d):
                for c in range(comps):
                    q = (n * comps + c) * size_z
                    drive[z, n, d, c] = jnp.where(
                        high, got[NSTEP - 1 - d, :, q:q + size_z], got[d - 1, :, q:q + size_z]
                    )
        speed = jnp.where(
            own if z == 0 else jnp.logical_not(own),
            speed_row(ints_ref, speed_ref),
            speed_row(intso_ref, speed_ref),
        )
        near = own if z == 0 else jnp.logical_not(own)
        for d in range(1, NSTEP + 1):
            x = jnp.where(high, size_x - d, d - 1)
            ups, lows = [], []
            for c in range(comps):
                upper, lower = sides(scal_ref, side_ref, sideo_ref, z * tiles + c * size_x + x)
                ups.append(upper)
                lows.append(lower)
                tile_now, tile_old = halo_tiles(upper, lower)
                centre = jnp.where(near, un_ref[c, x], uno_ref[c, x])
                now[z, d, c] = jnp.concatenate([centre, tile_now], axis=0)
                if d < NSTEP:
                    centre = jnp.where(near, up_ref[c, x], upo_ref[c, x])
                    old[z, d, c] = jnp.concatenate([centre, tile_old], axis=0)
            if d < NSTEP:
                centre = jnp.where(near, lat_ref[x], lato_ref[x]) * speed
                rate[z, d] = jnp.concatenate([centre, halo_rate(ups, lows)], axis=0)
    for z in range(2):
        for c in range(comps):
            out_ref[z, c] = now[z, 1, c]
        for d in (1, 2):
            out_ref[z, NSTEP * comps + d - 1] = rate[z, d]
    for n in range(1, NSTEP):
        later = {}
        for d in range(1, NSTEP - n + 1):
            for c in range(comps):
                sums = inplane(now[0, d, c], now[1, d, c])
                for z in range(2):
                    lap = sums[z] + now[z, d + 1, c]
                    if d > 1:
                        lap = lap + now[z, d - 1, c]
                    later[z, d, c] = (
                        2.0 * now[z, d, c] - old[z, d, c] + rate[z, d] * lap + drive[z, n - 1, d, c]
                    )
        old, now = now, later
        for z in range(2):
            for c in range(comps):
                out_ref[z, n * comps + c] = now[z, 1, c]


def panel_keys_of(z, own, ints_ref, intso_ref, o, panels, rows, size_x, size_y, size_z):
    near = own if z == 0 else jnp.logical_not(own)
    zblocks = size_z // 16
    mine = panel_keys(ints_ref, o, panels, rows, size_x, size_y, zblocks)
    theirs = panel_keys(intso_ref, o, panels, rows, size_x, size_y, zblocks)
    return tuple(jnp.where(near, one, two) for one, two in zip(mine, theirs))


def local_kernel(
    scal_ref, speed_ref, un_ref, up_ref, lat_ref, uno_ref, upo_ref, lato_ref, ints_ref, intso_ref,
    side_ref, sideo_ref, *rest,
):
    *sets, final_ref, before_ref, face_ref, ratef_ref, all_ref, now_ref, old_ref, rate_ref, drive_ref = rest
    comps, size_x, size_y, size_z = un_ref.shape
    rows = size_y + HALO
    tiles = comps * size_x
    o, mine = scal_ref[1], scal_ref[2]
    forces = place_forces(scal_ref, sets, all_ref)
    panels = forces.shape[1]
    own = mine == 0
    for z in range(2):
        keys, depth = panel_keys_of(z, own, ints_ref, intso_ref, o, panels, rows, size_x, size_y, size_z)
        wide = spread_forces(forces[z], depth, size_z, 16, NSTEP)
        node = iota((size_x * rows, keys.shape[1]), 0)
        hit = (node == keys).astype(F32).astype(BF16)
        for n in range(NSTEP):
            span = comps * size_z
            got = jnp.dot(hit, wide[:, n * span:(n + 1) * span], preferred_element_type=F32)
            for c in range(comps):
                drive_ref[n, z, c] = got[:, c * size_z:(c + 1) * size_z].reshape(size_x, rows, size_z)
    edge = jnp.zeros((rows, size_z), F32)
    for z in range(2):
        for c in range(comps):
            for ref in (now_ref, old_ref):
                ref[z, c, 0] = edge
                ref[z, c, size_x + 1] = edge
    for z_at, un, up, lat, ints in (
        (mine, un_ref, up_ref, lat_ref, ints_ref),
        (1 - mine, uno_ref, upo_ref, lato_ref, intso_ref),
    ):
        speed = speed_row(ints, speed_ref)
        ups, lows = [], []
        for c in range(comps):
            upper, lower = sides(scal_ref, side_ref, sideo_ref, pl.ds(z_at * tiles + c * size_x, size_x))
            ups.append(upper)
            lows.append(lower)
            tile_now, tile_old = halo_tiles(upper, lower)
            now_ref[z_at, c, 1:size_x + 1, 0:size_y] = un[c]
            now_ref[z_at, c, 1:size_x + 1, size_y:rows] = tile_now
            old_ref[z_at, c, 1:size_x + 1, 0:size_y] = up[c]
            old_ref[z_at, c, 1:size_x + 1, size_y:rows] = tile_old
        rate_ref[z_at, :, 0:size_y] = lat[...] * speed[None]
        rate_ref[z_at, :, size_y:rows] = halo_rate(ups, lows)
    for side in range(2):
        for z in range(2):
            for d in range(NSTEP):
                ratef_ref[side, z, d] = rate_ref[z, d if side else size_x - 1 - d]
    refs = [now_ref, old_ref]
    for n in range(NSTEP):
        now, old = refs[n % 2], refs[(n + 1) % 2]
        for side in range(2):
            for z in range(2):
                for c in range(comps):
                    face_ref[side, z, n * comps + c] = now[z, c, 1 if side else size_x]

        def step(x, carry):
            for c in range(comps):
                centre = now[0, c, x + 1], now[1, c, x + 1]
                sums = inplane(*centre)
                for z in range(2):
                    lap = sums[z] + (now[z, c, x] + now[z, c, x + 2])
                    old[z, c, x + 1] = (
                        2.0 * centre[z] - old[z, c, x + 1] + rate_ref[z, x] * lap + drive_ref[n, z, c, x]
                    )
            return carry

        lax.fori_loop(0, size_x, step, 0)
    now, old = refs[NSTEP % 2], refs[(NSTEP + 1) % 2]
    for c in range(comps):
        final_ref[c] = now[mine, c, 1:size_x + 1, 0:size_y]
        before_ref[c] = old[mine, c, 1:size_x + 1, 0:size_y]


def join_kernel(
    scal_ref, final_in, before_in, face_ref, ratef_ref, recv_ref, recvo_ref, final_ref, before_ref
):
    comps, size_x, size_y, size_z = final_in.shape
    a, mine = scal_ref[0], scal_ref[2]
    own = mine == 0
    high = lax.rem(a + mine, 2) == 0
    final_ref[...] = final_in[...]
    before_ref[...] = before_in[...]
    for side in range(2):
        is_high = side == 0
        here = high if is_high else jnp.logical_not(high)
        inside = a < scal_ref[3] - 1 if is_high else a > 0

        def theirs(z, at):
            return jnp.where(inside, jnp.where(here, recv_ref[z, at], recvo_ref[z, at]), 0.0)

        rate = {}
        for z in range(2):
            for m in range(NSTEP):
                rate[z, -m] = ratef_ref[side, z, m]
            for m in (1, 2):
                rate[z, m] = theirs(z, NSTEP * comps + m - 1)
        for c in range(comps):
            last, now = {}, {}
            for n in range(NSTEP):
                later = {}
                top = min(n + 1, NSTEP - 1 - n)
                for m in range(-n, top + 1):
                    centre = [now.get((z, m)) for z in range(2)]
                    sums = inplane(*centre) if centre[0] is not None else (None, None)
                    for z in range(2):
                        terms = [sums[z], now.get((z, m - 1)), now.get((z, m + 1))]
                        if m == 0:
                            terms.append(theirs(z, n * comps + c))
                        if m == 1:
                            terms.append(face_ref[side, z, n * comps + c])
                        terms = [t for t in terms if t is not None]
                        lap = functools.reduce(lambda p, q: p + q, terms)
                        value = rate[z, m] * lap
                        if centre[z] is not None:
                            value = value + 2.0 * centre[z]
                        if (z, m) in last:
                            value = value - last[z, m]
                        later[z, m] = value
                last, now = now, later
            for target, values in ((final_ref, now), (before_ref, last)):
                for m in range(0, -NSTEP, -1):
                    if (0, m) not in values:
                        continue
                    x = size_x - 1 + m if is_high else -m
                    add = jnp.where(own, values[0, m], values[1, m])[0:size_y]
                    target[c, x] = target[c, x] + add


def send(value, mesh_sizes, route):
    nx, ny, nz = mesh_sizes
    number = lambda i, j, k: (i * ny + j) * nz + k
    pairs = [
        (number(i, j, k), number(*route(i, j, k))) for i in range(nx) for j in range(ny) for k in range(nz)
    ]
    return lax.ppermute(value, ("gx", "gy", "gz"), pairs)


def partner(i, core, count):
    step = 1 if (i + core) % 2 == 0 else -1
    return (i + step) % count


def per_device(
    u_now, u_prev, panels, panel_owner, panel_block, coupling, layer_depth, layer_speed, lateral
):
    sizes = tuple(lax.axis_size(axis) for axis in ("gx", "gy", "gz"))
    nx, ny, nz = sizes
    assert nx % 2 == 0 and ny % 2 == 0 and nz == 2
    comps, size_x, size_y, size_z = u_now.shape
    rows = size_y + HALO
    per_dev, spectral = panels.shape[2], panels.shape[4]
    npanels = ny * per_dev
    scal = jnp.stack(
        [lax.axis_index("gx"), lax.axis_index("gy"), lax.axis_index("gz"), jnp.int32(nx), jnp.int32(ny)]
    ).astype(jnp.int32)

    def swap(value):
        return send(value, sizes, lambda i, j, k: (i, j, 1 - k))

    def route_x(i, j, k):
        return partner(i, k, nx), j, k

    def route_y(i, j, k):
        to = partner(j, k, ny)
        if abs(to - j) != 1 or (ny == 2 and k == 1):
            return i ^ 1, j, k
        return i, to, k

    owner, block = panel_owner.reshape(-1), panel_block.reshape(-1)
    both = jnp.concatenate([layer_depth, owner, owner, block, block])
    ints = jnp.pad(both, (0, -both.shape[0] % 1024)).reshape(-1, size_z)
    un_o, up_o, lat_o, ints_o = swap(u_now), swap(u_prev), swap(lateral), swap(ints)

    vmem = pl.BlockSpec(memory_space=pltpu.VMEM)
    smem = pl.BlockSpec(memory_space=pltpu.SMEM)
    params = pltpu.CompilerParams(vmem_limit_bytes=48 * 1024 * 1024)
    table = jnp.asarray(wave_table(spectral, panels.shape[3]))
    force = pl.pallas_call(
        force_kernel,
        out_shape=jax.ShapeDtypeStruct((per_dev, table.shape[1]), F32),
        in_specs=[vmem] * 3,
        out_specs=vmem,
        compiler_params=params,
        name="force",
    )(panels.reshape(per_dev, panels.shape[3], spectral), coupling, table)
    force_o = swap(force)
    tiles = comps * size_x
    extra = 2 * (force.shape[1] // size_z) * (per_dev // HALO)
    state = (scal, layer_speed, u_now, u_prev, lateral, un_o, up_o, lat_o, ints, ints_o)
    state_specs = [smem] * 2 + [vmem] * 8
    packed, pair = pl.pallas_call(
        pack_kernel,
        out_shape=(
            jax.ShapeDtypeStruct((2 * tiles + extra, HALO, size_z), F32),
            jax.ShapeDtypeStruct((2,) + force.shape, F32),
        ),
        in_specs=state_specs + [vmem] * 2,
        out_specs=(vmem, vmem),
        compiler_params=params,
        name="pack",
    )(*state, force, force_o)
    side = send(packed, sizes, route_y)
    if ny == 4:
        far = send(pair, sizes, lambda i, j, k: (i, j ^ 2 if k == 0 else 3 - j, k))
        side_o, far_o = swap(side), swap(far)
        sets = (pair, side, side_o, far, far_o)
    else:
        side_o = swap(side)
        sets = (jnp.moveaxis(lax.all_gather(pair, "gy"), 0, 1).reshape(2, npanels, -1),)
    shared = state + (side, side_o) + sets
    shared_specs = state_specs + [vmem] * (2 + len(sets))
    all_scratch = pltpu.VMEM((2, npanels, force.shape[1]), F32)
    planes = NSTEP * comps
    sent = pl.pallas_call(
        face_kernel,
        out_shape=jax.ShapeDtypeStruct((2, planes + 2, rows, size_z), F32),
        in_specs=shared_specs,
        out_specs=vmem,
        scratch_shapes=[all_scratch],
        compiler_params=params,
        name="face",
    )(*shared)
    recv = send(sent, sizes, route_x)
    final, before, face, ratef = pl.pallas_call(
        local_kernel,
        out_shape=(
            jax.ShapeDtypeStruct(u_now.shape, F32),
            jax.ShapeDtypeStruct(u_now.shape, F32),
            jax.ShapeDtypeStruct((2, 2, planes, rows, size_z), F32),
            jax.ShapeDtypeStruct((2, 2, NSTEP, rows, size_z), F32),
        ),
        in_specs=shared_specs,
        out_specs=(vmem,) * 4,
        scratch_shapes=[
            all_scratch,
            pltpu.VMEM((2, comps, size_x + 2, rows, size_z), F32),
            pltpu.VMEM((2, comps, size_x + 2, rows, size_z), F32),
            pltpu.VMEM((2, size_x, rows, size_z), F32),
            pltpu.VMEM((NSTEP, 2, comps, size_x, rows, size_z), F32),
        ],
        compiler_params=params,
        name="local",
    )(*shared)
    recv_o = swap(recv)
    return pl.pallas_call(
        join_kernel,
        out_shape=(
            jax.ShapeDtypeStruct(u_now.shape, F32),
            jax.ShapeDtypeStruct(u_now.shape, F32),
        ),
        in_specs=[smem] + [vmem] * 6,
        out_specs=(vmem, vmem),
        compiler_params=params,
        name="join",
    )(scal, final, before, face, ratef, recv, recv_o)


def solution(mesh):
    in_specs = (
        P(None, "gx", "gy", "gz"),
        P(None, "gx", "gy", "gz"),
        P("gx", "gz", "gy", None, None),
        P("gx", "gz", None, None),
        P("gx", "gz", None),
        P(),
        P("gz"),
        P(),
        P("gx", "gy", "gz"),
    )
    out_specs = (P(None, "gx", "gy", "gz"), P(None, "gx", "gy", "gz"))
    return jax.shard_map(
        per_device, mesh=mesh, in_specs=in_specs, out_specs=out_specs, check_vma=False
    )
```

time: 179 us -> 48.4 us (0.27)
  the two profiles are of different devices: /device:TPU:12 before, /device:TPU:0 now
where the time goes in v1:
time: 48.4 us; the launch traced here: 48 us
  waiting for transfers between devices  19.1 us (39%)
  Pallas kernels  14.1 us (29%)
  starting transfers between devices  9.5 us (20%)
  local copies, waits for them, and re-layouts  4.45 us (9%)
  between operations  0.73 us (2%)
    ppermute x11, waiting for transfers between devices, send(): return lax.ppermute(value, ('gx', 'gy', 'gz'), pairs)  19.1 us
    ppermute x11, starting transfers between devices, send(): return lax.ppermute(value, ('gx', 'gy', 'gz'), pairs)  9.5 us
    pallas_call x1, Pallas kernels, per_device(): pl.pallas_call(local_kernel, out_shape=(jax.ShapeDtypeStruct(u_now.shape,...  9.34 us
    unnamed x14, local copies, waits for them, and re-layouts  3.64 us
    pallas_call x1, Pallas kernels, per_device(): pl.pallas_call(join_kernel, out_shape=(jax.ShapeDtypeStruct(u_now.shape,...  2.37 us
    pallas_call x1, Pallas kernels, per_device(): pl.pallas_call(face_kernel, out_shape=jax.ShapeDtypeStruct((2, planes + 2...  1.32 us
  transfers between devices with their start and end apart: 11, of which 5 were waited for; matrix products, arithmetic and copies ran while one was open for 2% of the time, Pallas kernels for 20%

profile of v1, /device:TPU:0, one launch (start us, length us, event | category | flops | bytes accessed | tf_op | source)
XLA Modules:
  0.0 48.0 jit_solution(2074460903627443110)
XLA Ops:
  0.6 0.0 copy-start
  0.6 0.5 %collective-permute-start = (f32[3,16,16,128]{3,2,1,0:T(8,128)}, f32[3,16,16,128]{3,2,1,0:T(8,128)S(1)}, u32[]{:S(2)}, u32[]{:S(2)}) collective-permute-start(f32[3,16,16,128]{3,2,1,0:T(8,128)} %un_ref.5), channel_id=1, source_target_pairs={{0,1},{1,0},{2,3},{3,2},{4,5},{5,4},{6,7},{7,6},{8,9},{9,8},{10,11... | collective-permute-start | bytes 1179656 | tf_op jit(solution)/shard_map/ppermute | solution.py:446
  1.2 0.1 collective-permute-start.1
  1.2 0.4 collective-permute-start.2
  1.7 0.8 %concatenate.3 = s32[384]{0:T(512)S(1)} concatenate(s32[128]{0:T(128)} %param.16, s32[64]{0:T(128)} %bitcast.9, s32[64]{0:T(128)} %bitcast.10, s32[64]{0:T(128)} %bitcast.11, s32[64]{0:T(128)} %bitcast.12), dimensions={0} | concatenate | bytes 3072 | tf_op jit(solution)/shard_map/concatenate | solution.py:481
  2.5 0.1 collective-permute-start.3
  2.6 0.0 copy-start.3
  2.6 1.0 %copy-done.3 = bf16[1,1,16,48,256]{4,3,2,1,0:T(8,128)(2,1)S(1)} copy-done((bf16[1,1,16,48,256]{4,3,2,1,0:T(8,128)(2,1)S(1)}, bf16[1,1,16,48,256]{4,3,2,1,0:T(8,128)(2,1)}, u32[]{:S(2)}) %copy-start.3) | copy-done | bytes 393240
  3.6 0.0 copy-start.4
  3.6 0.9 %copy-done.4 = bf16[256,256]{1,0:T(8,128)(2,1)S(1)} copy-done((bf16[256,256]{1,0:T(8,128)(2,1)S(1)}, bf16[256,256]{1,0:T(8,128)(2,1)}, u32[]{:S(2)}) %copy-start.4) | copy-done | bytes 131096
  4.5 0.0 copy-start.5
  4.5 0.7 %copy-done.5 = f32[3,16,16]{2,1,0:T(8,128)S(1)} copy-done((f32[3,16,16]{2,1,0:T(8,128)S(1)}, f32[3,16,16]{2,1,0:T(8,128)}, u32[]{:S(2)}) %copy-start.5) | copy-done | bytes 3096
  5.2 0.0 copy-start.2
  5.2 0.5 force.1.force_ref
  5.7 0.5 %collective-permute-start.4 = (f32[16,256]{1,0:T(8,128)S(1)}, f32[16,256]{1,0:T(8,128)S(1)}, u32[]{:S(2)}, u32[]{:S(2)}) collective-permute-start(f32[16,256]{1,0:T(8,128)S(1)} %force.1.force_ref), channel_id=1, source_target_pairs={{0,1},{1,0},{2,3},{3,2},{4,5},{5,4},{6,7},{7,6},{8,9},{9,8},{10,11... | collective-permute-start | bytes 49160 | tf_op jit(solution)/shard_map/ppermute | solution.py:446
  6.2 0.0 copy-start.6
  6.2 0.1 pad_add_fusion.scal_ref
  6.3 0.0 collective-permute-done.3.intso_ref
  6.3 0.8 %collective-permute-done.4.forceo_ref = f32[16,256]{1,0:T(8,128)S(1)} collective-permute-done((f32[16,256]{1,0:T(8,128)S(1)}, f32[16,256]{1,0:T(8,128)S(1)}, u32[]{:S(2)}, u32[]{:S(2)}) %collective-permute-start.4) | collective-permute-done | bytes 16416 | tf_op jit(solution)/shard_map/ppermute | solution.py:446
  7.0 0.0 collective-permute-done.2.lato_ref
  7.0 0.0 collective-permute-done.uno_ref
  7.0 0.0 collective-permute-done.1.upo_ref
  7.0 0.0 copy-done
  7.0 0.0 copy-done.2
  7.0 0.0 copy-done.6
  7.0 0.0 copy-start.1
  7.1 1.0 %copy-done.1 = f32[3,16,16,128]{3,2,1,0:T(8,128)S(1)} copy-done((f32[3,16,16,128]{3,2,1,0:T(8,128)S(1)}, f32[3,16,16,128]{3,2,1,0:T(8,128)}, u32[]{:S(2)}) %copy-start.1) | copy-done | bytes 393240
  8.0 0.6 %pack.1 = (f32[104,8,128]{2,1,0:T(8,128)S(1)}, f32[2,16,256]{2,1,0:T(8,128)S(1)}) custom-call(s32[5]{0:T(128)S(1)} %pad_add_fusion.scal_ref, f32[8]{0:T(128)S(1)} %copy-done.6, f32[3,16,16,128]{3,2,1,0:T(8,128)S(1)} %copy-done, f32[3,16,16,128]{3,2,1,0:T(8,128)S(1)} %copy-done.1, f32[16,16,128]{2,1,0:T(8,128)S(1)} %copy-done.2, ...), custom_call_target="tpu_custom_call" | custom-call | tf_op jit(solution)/shard_map/pack/pallas_call | solution.py:502
  8.7 3.0 %collective-permute-start.5 = (f32[104,8,128]{2,1,0:T(8,128)S(1)}, f32[104,8,128]{2,1,0:T(8,128)S(1)}, u32[]{:S(2)}, u32[]{:S(2)}) collective-permute-start(f32[104,8,128]{2,1,0:T(8,128)S(1)} %get-tuple-element.8), channel_id=1, source_target_pairs={{0,2},{1,9},{2,0},{3,5},{4,6},{5,3},{6,4},{7,15},{8,10},{9,1},{10,... | collective-permute-start | bytes 1277960 | tf_op jit(solution)/shard_map/ppermute | solution.py:446
  11.7 6.1 %collective-permute-done.5.side_ref.rest_1_ = f32[104,8,128]{2,1,0:T(8,128)S(1)} collective-permute-done((f32[104,8,128]{2,1,0:T(8,128)S(1)}, f32[104,8,128]{2,1,0:T(8,128)S(1)}, u32[]{:S(2)}, u32[]{:S(2)}) %collective-permute-start.5) | collective-permute-done | bytes 426016 | tf_op jit(solution)/shard_map/ppermute | solution.py:446
  17.8 0.0 collective-permute-start.6
  17.8 3.0 %collective-permute-start.7 = (f32[2,16,256]{2,1,0:T(8,128)S(1)}, f32[2,16,256]{2,1,0:T(8,128)S(1)}, u32[]{:S(2)}, u32[]{:S(2)}) collective-permute-start(f32[2,16,256]{2,1,0:T(8,128)S(1)} %get-tuple-element.9.rest_0_), channel_id=1, source_target_pairs={{0,4},{1,7},{2,6},{3,5},{4,0},{5,3},{6,2},{7,1},{8,12},{9,15},{10,... | collective-permute-start | bytes 98312 | tf_op jit(solution)/shard_map/ppermute | solution.py:446
  20.8 2.2 %collective-permute-done.7.rest_3_ = f32[2,16,256]{2,1,0:T(8,128)S(1)} collective-permute-done((f32[2,16,256]{2,1,0:T(8,128)S(1)}, f32[2,16,256]{2,1,0:T(8,128)S(1)}, u32[]{:S(2)}, u32[]{:S(2)}) %collective-permute-start.7) | collective-permute-done | bytes 32800 | tf_op jit(solution)/shard_map/ppermute | solution.py:446
  23.1 0.3 collective-permute-start.8
  23.4 0.9 %collective-permute-done.8.rest_4_ = f32[2,16,256]{2,1,0:T(8,128)S(1)} collective-permute-done((f32[2,16,256]{2,1,0:T(8,128)S(1)}, f32[2,16,256]{2,1,0:T(8,128)S(1)}, u32[]{:S(2)}, u32[]{:S(2)}) %collective-permute-start.8) | collective-permute-done | bytes 32800 | tf_op jit(solution)/shard_map/ppermute | solution.py:446
  24.3 0.0 collective-permute-done.6.sideo_ref.rest_2_
  24.3 1.3 %face.1 = f32[2,14,24,128]{3,2,1,0:T(8,128)S(1)} custom-call(s32[5]{0:T(128)S(1)} %pad_add_fusion.scal_ref, f32[8]{0:T(128)S(1)} %copy-done.6, f32[3,16,16,128]{3,2,1,0:T(8,128)S(1)} %copy-done, f32[3,16,16,128]{3,2,1,0:T(8,128)S(1)} %copy-done.1, f32[16,16,128]{2,1,0:T(8,128)S(1)} %copy-done.2, f32[3,16,16,128]{3,2,1,0:T(8,128)S(1)} %collective-permute-done.uno_ref, ...), custom_call_target="tpu_custom_call" | custom-call | tf_op jit(solution)/shard_map/face/pallas_call | solution.py:525
  25.6 1.6 %collective-permute-start.9 = (f32[2,14,24,128]{3,2,1,0:T(8,128)S(1)}, f32[2,14,24,128]{3,2,1,0:T(8,128)S(1)}, u32[]{:S(2)}, u32[]{:S(2)}) collective-permute-start(f32[2,14,24,128]{3,2,1,0:T(8,128)S(1)} %face.1), channel_id=1, source_target_pairs={{0,8},{1,25},{2,10},{3,27},{4,12},{5,29},{6,14},{7,31},{8,0},{9,17... | collective-permute-start | bytes 1032200 | tf_op jit(solution)/shard_map/ppermute | solution.py:446
  27.1 9.1 %collective-permute-done.9.recv_ref = f32[2,14,24,128]{3,2,1,0:T(8,128)S(1)} collective-permute-done((f32[2,14,24,128]{3,2,1,0:T(8,128)S(1)}, f32[2,14,24,128]{3,2,1,0:T(8,128)S(1)}, u32[]{:S(2)}, u32[]{:S(2)}) %collective-permute-start.9) | collective-permute-done | bytes 344096 | tf_op jit(solution)/shard_map/ppermute | solution.py:446
  36.3 0.0 collective-permute-start.10
  36.3 9.3 %local.1 = (f32[3,16,16,128]{3,2,1,0:T(8,128)S(1)}, f32[3,16,16,128]{3,2,1,0:T(8,128)S(1)}, f32[2,2,12,24,128]{4,3,2,1,0:T(8,128)S(1)}, f32[2,2,4,24,128]{4,3,2,1,0:T(8,128)S(1)}) custom-call(s32[5]{0:T(128)S(1)} %pad_add_fusion.scal_ref, f32[8]{0:T(128)S(1)} %copy-done.6, f32[3,16,16,128]{3,2,1,0:T(8,128)S(1)} %copy-done, f32[3,16,16,128]{3,2,1,0:T(8,128)S(1)} %copy-done.1, ...), custom_call_target="tpu_custom_call" | custom-call | tf_op jit(solution)/shard_map/local/pallas_call | solution.py:535
  45.6 0.0 collective-permute-done.10.recvo_ref
  45.6 2.4 %join.1 = (f32[3,16,16,128]{3,2,1,0:T(8,128)}, f32[3,16,16,128]{3,2,1,0:T(8,128)}) custom-call(s32[5]{0:T(128)S(1)} %pad_add_fusion.scal_ref, f32[3,16,16,128]{3,2,1,0:T(8,128)S(1)} %get-tuple-element.10.final_in, f32[3,16,16,128]{3,2,1,0:T(8,128)S(1)} %get-tuple-element.11.before_in, f32[2,2,12,24,128]{4,3,2,1,0:T(8,128)S(1)} %get-tuple-element.12.face_ref, ...), custom_call_target="tpu_custom_call" | custom-call | tf_op jit(solution)/shard_map/join/pallas_call | solution.py:556
  (2 shorter events, 0.0 us)
Async XLA Ops:
  0.6 6.4 %copy-start = (f32[3,16,16,128]{3,2,1,0:T(8,128)S(1)}, f32[3,16,16,128]{3,2,1,0:T(8,128)}, u32[]{:S(2)}) copy-start(f32[3,16,16,128]{3,2,1,0:T(8,128)} %un_ref.5) | copy-start | bytes 1179652
  0.6 6.4 %collective-permute-start = (f32[3,16,16,128]{3,2,1,0:T(8,128)}, f32[3,16,16,128]{3,2,1,0:T(8,128)S(1)}, u32[]{:S(2)}, u32[]{:S(2)}) collective-permute-start(f32[3,16,16,128]{3,2,1,0:T(8,128)} %un_ref.5), channel_id=1, source_target_pairs={{0,1},{1,0},{2,3},{3,2},{4,5},{5,4},{6,7},{7,6},{8,9},{9,8},{10,11... | collective-permute-start | bytes 1179656 | tf_op jit(solution)/shard_map/ppermute | solution.py:446
  1.2 5.9 %collective-permute-start.1 = (f32[3,16,16,128]{3,2,1,0:T(8,128)}, f32[3,16,16,128]{3,2,1,0:T(8,128)S(1)}, u32[]{:S(2)}, u32[]{:S(2)}) collective-permute-start(f32[3,16,16,128]{3,2,1,0:T(8,128)} %up_ref.5), channel_id=1, source_target_pairs={{0,1},{1,0},{2,3},{3,2},{4,5},{5,4},{6,7},{7,6},{8,9},{9,8},{10,11... | collective-permute-start | bytes 1179656 | tf_op jit(solution)/shard_map/ppermute | solution.py:446
  1.2 5.8 %collective-permute-start.2 = (f32[16,16,128]{2,1,0:T(8,128)}, f32[16,16,128]{2,1,0:T(8,128)S(1)}, u32[]{:S(2)}, u32[]{:S(2)}) collective-permute-start(f32[16,16,128]{2,1,0:T(8,128)} %lat_ref.5), channel_id=1, source_target_pairs={{0,1},{1,0},{2,3},{3,2},{4,5},{5,4},{6,7},{7,6},{8,9},{9,8},{10,11... | collective-permute-start | bytes 393224 | tf_op jit(solution)/shard_map/ppermute | solution.py:446
  2.5 3.8 %collective-permute-start.3 = (s32[8,128]{1,0:T(8,128)S(1)}, s32[8,128]{1,0:T(8,128)S(1)}, u32[]{:S(2)}, u32[]{:S(2)}) collective-permute-start(s32[8,128]{1,0:T(8,128)S(1)} %pad_bitcast_fusion.ints_ref), channel_id=1, source_target_pairs={{0,1},{1,0},{2,3},{3,2},{4,5},{5,4},{6,7},{7,6},{8,9},{9,8},{10,11... | collective-permute-start | bytes 12296 | tf_op jit(solution)/shard_map/ppermute | solution.py:446
  2.6 1.0 %copy-start.3 = (bf16[1,1,16,48,256]{4,3,2,1,0:T(8,128)(2,1)S(1)}, bf16[1,1,16,48,256]{4,3,2,1,0:T(8,128)(2,1)}, u32[]{:S(2)}) copy-start(bf16[1,1,16,48,256]{4,3,2,1,0:T(8,128)(2,1)} %param.12) | copy-start | bytes 1179652
  3.6 0.9 %copy-start.4 = (bf16[256,256]{1,0:T(8,128)(2,1)S(1)}, bf16[256,256]{1,0:T(8,128)(2,1)}, u32[]{:S(2)}) copy-start(bf16[256,256]{1,0:T(8,128)(2,1)} %constant.17.clone.table_ref) | copy-start | bytes 393220
  4.5 0.7 %copy-start.5 = (f32[3,16,16]{2,1,0:T(8,128)S(1)}, f32[3,16,16]{2,1,0:T(8,128)}, u32[]{:S(2)}) copy-start(f32[3,16,16]{2,1,0:T(8,128)} %coupling_ref.1) | copy-start | bytes 9220
  5.2 1.8 %copy-start.2 = (f32[16,16,128]{2,1,0:T(8,128)S(1)}, f32[16,16,128]{2,1,0:T(8,128)}, u32[]{:S(2)}) copy-start(f32[16,16,128]{2,1,0:T(8,128)} %lat_ref.5) | copy-start | bytes 393220
  5.7 1.3 %collective-permute-start.4 = (f32[16,256]{1,0:T(8,128)S(1)}, f32[16,256]{1,0:T(8,128)S(1)}, u32[]{:S(2)}, u32[]{:S(2)}) collective-permute-start(f32[16,256]{1,0:T(8,128)S(1)} %force.1.force_ref), channel_id=1, source_target_pairs={{0,1},{1,0},{2,3},{3,2},{4,5},{5,4},{6,7},{7,6},{8,9},{9,8},{10,11... | collective-permute-start | bytes 49160 | tf_op jit(solution)/shard_map/ppermute | solution.py:446
  6.2 0.9 %copy-start.6 = (f32[8]{0:T(128)S(1)}, f32[8]{0:T(128)}, u32[]{:S(2)}) copy-start(f32[8]{0:T(128)} %speed_ref.5) | copy-start | bytes 100
  7.0 1.0 %copy-start.1 = (f32[3,16,16,128]{3,2,1,0:T(8,128)S(1)}, f32[3,16,16,128]{3,2,1,0:T(8,128)}, u32[]{:S(2)}) copy-start(f32[3,16,16,128]{3,2,1,0:T(8,128)} %up_ref.5) | copy-start | bytes 1179652
  8.7 9.1 %collective-permute-start.5 = (f32[104,8,128]{2,1,0:T(8,128)S(1)}, f32[104,8,128]{2,1,0:T(8,128)S(1)}, u32[]{:S(2)}, u32[]{:S(2)}) collective-permute-start(f32[104,8,128]{2,1,0:T(8,128)S(1)} %get-tuple-element.8), channel_id=1, source_target_pairs={{0,2},{1,9},{2,0},{3,5},{4,6},{5,3},{6,4},{7,15},{8,10},{9,1},{10,... | collective-permute-start | bytes 1277960 | tf_op jit(solution)/shard_map/ppermute | solution.py:446
  17.8 6.5 %collective-permute-start.6 = (f32[104,8,128]{2,1,0:T(8,128)S(1)}, f32[104,8,128]{2,1,0:T(8,128)S(1)}, u32[]{:S(2)}, u32[]{:S(2)}) collective-permute-start(f32[104,8,128]{2,1,0:T(8,128)S(1)} %collective-permute-done.5.side_ref.rest_1_), channel_id=1, source_target_pairs={{0,1},{1,0},{2,3},{3,2},{4,5},{5,4},{6,7},{7,6},{8,9},{9,8},{10,11... | collective-permute-start | bytes 1277960 | tf_op jit(solution)/shard_map/ppermute | solution.py:446
  17.8 5.3 %collective-permute-start.7 = (f32[2,16,256]{2,1,0:T(8,128)S(1)}, f32[2,16,256]{2,1,0:T(8,128)S(1)}, u32[]{:S(2)}, u32[]{:S(2)}) collective-permute-start(f32[2,16,256]{2,1,0:T(8,128)S(1)} %get-tuple-element.9.rest_0_), channel_id=1, source_target_pairs={{0,4},{1,7},{2,6},{3,5},{4,0},{5,3},{6,2},{7,1},{8,12},{9,15},{10,... | collective-permute-start | bytes 98312 | tf_op jit(solution)/shard_map/ppermute | solution.py:446
  23.1 1.2 %collective-permute-start.8 = (f32[2,16,256]{2,1,0:T(8,128)S(1)}, f32[2,16,256]{2,1,0:T(8,128)S(1)}, u32[]{:S(2)}, u32[]{:S(2)}) collective-permute-start(f32[2,16,256]{2,1,0:T(8,128)S(1)} %collective-permute-done.7.rest_3_), channel_id=1, source_target_pairs={{0,1},{1,0},{2,3},{3,2},{4,5},{5,4},{6,7},{7,6},{8,9},{9,8},{10,11... | collective-permute-start | bytes 98312 | tf_op jit(solution)/shard_map/ppermute | solution.py:446
  25.6 10.7 %collective-permute-start.9 = (f32[2,14,24,128]{3,2,1,0:T(8,128)S(1)}, f32[2,14,24,128]{3,2,1,0:T(8,128)S(1)}, u32[]{:S(2)}, u32[]{:S(2)}) collective-permute-start(f32[2,14,24,128]{3,2,1,0:T(8,128)S(1)} %face.1), channel_id=1, source_target_pairs={{0,8},{1,25},{2,10},{3,27},{4,12},{5,29},{6,14},{7,31},{8,0},{9,17... | collective-permute-start | bytes 1032200 | tf_op jit(solution)/shard_map/ppermute | solution.py:446
  36.3 9.4 %collective-permute-start.10 = (f32[2,14,24,128]{3,2,1,0:T(8,128)S(1)}, f32[2,14,24,128]{3,2,1,0:T(8,128)S(1)}, u32[]{:S(2)}, u32[]{:S(2)}) collective-permute-start(f32[2,14,24,128]{3,2,1,0:T(8,128)S(1)} %collective-permute-done.9.recv_ref), channel_id=1, source_target_pairs={{0,1},{1,0},{2,3},{3,2},{4,5},{5,4},{6,7},{7,6},{8,9},{9,8},{10,11... | collective-permute-start | bytes 1032200 | tf_op jit(solution)/shard_map/ppermute | solution.py:446

commit v2 on v1

--- a/solution.py
+++ b/solution.py
@@ -11,6 +11,8 @@
 
 NSTEP = 4
 HALO = 8
+LANES = 128
+PANELS = 16
 F32 = jnp.float32
 BF16 = jnp.bfloat16
 
@@ -59,14 +61,28 @@
 
 
 def speed_row(ints_ref, speed_ref):
-    depth = ints_ref[0:1, :]
+    depth = integers(ints_ref, LANES, 0)
     row = jnp.zeros(depth.shape, F32)
     for layer in range(speed_ref.shape[0]):
         row = jnp.where(depth == layer, speed_ref[layer], row)
     return row
 
 
-def force_kernel(panels_ref, coupling_ref, table_ref, force_ref):
+def prepare_kernel(
+    panels_hbm, coupling_hbm, table_hbm, depth_hbm, owner_hbm, block_hbm, un_hbm, up_hbm, lat_hbm,
+    out_ref, un_ref, up_ref, lat_ref,
+    panels_ref, coupling_ref, table_ref, depth_ref, owner_ref, block_ref, sems,
+):
+    pairs = (
+        (panels_hbm, panels_ref), (table_hbm, table_ref), (coupling_hbm, coupling_ref),
+        (depth_hbm, depth_ref), (owner_hbm, owner_ref), (block_hbm, block_ref),
+        (un_hbm, un_ref), (up_hbm, up_ref), (lat_hbm, lat_ref),
+    )
+    copies = [pltpu.make_async_copy(src, dst, sems.at[i]) for i, (src, dst) in enumerate(pairs)]
+    for copy in copies:
+        copy.start()
+    for copy in copies[:6]:
+        copy.wait()
     count, rows, spectral = panels_ref.shape
     comps, block = 3, rows // 3
     lanes = table_ref.shape[1]
@@ -85,12 +101,33 @@
     for step in range(1, NSTEP):
         same = same | (comp_lane == comp_row + step * comps)
     spread = jnp.where(same, spread, 0.0)
-    force_ref[...] = jnp.sum(free.reshape(count, rows, lanes) * spread[None], axis=1)
+    out_ref[0:count] = jnp.sum(free.reshape(count, rows, lanes) * spread[None], axis=1)
+    out_ref[count:] = jnp.zeros((out_ref.shape[0] - count, lanes), F32)
+    pieces = [depth_ref[...]]
+    for ref in (owner_ref, block_ref):
+        twice = jnp.concatenate([ref[...], ref[...]], axis=1)
+        pieces += [twice[:, i:i + LANES] for i in range(0, twice.shape[1], LANES)]
+    for i, piece in enumerate(pieces):
+        row, at = count + i * LANES // lanes, i * LANES % lanes
+        out_ref[row:row + 1, at:at + LANES] = piece.astype(F32)
+    for copy in copies[6:]:
+        copy.wait()
+
+
+def integers(ref, panels, which):
+    lanes = ref.shape[1]
+    width = -(-2 * panels // LANES)
+    first, number = ((0, 1), (1, width), (1 + width, width))[which]
+    out = []
+    for i in range(first, first + number):
+        row, at = PANELS + i * LANES // lanes, i * LANES % lanes
+        out.append(ref[row:row + 1, at:at + LANES].astype(jnp.int32))
+    return jnp.concatenate(out, axis=1)
 
 
 def pack_kernel(
     scal_ref, speed_ref, un_ref, up_ref, lat_ref, uno_ref, upo_ref, lato_ref, ints_ref, intso_ref,
-    force_ref, forceo_ref, out_ref, pair_ref,
+    out_ref, pair_ref,
 ):
     mine = scal_ref[2]
     high = lax.rem(scal_ref[1] + mine, 2) == 0
@@ -123,9 +160,9 @@
     def _():
         fill(False)
 
-    count, lanes = force_ref.shape
-    for z_at, force in ((mine, force_ref), (1 - mine, forceo_ref)):
-        pair_ref[z_at] = force[...]
+    count, lanes = PANELS, ints_ref.shape[1]
+    for z_at, force in ((mine, ints_ref), (1 - mine, intso_ref)):
+        pair_ref[z_at] = force[0:count]
         for part in range(lanes // size_z):
             for piece in range(count // HALO):
                 at = 2 * tiles + (z_at * (lanes // size_z) + part) * (count // HALO) + piece
@@ -164,9 +201,8 @@
 
 
 def panel_keys(ints_ref, o, panels, rows, size_x, size_y, zblocks):
-    owner = jnp.concatenate([ints_ref[1 + i:2 + i, :] for i in range(-(-2 * panels // 128))], axis=1)
-    half = 1 + owner.shape[1] // 128
-    block = jnp.concatenate([ints_ref[half + i:half + 1 + i, :] for i in range(-(-2 * panels // 128))], axis=1)
+    owner = integers(ints_ref, panels, 1)
+    block = integers(ints_ref, panels, 2)
     depth = block & (zblocks - 1)
     y = (block >> shift_of(zblocks)) & (size_y - 1)
     x = block >> (shift_of(zblocks) + shift_of(size_y))
@@ -477,42 +513,64 @@
             return i ^ 1, j, k
         return i, to, k
 
-    owner, block = panel_owner.reshape(-1), panel_block.reshape(-1)
-    both = jnp.concatenate([layer_depth, owner, owner, block, block])
-    ints = jnp.pad(both, (0, -both.shape[0] % 1024)).reshape(-1, size_z)
-    un_o, up_o, lat_o, ints_o = swap(u_now), swap(u_prev), swap(lateral), swap(ints)
+    assert per_dev == PANELS and size_z == LANES
+    un_o, up_o, lat_o = swap(u_now), swap(u_prev), swap(lateral)
 
     vmem = pl.BlockSpec(memory_space=pltpu.VMEM)
     smem = pl.BlockSpec(memory_space=pltpu.SMEM)
     params = pltpu.CompilerParams(vmem_limit_bytes=48 * 1024 * 1024)
     table = jnp.asarray(wave_table(spectral, panels.shape[3]))
-    force = pl.pallas_call(
-        force_kernel,
-        out_shape=jax.ShapeDtypeStruct((per_dev, table.shape[1]), F32),
-        in_specs=[vmem] * 3,
-        out_specs=vmem,
+    width = table.shape[1]
+    number = LANES + 4 * npanels
+    extra_rows = -(-(-(-number // width)) // 8) * 8
+    ints, un_v, up_v, lat_v = pl.pallas_call(
+        prepare_kernel,
+        out_shape=(
+            jax.ShapeDtypeStruct((per_dev + extra_rows, width), F32),
+            jax.ShapeDtypeStruct(u_now.shape, F32),
+            jax.ShapeDtypeStruct(u_prev.shape, F32),
+            jax.ShapeDtypeStruct(lateral.shape, F32),
+        ),
+        in_specs=[pl.BlockSpec(memory_space=pl.ANY)] * 9,
+        out_specs=(vmem,) * 4,
+        scratch_shapes=[
+            pltpu.VMEM((per_dev,) + panels.shape[3:], BF16),
+            pltpu.VMEM(coupling.shape, F32),
+            pltpu.VMEM(table.shape, BF16),
+            pltpu.VMEM((1, size_z), jnp.int32),
+            pltpu.VMEM((1, npanels), jnp.int32),
+            pltpu.VMEM((1, npanels), jnp.int32),
+            pltpu.SemaphoreType.DMA((9,)),
+        ],
         compiler_params=params,
-        name="force",
-    )(panels.reshape(per_dev, panels.shape[3], spectral), coupling, table)
-    force_o = swap(force)
+        name="prepare",
+    )(*(
+        pltpu.with_memory_space_constraint(value, pltpu.HBM)
+        for value in (
+            panels.reshape((per_dev,) + panels.shape[3:]), coupling, table, layer_depth.reshape(1, -1),
+            panel_owner.reshape(1, -1), panel_block.reshape(1, -1), u_now, u_prev, lateral,
+        )
+    ))
+    ints_o = swap(ints)
     tiles = comps * size_x
-    extra = 2 * (force.shape[1] // size_z) * (per_dev // HALO)
-    state = (scal, layer_speed, u_now, u_prev, lateral, un_o, up_o, lat_o, ints, ints_o)
+    extra = 2 * (width // size_z) * (per_dev // HALO)
+    state = (scal, layer_speed, un_v, up_v, lat_v, un_o, up_o, lat_o, ints, ints_o)
     state_specs = [smem] * 2 + [vmem] * 8
     packed, pair = pl.pallas_call(
         pack_kernel,
         out_shape=(
             jax.ShapeDtypeStruct((2 * tiles + extra, HALO, size_z), F32),
-            jax.ShapeDtypeStruct((2,) + force.shape, F32),
+            jax.ShapeDtypeStruct((2, per_dev, width), F32),
         ),
-        in_specs=state_specs + [vmem] * 2,
+        in_specs=state_specs,
         out_specs=(vmem, vmem),
         compiler_params=params,
         name="pack",
-    )(*state, force, force_o)
+    )(*state)
     side = send(packed, sizes, route_y)
     if ny == 4:
         far = send(pair, sizes, lambda i, j, k: (i, j ^ 2 if k == 0 else 3 - j, k))
+        side, far = lax.optimization_barrier((side, far))
         side_o, far_o = swap(side), swap(far)
         sets = (pair, side, side_o, far, far_o)
     else:
@@ -520,7 +578,7 @@
         sets = (jnp.moveaxis(lax.all_gather(pair, "gy"), 0, 1).reshape(2, npanels, -1),)
     shared = state + (side, side_o) + sets
     shared_specs = state_specs + [vmem] * (2 + len(sets))
-    all_scratch = pltpu.VMEM((2, npanels, force.shape[1]), F32)
+    all_scratch = pltpu.VMEM((2, npanels, width), F32)
     planes = NSTEP * comps
     sent = pl.pallas_call(
         face_kernel,
@@ -552,6 +610,7 @@
         compiler_params=params,
         name="local",
     )(*shared)
+    final, before, face, ratef, recv = lax.optimization_barrier((final, before, face, ratef, recv))
     recv_o = swap(recv)
     return pl.pallas_call(
         join_kernel,

time: 48.4 us -> 34.6 us (0.71)
  waiting for transfers between devices: 19.1 us -> 7.85 us
  local copies, waits for them, and re-layouts: 4.45 us -> 0.65 us
  Pallas kernels: 14.1 us -> 15.3 us
    ppermute x11 -> x10, waiting for transfers between devices: 19.1 us -> 7.85 us  [send(): return lax.ppermute(value, ('gx', 'gy', 'gz'), pairs)]
    unnamed x14 -> x2, local copies, waits for them, and re-layouts: 3.64 us -> 0.65 us
    pallas_call x1, Pallas kernels: 0.46 us -> 1.59 us  [per_device(): pl.pallas_call(prepare_kernel, out_shape=(jax.ShapeDtypeStruct((per_dev +...]
    concatenate x1 -> x0, local copies, waits for them, and re-layouts: 0.81 us -> none  [per_device(): both = jnp.concatenate([layer_depth, owner, owner, block, block])]
    ppermute x11 -> x10, starting transfers between devices: 9.5 us -> 9.95 us  [send(): return lax.ppermute(value, ('gx', 'gy', 'gz'), pairs)]
  transfers between devices with their start and end apart: 11 -> 10, of which waited for: 5 -> 5; matrix products, arithmetic and copies ran while one was open for 2% -> 0% of each run, Pallas kernels for 20% -> 32%
where the time goes in v2:
time: 34.6 us; the launch traced here: 34.5 us
  Pallas kernels  15.3 us (44%)
  starting transfers between devices  9.95 us (29%)
  waiting for transfers between devices  7.85 us (23%)
  between operations  0.69 us (2%)
  local copies, waits for them, and re-layouts  0.65 us (2%)
    ppermute x10, starting transfers between devices, send(): return lax.ppermute(value, ('gx', 'gy', 'gz'), pairs)  9.95 us
    pallas_call x1, Pallas kernels, per_device(): pl.pallas_call(local_kernel, out_shape=(jax.ShapeDtypeStruct(u_now.shape,...  9.34 us
    ppermute x10, waiting for transfers between devices, send(): return lax.ppermute(value, ('gx', 'gy', 'gz'), pairs)  7.85 us
    pallas_call x1, Pallas kernels, per_device(): pl.pallas_call(join_kernel, out_shape=(jax.ShapeDtypeStruct(u_now.shape,...  2.37 us
    pallas_call x1, Pallas kernels, per_device(): pl.pallas_call(prepare_kernel, out_shape=(jax.ShapeDtypeStruct((per_dev +...  1.59 us
    pallas_call x1, Pallas kernels, per_device(): pl.pallas_call(face_kernel, out_shape=jax.ShapeDtypeStruct((2, planes + 2...  1.34 us
  transfers between devices with their start and end apart: 10, of which 5 were waited for; matrix products, arithmetic and copies ran while one was open for 0% of the time, Pallas kernels for 32%

profile of v2, /device:TPU:0, one launch (start us, length us, event | category | flops | bytes accessed | tf_op | source)
XLA Modules:
  0.0 34.5 jit_solution(10071781997080582033)
XLA Ops:
  0.6 0.5 %collective-permute-start = (f32[3,16,16,128]{3,2,1,0:T(8,128)}, f32[3,16,16,128]{3,2,1,0:T(8,128)S(1)}, u32[]{:S(2)}, u32[]{:S(2)}) collective-permute-start(f32[3,16,16,128]{3,2,1,0:T(8,128)} %un_hbm.1), channel_id=1, source_target_pairs={{0,1},{1,0},{2,3},{3,2},{4,5},{5,4},{6,7},{7,6},{8,9},{9,8},{10,11... | collective-permute-start | bytes 1179656 | tf_op jit(solution)/shard_map/ppermute | solution.py:482
  1.2 0.1 collective-permute-start.1
  1.2 0.4 %collective-permute-start.2 = (f32[16,16,128]{2,1,0:T(8,128)}, f32[16,16,128]{2,1,0:T(8,128)S(1)}, u32[]{:S(2)}, u32[]{:S(2)}) collective-permute-start(f32[16,16,128]{2,1,0:T(8,128)} %lat_hbm.1), channel_id=1, source_target_pairs={{0,1},{1,0},{2,3},{3,2},{4,5},{5,4},{6,7},{7,6},{8,9},{9,8},{10,11... | collective-permute-start | bytes 393224 | tf_op jit(solution)/shard_map/ppermute | solution.py:482
  1.7 1.6 %prepare.1 = (f32[24,256]{1,0:T(8,128)S(1)}, f32[3,16,16,128]{3,2,1,0:T(8,128)S(1)}, f32[3,16,16,128]{3,2,1,0:T(8,128)S(1)}, f32[16,16,128]{2,1,0:T(8,128)S(1)}) custom-call(bf16[16,48,256]{2,1,0:T(8,128)(2,1)} %bitcast.7, f32[3,16,16]{2,1,0:T(8,128)} %coupling_hbm.1, bf16[256,256]{1,0:T(8,128)(2,1)} %constant.15.clone.table_hbm, s32[1,128]{1,0:T(1,128)} %bitcast.8, ...), custom_call_target="tpu_custom_call" | custom-call | tf_op jit(solution)/shard_map/prepare/pallas_call | solution.py:526
  3.3 0.1 collective-permute-start.3
  3.4 0.1 pad_add_fusion.scal_ref
  3.5 1.0 %collective-permute-done.3.intso_ref = f32[24,256]{1,0:T(8,128)S(1)} collective-permute-done((f32[24,256]{1,0:T(8,128)S(1)}, f32[24,256]{1,0:T(8,128)S(1)}, u32[]{:S(2)}, u32[]{:S(2)}) %collective-permute-start.3) | collective-permute-done | bytes 24608 | tf_op jit(solution)/shard_map/ppermute | solution.py:482
  4.5 0.0 collective-permute-done.2.lato_ref
  4.5 0.0 collective-permute-done.uno_ref
  4.5 0.0 collective-permute-done.1.upo_ref
  4.5 0.0 copy-start
  4.5 0.6 %copy-done = f32[8]{0:T(128)S(1)} copy-done((f32[8]{0:T(128)S(1)}, f32[8]{0:T(128)}, u32[]{:S(2)}) %copy-start) | copy-done | bytes 56
  5.2 0.6 %pack.1 = (f32[104,8,128]{2,1,0:T(8,128)S(1)}, f32[2,16,256]{2,1,0:T(8,128)S(1)}) custom-call(s32[5]{0:T(128)S(1)} %pad_add_fusion.scal_ref, f32[8]{0:T(128)S(1)} %copy-done, f32[3,16,16,128]{3,2,1,0:T(8,128)S(1)} %get-tuple-element.19.un_ref, f32[3,16,16,128]{3,2,1,0:T(8,128)S(1)} %get-tuple-element.20.up_ref, ...), custom_call_target="tpu_custom_call" | custom-call | tf_op jit(solution)/shard_map/pack/pallas_call | solution.py:559
  5.8 2.8 %collective-permute-start.4 = (f32[104,8,128]{2,1,0:T(8,128)S(1)}, f32[104,8,128]{2,1,0:T(8,128)S(1)}, u32[]{:S(2)}, u32[]{:S(2)}) collective-permute-start(f32[104,8,128]{2,1,0:T(8,128)S(1)} %get-tuple-element.23), channel_id=1, source_target_pairs={{0,2},{1,9},{2,0},{3,5},{4,6},{5,3},{6,4},{7,15},{8,10},{9,1},{10,... | collective-permute-start | bytes 1277960 | tf_op jit(solution)/shard_map/ppermute | solution.py:482
  8.6 2.6 %collective-permute-start.5 = (f32[2,16,256]{2,1,0:T(8,128)S(1)}, f32[2,16,256]{2,1,0:T(8,128)S(1)}, u32[]{:S(2)}, u32[]{:S(2)}) collective-permute-start(f32[2,16,256]{2,1,0:T(8,128)S(1)} %get-tuple-element.24.rest_0_), channel_id=1, source_target_pairs={{0,4},{1,7},{2,6},{3,5},{4,0},{5,3},{6,2},{7,1},{8,12},{9,15},{10,... | collective-permute-start | bytes 98312 | tf_op jit(solution)/shard_map/ppermute | solution.py:482
  11.2 3.8 %collective-permute-done.5.rest_3_ = f32[2,16,256]{2,1,0:T(8,128)S(1)} collective-permute-done((f32[2,16,256]{2,1,0:T(8,128)S(1)}, f32[2,16,256]{2,1,0:T(8,128)S(1)}, u32[]{:S(2)}, u32[]{:S(2)}) %collective-permute-start.5) | collective-permute-done | bytes 32800 | tf_op jit(solution)/shard_map/ppermute | solution.py:482
  15.0 0.5 %collective-permute-done.4.side_ref.rest_1_ = f32[104,8,128]{2,1,0:T(8,128)S(1)} collective-permute-done((f32[104,8,128]{2,1,0:T(8,128)S(1)}, f32[104,8,128]{2,1,0:T(8,128)S(1)}, u32[]{:S(2)}, u32[]{:S(2)}) %collective-permute-start.4) | collective-permute-done | bytes 426016 | tf_op jit(solution)/shard_map/ppermute | solution.py:482
  15.4 0.0 collective-permute-start.6
  15.4 0.5 %collective-permute-start.7 = (f32[2,16,256]{2,1,0:T(8,128)S(1)}, f32[2,16,256]{2,1,0:T(8,128)S(1)}, u32[]{:S(2)}, u32[]{:S(2)}) collective-permute-start(f32[2,16,256]{2,1,0:T(8,128)S(1)} %collective-permute-done.5.rest_3_), channel_id=1, source_target_pairs={{0,1},{1,0},{2,3},{3,2},{4,5},{5,4},{6,7},{7,6},{8,9},{9,8},{10,11... | collective-permute-start | bytes 98312 | tf_op jit(solution)/shard_map/ppermute | solution.py:482
  15.9 1.3 %collective-permute-done.7.rest_4_ = f32[2,16,256]{2,1,0:T(8,128)S(1)} collective-permute-done((f32[2,16,256]{2,1,0:T(8,128)S(1)}, f32[2,16,256]{2,1,0:T(8,128)S(1)}, u32[]{:S(2)}, u32[]{:S(2)}) %collective-permute-start.7) | collective-permute-done | bytes 32800 | tf_op jit(solution)/shard_map/ppermute | solution.py:482
  17.3 0.0 collective-permute-done.6.sideo_ref.rest_2_
  17.3 1.3 %face.1 = f32[2,14,24,128]{3,2,1,0:T(8,128)S(1)} custom-call(s32[5]{0:T(128)S(1)} %pad_add_fusion.scal_ref, f32[8]{0:T(128)S(1)} %copy-done, f32[3,16,16,128]{3,2,1,0:T(8,128)S(1)} %get-tuple-element.19.un_ref, f32[3,16,16,128]{3,2,1,0:T(8,128)S(1)} %get-tuple-element.20.up_ref, f32[16,16,128]{2,1,0:T(8,128)S(1)} %get-tuple-element.21.lat_ref, ...), custom_call_target="tpu_custom_call" | custom-call | tf_op jit(solution)/shard_map/face/pallas_call | solution.py:583
  18.6 2.0 %collective-permute-start.8 = (f32[2,14,24,128]{3,2,1,0:T(8,128)S(1)}, f32[2,14,24,128]{3,2,1,0:T(8,128)S(1)}, u32[]{:S(2)}, u32[]{:S(2)}) collective-permute-start(f32[2,14,24,128]{3,2,1,0:T(8,128)S(1)} %face.1), channel_id=1, source_target_pairs={{0,8},{1,25},{2,10},{3,27},{4,12},{5,29},{6,14},{7,31},{8,0},{9,17... | collective-permute-start | bytes 1032200 | tf_op jit(solution)/shard_map/ppermute | solution.py:482
  20.6 9.3 %local.1 = (f32[3,16,16,128]{3,2,1,0:T(8,128)S(1)}, f32[3,16,16,128]{3,2,1,0:T(8,128)S(1)}, f32[2,2,12,24,128]{4,3,2,1,0:T(8,128)S(1)}, f32[2,2,4,24,128]{4,3,2,1,0:T(8,128)S(1)}) custom-call(s32[5]{0:T(128)S(1)} %pad_add_fusion.scal_ref, f32[8]{0:T(128)S(1)} %copy-done, f32[3,16,16,128]{3,2,1,0:T(8,128)S(1)} %get-tuple-element.19.un_ref, ...), custom_call_target="tpu_custom_call" | custom-call | tf_op jit(solution)/shard_map/local/pallas_call | solution.py:593
  29.9 0.0 collective-permute-done.8.recv_ref
  30.0 0.9 %collective-permute-start.9 = (f32[2,14,24,128]{3,2,1,0:T(8,128)S(1)}, f32[2,14,24,128]{3,2,1,0:T(8,128)S(1)}, u32[]{:S(2)}, u32[]{:S(2)}) collective-permute-start(f32[2,14,24,128]{3,2,1,0:T(8,128)S(1)} %collective-permute-done.8.recv_ref), channel_id=1, source_target_pairs={{0,1},{1,0},{2,3},{3,2},{4,5},{5,4},{6,7},{7,6},{8,9},{9,8},{10,11... | collective-permute-start | bytes 1032200 | tf_op jit(solution)/shard_map/ppermute | solution.py:482
  30.8 1.3 %collective-permute-done.9.recvo_ref = f32[2,14,24,128]{3,2,1,0:T(8,128)S(1)} collective-permute-done((f32[2,14,24,128]{3,2,1,0:T(8,128)S(1)}, f32[2,14,24,128]{3,2,1,0:T(8,128)S(1)}, u32[]{:S(2)}, u32[]{:S(2)}) %collective-permute-start.9) | collective-permute-done | bytes 344096 | tf_op jit(solution)/shard_map/ppermute | solution.py:482
  32.1 2.4 %join.1 = (f32[3,16,16,128]{3,2,1,0:T(8,128)}, f32[3,16,16,128]{3,2,1,0:T(8,128)}) custom-call(s32[5]{0:T(128)S(1)} %pad_add_fusion.scal_ref, f32[3,16,16,128]{3,2,1,0:T(8,128)S(1)} %get-tuple-element.31.final_in, f32[3,16,16,128]{3,2,1,0:T(8,128)S(1)} %get-tuple-element.32.before_in, f32[2,2,12,24,128]{4,3,2,1,0:T(8,128)S(1)} %get-tuple-element.33.face_ref, ...), custom_call_target="tpu_custom_call" | custom-call | tf_op jit(solution)/shard_map/join/pallas_call | solution.py:615
  (1 shorter events, 0.0 us)
Async XLA Ops:
  0.6 3.9 %collective-permute-start = (f32[3,16,16,128]{3,2,1,0:T(8,128)}, f32[3,16,16,128]{3,2,1,0:T(8,128)S(1)}, u32[]{:S(2)}, u32[]{:S(2)}) collective-permute-start(f32[3,16,16,128]{3,2,1,0:T(8,128)} %un_hbm.1), channel_id=1, source_target_pairs={{0,1},{1,0},{2,3},{3,2},{4,5},{5,4},{6,7},{7,6},{8,9},{9,8},{10,11... | collective-permute-start | bytes 1179656 | tf_op jit(solution)/shard_map/ppermute | solution.py:482
  1.2 3.4 %collective-permute-start.1 = (f32[3,16,16,128]{3,2,1,0:T(8,128)}, f32[3,16,16,128]{3,2,1,0:T(8,128)S(1)}, u32[]{:S(2)}, u32[]{:S(2)}) collective-permute-start(f32[3,16,16,128]{3,2,1,0:T(8,128)} %up_hbm.1), channel_id=1, source_target_pairs={{0,1},{1,0},{2,3},{3,2},{4,5},{5,4},{6,7},{7,6},{8,9},{9,8},{10,11... | collective-permute-start | bytes 1179656 | tf_op jit(solution)/shard_map/ppermute | solution.py:482
  1.2 3.3 %collective-permute-start.2 = (f32[16,16,128]{2,1,0:T(8,128)}, f32[16,16,128]{2,1,0:T(8,128)S(1)}, u32[]{:S(2)}, u32[]{:S(2)}) collective-permute-start(f32[16,16,128]{2,1,0:T(8,128)} %lat_hbm.1), channel_id=1, source_target_pairs={{0,1},{1,0},{2,3},{3,2},{4,5},{5,4},{6,7},{7,6},{8,9},{9,8},{10,11... | collective-permute-start | bytes 393224 | tf_op jit(solution)/shard_map/ppermute | solution.py:482
  3.3 1.3 %collective-permute-start.3 = (f32[24,256]{1,0:T(8,128)S(1)}, f32[24,256]{1,0:T(8,128)S(1)}, u32[]{:S(2)}, u32[]{:S(2)}) collective-permute-start(f32[24,256]{1,0:T(8,128)S(1)} %get-tuple-element.22.ints_ref), channel_id=1, source_target_pairs={{0,1},{1,0},{2,3},{3,2},{4,5},{5,4},{6,7},{7,6},{8,9},{9,8},{10,11... | collective-permute-start | bytes 73736 | tf_op jit(solution)/shard_map/ppermute | solution.py:482
  4.5 0.7 %copy-start = (f32[8]{0:T(128)S(1)}, f32[8]{0:T(128)}, u32[]{:S(2)}) copy-start(f32[8]{0:T(128)} %speed_ref.5) | copy-start | bytes 100
  5.8 9.6 %collective-permute-start.4 = (f32[104,8,128]{2,1,0:T(8,128)S(1)}, f32[104,8,128]{2,1,0:T(8,128)S(1)}, u32[]{:S(2)}, u32[]{:S(2)}) collective-permute-start(f32[104,8,128]{2,1,0:T(8,128)S(1)} %get-tuple-element.23), channel_id=1, source_target_pairs={{0,2},{1,9},{2,0},{3,5},{4,6},{5,3},{6,4},{7,15},{8,10},{9,1},{10,... | collective-permute-start | bytes 1277960 | tf_op jit(solution)/shard_map/ppermute | solution.py:482
  8.6 6.3 %collective-permute-start.5 = (f32[2,16,256]{2,1,0:T(8,128)S(1)}, f32[2,16,256]{2,1,0:T(8,128)S(1)}, u32[]{:S(2)}, u32[]{:S(2)}) collective-permute-start(f32[2,16,256]{2,1,0:T(8,128)S(1)} %get-tuple-element.24.rest_0_), channel_id=1, source_target_pairs={{0,4},{1,7},{2,6},{3,5},{4,0},{5,3},{6,2},{7,1},{8,12},{9,15},{10,... | collective-permute-start | bytes 98312 | tf_op jit(solution)/shard_map/ppermute | solution.py:482
  15.4 1.8 %collective-permute-start.6 = (f32[104,8,128]{2,1,0:T(8,128)S(1)}, f32[104,8,128]{2,1,0:T(8,128)S(1)}, u32[]{:S(2)}, u32[]{:S(2)}) collective-permute-start(f32[104,8,128]{2,1,0:T(8,128)S(1)} %collective-permute-done.4.side_ref.rest_1_), channel_id=1, source_target_pairs={{0,1},{1,0},{2,3},{3,2},{4,5},{5,4},{6,7},{7,6},{8,9},{9,8},{10,11... | collective-permute-start | bytes 1277960 | tf_op jit(solution)/shard_map/ppermute | solution.py:482
  15.4 1.8 %collective-permute-start.7 = (f32[2,16,256]{2,1,0:T(8,128)S(1)}, f32[2,16,256]{2,1,0:T(8,128)S(1)}, u32[]{:S(2)}, u32[]{:S(2)}) collective-permute-start(f32[2,16,256]{2,1,0:T(8,128)S(1)} %collective-permute-done.5.rest_3_), channel_id=1, source_target_pairs={{0,1},{1,0},{2,3},{3,2},{4,5},{5,4},{6,7},{7,6},{8,9},{9,8},{10,11... | collective-permute-start | bytes 98312 | tf_op jit(solution)/shard_map/ppermute | solution.py:482
  18.6 11.3 %collective-permute-start.8 = (f32[2,14,24,128]{3,2,1,0:T(8,128)S(1)}, f32[2,14,24,128]{3,2,1,0:T(8,128)S(1)}, u32[]{:S(2)}, u32[]{:S(2)}) collective-permute-start(f32[2,14,24,128]{3,2,1,0:T(8,128)S(1)} %face.1), channel_id=1, source_target_pairs={{0,8},{1,25},{2,10},{3,27},{4,12},{5,29},{6,14},{7,31},{8,0},{9,17... | collective-permute-start | bytes 1032200 | tf_op jit(solution)/shard_map/ppermute | solution.py:482
  30.0 2.2 %collective-permute-start.9 = (f32[2,14,24,128]{3,2,1,0:T(8,128)S(1)}, f32[2,14,24,128]{3,2,1,0:T(8,128)S(1)}, u32[]{:S(2)}, u32[]{:S(2)}) collective-permute-start(f32[2,14,24,128]{3,2,1,0:T(8,128)S(1)} %collective-permute-done.8.recv_ref), channel_id=1, source_target_pairs={{0,1},{1,0},{2,3},{3,2},{4,5},{5,4},{6,7},{7,6},{8,9},{9,8},{10,11... | collective-permute-start | bytes 1032200 | tf_op jit(solution)/shard_map/ppermute | solution.py:482

commit v3 on v2

--- a/solution.py
+++ b/solution.py
@@ -13,6 +13,7 @@
 HALO = 8
 LANES = 128
 PANELS = 16
+TOP = 32767.0
 F32 = jnp.float32
 BF16 = jnp.bfloat16
 
@@ -60,28 +61,66 @@
     return sum0, sum1
 
 
-def speed_row(ints_ref, speed_ref):
-    depth = integers(ints_ref, LANES, 0)
-    row = jnp.zeros(depth.shape, F32)
-    for layer in range(speed_ref.shape[0]):
-        row = jnp.where(depth == layer, speed_ref[layer], row)
-    return row
+def row_scales(exponents):
+    return jnp.exp2(exponents) * (1.0 / TOP)
+
+
+def quantize(tiles_ref, out_ref):
+    number = tiles_ref.shape[0]
+    lane = iota(tiles_ref.shape[1:], 1)
+    peak = jnp.zeros(tiles_ref.shape[1:], F32)
+    for t in range(number):
+        peak = jnp.where(lane == t, jnp.max(jnp.abs(tiles_ref[t]), axis=1, keepdims=True), peak)
+    exponents = jnp.ceil(jnp.log2(jnp.maximum(peak, 1e-30)))
+    factor = jnp.exp2(-exponents) * TOP
+
+    def coded(t):
+        scaled = jnp.round(tiles_ref[t] * factor[:, t:t + 1])
+        return jnp.clip(scaled, -TOP, TOP).astype(jnp.int32)
+
+    zero = jnp.zeros(tiles_ref.shape[1:], jnp.int32)
+    parts = [coded(t) for t in range(number)] + [zero] * (number % 2)
+    parts += [exponents.astype(jnp.int32), zero]
+    for i in range(out_ref.shape[0]):
+        out_ref[i] = jnp.concatenate(parts[2 * i:2 * i + 2], axis=0).astype(jnp.int16)
+
+
+def coded_shape(number):
+    return ((number + 1) // 2 + 1, 2 * HALO, LANES)
+
+
+def scales_of(ref):
+    return row_scales(ref[ref.shape[0] - 1].astype(jnp.int32)[0:HALO].astype(F32))
+
+
+def expand(ref, tiles_ref, blocks):
+    for at, scale in blocks:
+        pair = ref[at].astype(jnp.int32).astype(F32)
+        tiles_ref[2 * at] = pair[0:HALO] * scale[0]
+        tiles_ref[2 * at + 1] = pair[HALO:] * scale[1]
+
+
+def expand_all(ref, tiles_ref):
+    scale = scales_of(ref)
+    expand(ref, tiles_ref, [
+        (i, (scale[:, 2 * i:2 * i + 1], scale[:, 2 * i + 1:2 * i + 2])) for i in range(tiles_ref.shape[0] // 2)
+    ])
 
 
 def prepare_kernel(
-    panels_hbm, coupling_hbm, table_hbm, depth_hbm, owner_hbm, block_hbm, un_hbm, up_hbm, lat_hbm,
+    panels_hbm, coupling_hbm, table_hbm, depth_hbm, owner_hbm, block_hbm, speed_hbm, un_hbm, up_hbm, lat_hbm,
     out_ref, un_ref, up_ref, lat_ref,
-    panels_ref, coupling_ref, table_ref, depth_ref, owner_ref, block_ref, sems,
+    panels_ref, coupling_ref, table_ref, depth_ref, owner_ref, block_ref, speed_ref, sems,
 ):
     pairs = (
         (panels_hbm, panels_ref), (table_hbm, table_ref), (coupling_hbm, coupling_ref),
-        (depth_hbm, depth_ref), (owner_hbm, owner_ref), (block_hbm, block_ref),
+        (depth_hbm, depth_ref), (owner_hbm, owner_ref), (block_hbm, block_ref), (speed_hbm, speed_ref),
         (un_hbm, un_ref), (up_hbm, up_ref), (lat_hbm, lat_ref),
     )
     copies = [pltpu.make_async_copy(src, dst, sems.at[i]) for i, (src, dst) in enumerate(pairs)]
     for copy in copies:
         copy.start()
-    for copy in copies[:6]:
+    for copy in copies[:7]:
         copy.wait()
     count, rows, spectral = panels_ref.shape
     comps, block = 3, rows // 3
@@ -103,31 +142,34 @@
     spread = jnp.where(same, spread, 0.0)
     out_ref[0:count] = jnp.sum(free.reshape(count, rows, lanes) * spread[None], axis=1)
     out_ref[count:] = jnp.zeros((out_ref.shape[0] - count, lanes), F32)
-    pieces = [depth_ref[...]]
+    speed = jnp.zeros(depth_ref.shape, F32)
+    for layer in range(speed_ref.shape[0]):
+        speed = jnp.where(depth_ref[...] == layer, speed_ref[layer], speed)
+    pieces = [speed]
     for ref in (owner_ref, block_ref):
         twice = jnp.concatenate([ref[...], ref[...]], axis=1)
         pieces += [twice[:, i:i + LANES] for i in range(0, twice.shape[1], LANES)]
     for i, piece in enumerate(pieces):
         row, at = count + i * LANES // lanes, i * LANES % lanes
         out_ref[row:row + 1, at:at + LANES] = piece.astype(F32)
-    for copy in copies[6:]:
+    for copy in copies[7:]:
         copy.wait()
 
 
-def integers(ref, panels, which):
+def listed(ref, panels, which):
     lanes = ref.shape[1]
     width = -(-2 * panels // LANES)
     first, number = ((0, 1), (1, width), (1 + width, width))[which]
     out = []
     for i in range(first, first + number):
         row, at = PANELS + i * LANES // lanes, i * LANES % lanes
-        out.append(ref[row:row + 1, at:at + LANES].astype(jnp.int32))
+        out.append(ref[row:row + 1, at:at + LANES])
     return jnp.concatenate(out, axis=1)
 
 
 def pack_kernel(
-    scal_ref, speed_ref, un_ref, up_ref, lat_ref, uno_ref, upo_ref, lato_ref, ints_ref, intso_ref,
-    out_ref, pair_ref,
+    scal_ref, un_ref, up_ref, lat_ref, uno_ref, upo_ref, lato_ref, ints_ref, intso_ref,
+    coded_ref, pair_ref, out_ref,
 ):
     mine = scal_ref[2]
     high = lax.rem(scal_ref[1] + mine, 2) == 0
@@ -142,7 +184,7 @@
             (mine, un_ref, up_ref, lat_ref, ints_ref),
             (1 - mine, uno_ref, upo_ref, lato_ref, intso_ref),
         ):
-            rate = lat[:, base:base + HALO, :] * speed_row(ints, speed_ref)[None]
+            rate = lat[:, base:base + HALO, :] * listed(ints, LANES, 0)[None]
             for c in range(comps):
                 now = un[c, :, base:base + HALO, :]
                 old = spin(up[c, :, base:base + HALO, :], HALO // 2, 1)
@@ -167,6 +209,7 @@
             for piece in range(count // HALO):
                 at = 2 * tiles + (z_at * (lanes // size_z) + part) * (count // HALO) + piece
                 out_ref[at] = force[piece * HALO:(piece + 1) * HALO, part * size_z:(part + 1) * size_z]
+    quantize(out_ref, coded_ref)
 
 
 def place_forces(scal_ref, sets, all_ref):
@@ -201,8 +244,8 @@
 
 
 def panel_keys(ints_ref, o, panels, rows, size_x, size_y, zblocks):
-    owner = integers(ints_ref, panels, 1)
-    block = integers(ints_ref, panels, 2)
+    owner = listed(ints_ref, panels, 1).astype(jnp.int32)
+    block = listed(ints_ref, panels, 2).astype(jnp.int32)
     depth = block & (zblocks - 1)
     y = (block >> shift_of(zblocks)) & (size_y - 1)
     x = block >> (shift_of(zblocks) + shift_of(size_y))
@@ -262,16 +305,28 @@
 
 
 def face_kernel(
-    scal_ref, speed_ref, un_ref, up_ref, lat_ref, uno_ref, upo_ref, lato_ref, ints_ref, intso_ref,
-    side_ref, sideo_ref, *rest,
+    scal_ref, un_ref, up_ref, lat_ref, uno_ref, upo_ref, lato_ref, ints_ref, intso_ref,
+    coded_ref, codedo_ref, *rest,
 ):
-    *sets, out_ref, all_ref = rest
+    *sets, out_ref, all_ref, side_ref, sideo_ref, faces_ref = rest
     comps, size_x, size_y, size_z = un_ref.shape
     rows = size_y + HALO
     tiles = comps * size_x
     a, o, mine = scal_ref[0], scal_ref[1], scal_ref[2]
     high = lax.rem(a + mine, 2) == 0
-    forces = place_forces(scal_ref, sets, all_ref)
+    skip = jnp.where(high, size_x - NSTEP, 0)
+    for ref, tiles_ref in ((coded_ref, side_ref), (codedo_ref, sideo_ref)):
+        scale = scales_of(ref)
+        moved = pltpu.roll(scale, lax.rem(LANES - skip, LANES), 1)
+        blocks = []
+        for first in range(0, 2 * tiles, size_x):
+            for i in range(first, first + NSTEP, 2):
+                at = i // 2 + lax.div(skip, 2)
+                blocks.append((at, (moved[:, i:i + 1], moved[:, i + 1:i + 2])))
+        for i in range(2 * tiles, tiles_ref.shape[0], 2):
+            blocks.append((i // 2, (scale[:, i:i + 1], scale[:, i + 1:i + 2])))
+        expand(ref, tiles_ref, blocks)
+    forces = place_forces(scal_ref, with_sides(sets, side_ref, sideo_ref), all_ref)
     panels = forces.shape[1]
     own = mine == 0
     now, old, rate, drive = {}, {}, {}, {}
@@ -292,8 +347,8 @@
                     )
         speed = jnp.where(
             own if z == 0 else jnp.logical_not(own),
-            speed_row(ints_ref, speed_ref),
-            speed_row(intso_ref, speed_ref),
+            listed(ints_ref, LANES, 0),
+            listed(intso_ref, LANES, 0),
         )
         near = own if z == 0 else jnp.logical_not(own)
         for d in range(1, NSTEP + 1):
@@ -312,11 +367,7 @@
             if d < NSTEP:
                 centre = jnp.where(near, lat_ref[x], lato_ref[x]) * speed
                 rate[z, d] = jnp.concatenate([centre, halo_rate(ups, lows)], axis=0)
-    for z in range(2):
-        for c in range(comps):
-            out_ref[z, c] = now[z, 1, c]
-        for d in (1, 2):
-            out_ref[z, NSTEP * comps + d - 1] = rate[z, d]
+    series = {(z, 0, c): now[z, 1, c] for z in range(2) for c in range(comps)}
     for n in range(1, NSTEP):
         later = {}
         for d in range(1, NSTEP - n + 1):
@@ -332,7 +383,54 @@
         old, now = now, later
         for z in range(2):
             for c in range(comps):
-                out_ref[z, n * comps + c] = now[z, 1, c]
+                series[z, n, c] = now[z, 1, c]
+    sub = iota((HALO, size_z), 0)
+    middle = (sub == HALO // 2 - 1) | (sub == HALO // 2)
+    ends = (sub < 2) | (sub >= HALO - 2)
+    for z in range(2):
+        planes = [series[z, n, c] for n in range(NSTEP) for c in range(comps)] + [rate[z, 1], rate[z, 2]]
+        rims = [plane[size_y:rows] for plane in planes]
+        tails = [jnp.where(middle, spin(rims[2 * comps + c], HALO // 2, 0), rims[c]) for c in range(comps)]
+        tails.append(jnp.where(ends, rims[comps], spin(rims[comps + 1], HALO // 2, 0)))
+        tails.append(jnp.where(ends, rims[comps + 2], spin(rims[NSTEP * comps], HALO // 2, 0)))
+        base = z * face_tiles(comps)
+        for i, plane in enumerate(planes):
+            for half in range(2):
+                faces_ref[base + 2 * i + half] = plane[half * HALO:(half + 1) * HALO]
+        for i, tail in enumerate(tails):
+            faces_ref[base + 2 * len(planes) + i] = tail
+    quantize(faces_ref, out_ref)
+
+
+def face_tiles(comps):
+    return 2 * (NSTEP * comps + 2) + comps + 2
+
+
+def face_plane(tiles_ref, z, i, comps):
+    count = NSTEP * comps + 2
+    base = z * face_tiles(comps)
+    tail = base + 2 * count
+    parts = [tiles_ref[base + 2 * i], tiles_ref[base + 2 * i + 1]]
+    turned = lambda at: spin(tiles_ref[at], HALO // 2, 0)
+    if i < comps:
+        parts.append(tiles_ref[tail + i])
+    elif i < comps + 3:
+        at, other = ((tail + comps, False), (tail + comps, True), (tail + comps + 1, False))[i - comps]
+        parts.append(turned(at) if other else tiles_ref[at])
+    elif 2 * comps <= i < 3 * comps:
+        parts.append(turned(tail + i - 2 * comps))
+    elif i == NSTEP * comps:
+        parts.append(turned(tail + comps + 1))
+    else:
+        parts.append(jnp.zeros(parts[0].shape, F32))
+    return jnp.concatenate(parts, axis=0)
+
+
+def with_sides(sets, side_ref, sideo_ref):
+    if len(sets) == 1:
+        return sets
+    own_ref, far_ref, faro_ref = sets
+    return own_ref, side_ref, sideo_ref, far_ref, faro_ref
 
 
 def panel_keys_of(z, own, ints_ref, intso_ref, o, panels, rows, size_x, size_y, size_z):
@@ -344,15 +442,18 @@
 
 
 def local_kernel(
-    scal_ref, speed_ref, un_ref, up_ref, lat_ref, uno_ref, upo_ref, lato_ref, ints_ref, intso_ref,
-    side_ref, sideo_ref, *rest,
+    scal_ref, un_ref, up_ref, lat_ref, uno_ref, upo_ref, lato_ref, ints_ref, intso_ref,
+    coded_ref, codedo_ref, *rest,
 ):
-    *sets, final_ref, before_ref, face_ref, ratef_ref, all_ref, now_ref, old_ref, rate_ref, drive_ref = rest
+    *sets, final_ref, before_ref, face_ref, ratef_ref, all_ref, side_ref, sideo_ref = rest[:-4]
+    now_ref, old_ref, rate_ref, drive_ref = rest[-4:]
     comps, size_x, size_y, size_z = un_ref.shape
     rows = size_y + HALO
     tiles = comps * size_x
     o, mine = scal_ref[1], scal_ref[2]
-    forces = place_forces(scal_ref, sets, all_ref)
+    expand_all(coded_ref, side_ref)
+    expand_all(codedo_ref, sideo_ref)
+    forces = place_forces(scal_ref, with_sides(sets, side_ref, sideo_ref), all_ref)
     panels = forces.shape[1]
     own = mine == 0
     for z in range(2):
@@ -375,7 +476,7 @@
         (mine, un_ref, up_ref, lat_ref, ints_ref),
         (1 - mine, uno_ref, upo_ref, lato_ref, intso_ref),
     ):
-        speed = speed_row(ints, speed_ref)
+        speed = listed(ints, LANES, 0)
         ups, lows = [], []
         for c in range(comps):
             upper, lower = sides(scal_ref, side_ref, sideo_ref, pl.ds(z_at * tiles + c * size_x, size_x))
@@ -411,7 +512,7 @@
                     )
             return carry
 
-        lax.fori_loop(0, size_x, step, 0)
+        lax.fori_loop(0, size_x, step, 0, unroll=4)
     now, old = refs[NSTEP % 2], refs[(NSTEP + 1) % 2]
     for c in range(comps):
         final_ref[c] = now[mine, c, 1:size_x + 1, 0:size_y]
@@ -419,12 +520,15 @@
 
 
 def join_kernel(
-    scal_ref, final_in, before_in, face_ref, ratef_ref, recv_ref, recvo_ref, final_ref, before_ref
+    scal_ref, final_in, before_in, face_ref, ratef_ref, coded_ref, codedo_ref, final_ref, before_ref,
+    recv_ref, recvo_ref,
 ):
     comps, size_x, size_y, size_z = final_in.shape
     a, mine = scal_ref[0], scal_ref[2]
     own = mine == 0
     high = lax.rem(a + mine, 2) == 0
+    expand_all(coded_ref, recv_ref)
+    expand_all(codedo_ref, recvo_ref)
     final_ref[...] = final_in[...]
     before_ref[...] = before_in[...]
     for side in range(2):
@@ -433,7 +537,7 @@
         inside = a < scal_ref[3] - 1 if is_high else a > 0
 
         def theirs(z, at):
-            return jnp.where(inside, jnp.where(here, recv_ref[z, at], recvo_ref[z, at]), 0.0)
+            return jnp.where(inside, jnp.where(here, face_plane(recv_ref, z, at, comps), face_plane(recvo_ref, z, at, comps)), 0.0)
 
         rate = {}
         for z in range(2):
@@ -531,7 +635,7 @@
             jax.ShapeDtypeStruct(u_prev.shape, F32),
             jax.ShapeDtypeStruct(lateral.shape, F32),
         ),
-        in_specs=[pl.BlockSpec(memory_space=pl.ANY)] * 9,
+        in_specs=[pl.BlockSpec(memory_space=pl.ANY)] * 10,
         out_specs=(vmem,) * 4,
         scratch_shapes=[
             pltpu.VMEM((per_dev,) + panels.shape[3:], BF16),
@@ -540,7 +644,8 @@
             pltpu.VMEM((1, size_z), jnp.int32),
             pltpu.VMEM((1, npanels), jnp.int32),
             pltpu.VMEM((1, npanels), jnp.int32),
-            pltpu.SemaphoreType.DMA((9,)),
+            pltpu.SMEM(layer_speed.shape, F32),
+            pltpu.SemaphoreType.DMA((10,)),
         ],
         compiler_params=params,
         name="prepare",
@@ -548,22 +653,24 @@
         pltpu.with_memory_space_constraint(value, pltpu.HBM)
         for value in (
             panels.reshape((per_dev,) + panels.shape[3:]), coupling, table, layer_depth.reshape(1, -1),
-            panel_owner.reshape(1, -1), panel_block.reshape(1, -1), u_now, u_prev, lateral,
+            panel_owner.reshape(1, -1), panel_block.reshape(1, -1), layer_speed, u_now, u_prev, lateral,
         )
     ))
     ints_o = swap(ints)
     tiles = comps * size_x
     extra = 2 * (width // size_z) * (per_dev // HALO)
-    state = (scal, layer_speed, un_v, up_v, lat_v, un_o, up_o, lat_o, ints, ints_o)
-    state_specs = [smem] * 2 + [vmem] * 8
+    state = (scal, un_v, up_v, lat_v, un_o, up_o, lat_o, ints, ints_o)
+    state_specs = [smem] + [vmem] * 8
+    tiles_scratch = pltpu.VMEM((2 * tiles + extra, HALO, size_z), F32)
     packed, pair = pl.pallas_call(
         pack_kernel,
         out_shape=(
-            jax.ShapeDtypeStruct((2 * tiles + extra, HALO, size_z), F32),
+            jax.ShapeDtypeStruct(coded_shape(2 * tiles + extra), jnp.int16),
             jax.ShapeDtypeStruct((2, per_dev, width), F32),
         ),
         in_specs=state_specs,
         out_specs=(vmem, vmem),
+        scratch_shapes=[tiles_scratch],
         compiler_params=params,
         name="pack",
     )(*state)
@@ -572,7 +679,7 @@
         far = send(pair, sizes, lambda i, j, k: (i, j ^ 2 if k == 0 else 3 - j, k))
         side, far = lax.optimization_barrier((side, far))
         side_o, far_o = swap(side), swap(far)
-        sets = (pair, side, side_o, far, far_o)
+        sets = (pair, far, far_o)
     else:
         side_o = swap(side)
         sets = (jnp.moveaxis(lax.all_gather(pair, "gy"), 0, 1).reshape(2, npanels, -1),)
@@ -580,12 +687,13 @@
     shared_specs = state_specs + [vmem] * (2 + len(sets))
     all_scratch = pltpu.VMEM((2, npanels, width), F32)
     planes = NSTEP * comps
+    face_scratch = pltpu.VMEM((2 * face_tiles(comps), HALO, size_z), F32)
     sent = pl.pallas_call(
         face_kernel,
-        out_shape=jax.ShapeDtypeStruct((2, planes + 2, rows, size_z), F32),
+        out_shape=jax.ShapeDtypeStruct(coded_shape(2 * face_tiles(comps)), jnp.int16),
         in_specs=shared_specs,
         out_specs=vmem,
-        scratch_shapes=[all_scratch],
+        scratch_shapes=[all_scratch, tiles_scratch, tiles_scratch, face_scratch],
         compiler_params=params,
         name="face",
     )(*shared)
@@ -602,6 +710,8 @@
         out_specs=(vmem,) * 4,
         scratch_shapes=[
             all_scratch,
+            tiles_scratch,
+            tiles_scratch,
             pltpu.VMEM((2, comps, size_x + 2, rows, size_z), F32),
             pltpu.VMEM((2, comps, size_x + 2, rows, size_z), F32),
             pltpu.VMEM((2, size_x, rows, size_z), F32),
@@ -620,6 +730,7 @@
         ),
         in_specs=[smem] + [vmem] * 6,
         out_specs=(vmem, vmem),
+        scratch_shapes=[face_scratch, face_scratch],
         compiler_params=params,
         name="join",
     )(scal, final, before, face, ratef, recv, recv_o)

time: 34.6 us -> 29.6 us (0.86)
  Pallas kernels: 15.3 us -> 13.4 us
  waiting for transfers between devices: 7.85 us -> 6.03 us
  starting transfers between devices: 9.95 us -> 9.23 us
  local copies, waits for them, and re-layouts: 0.65 us -> 0.01 us
    pallas_call x1, Pallas kernels: 9.34 us -> 6.05 us  [per_device(): pl.pallas_call(local_kernel, out_shape=(jax.ShapeDtypeStruct(u_now.shape,...]
    ppermute x10, waiting for transfers between devices: 7.85 us -> 6.03 us  [send(): return lax.ppermute(value, ('gx', 'gy', 'gz'), pairs)]
    pallas_call x2, Pallas kernels: 1.97 us -> 3.03 us  [the longest x1 1.9 us: per_device(): pl.pallas_call(face_kernel, out_shape=jax.ShapeDtypeStruct(coded_shape(2...]
    ppermute x10, starting transfers between devices: 9.95 us -> 9.23 us  [send(): return lax.ppermute(value, ('gx', 'gy', 'gz'), pairs)]
    unnamed x2 -> x0, local copies, waits for them, and re-layouts: 0.65 us -> none
    pallas_call x1, Pallas kernels: 2.37 us -> 2.76 us  [per_device(): pl.pallas_call(join_kernel, out_shape=(jax.ShapeDtypeStruct(u_now.shape,...]
  transfers between devices with their start and end apart: 10 -> 10, of which waited for: 5 -> 4; matrix products, arithmetic and copies ran while one was open for 0% -> 0% of each run, Pallas kernels for 32% -> 26%
where the time goes in v3:
time: 29.6 us; the launch traced here: 29.5 us
  Pallas kernels  13.4 us (45%)
  starting transfers between devices  9.23 us (31%)
  waiting for transfers between devices  6.03 us (20%)
  between operations  0.69 us (2%)
    ppermute x10, starting transfers between devices, send(): return lax.ppermute(value, ('gx', 'gy', 'gz'), pairs)  9.23 us
    pallas_call x1, Pallas kernels, per_device(): pl.pallas_call(local_kernel, out_shape=(jax.ShapeDtypeStruct(u_now.shape,...  6.05 us
    ppermute x10, waiting for transfers between devices, send(): return lax.ppermute(value, ('gx', 'gy', 'gz'), pairs)  6.03 us
    pallas_call x1, Pallas kernels, per_device(): pl.pallas_call(join_kernel, out_shape=(jax.ShapeDtypeStruct(u_now.shape,...  2.76 us
    pallas_call x1, Pallas kernels, per_device(): pl.pallas_call(face_kernel, out_shape=jax.ShapeDtypeStruct(coded_shape(2...  1.9 us
    pallas_call x1, Pallas kernels, per_device(): pl.pallas_call(prepare_kernel, out_shape=(jax.ShapeDtypeStruct((per_dev +...  1.6 us
    pallas_call x1, Pallas kernels, per_device(): pl.pallas_call(pack_kernel, out_shape=(jax.ShapeDtypeStruct(coded_shape(2...  1.13 us
  transfers between devices with their start and end apart: 10, of which 4 were waited for; matrix products, arithmetic and copies ran while one was open for 0% of the time, Pallas kernels for 26%

profile of v3, /device:TPU:0, one launch (start us, length us, event | category | flops | bytes accessed | tf_op | source)
XLA Modules:
  0.0 29.5 jit_solution(7891692579262211146)
XLA Ops:
  0.6 0.5 %collective-permute-start = (f32[3,16,16,128]{3,2,1,0:T(8,128)}, f32[3,16,16,128]{3,2,1,0:T(8,128)S(1)}, u32[]{:S(2)}, u32[]{:S(2)}) collective-permute-start(f32[3,16,16,128]{3,2,1,0:T(8,128)} %un_hbm.1), channel_id=1, source_target_pairs={{0,1},{1,0},{2,3},{3,2},{4,5},{5,4},{6,7},{7,6},{8,9},{9,8},{10,11... | collective-permute-start | bytes 1179656 | tf_op jit(solution)/shard_map/ppermute | solution.py:586
  1.2 0.1 collective-permute-start.1
  1.2 0.4 %collective-permute-start.2 = (f32[16,16,128]{2,1,0:T(8,128)}, f32[16,16,128]{2,1,0:T(8,128)S(1)}, u32[]{:S(2)}, u32[]{:S(2)}) collective-permute-start(f32[16,16,128]{2,1,0:T(8,128)} %lat_hbm.1), channel_id=1, source_target_pairs={{0,1},{1,0},{2,3},{3,2},{4,5},{5,4},{6,7},{7,6},{8,9},{9,8},{10,11... | collective-permute-start | bytes 393224 | tf_op jit(solution)/shard_map/ppermute | solution.py:586
  1.7 1.6 %prepare.1 = (f32[24,256]{1,0:T(8,128)S(1)}, f32[3,16,16,128]{3,2,1,0:T(8,128)S(1)}, f32[3,16,16,128]{3,2,1,0:T(8,128)S(1)}, f32[16,16,128]{2,1,0:T(8,128)S(1)}) custom-call(bf16[16,48,256]{2,1,0:T(8,128)(2,1)} %bitcast.7, f32[3,16,16]{2,1,0:T(8,128)} %coupling_hbm.1, bf16[256,256]{1,0:T(8,128)(2,1)} %constant.15.clone.table_hbm, s32[1,128]{1,0:T(1,128)} %bitcast.8, ...), custom_call_target="tpu_custom_call" | custom-call | tf_op jit(solution)/shard_map/prepare/pallas_call | solution.py:630
  3.3 0.1 collective-permute-start.3
  3.4 0.1 pad_add_fusion.scal_ref
  3.5 1.0 %collective-permute-done.3.intso_ref = f32[24,256]{1,0:T(8,128)S(1)} collective-permute-done((f32[24,256]{1,0:T(8,128)S(1)}, f32[24,256]{1,0:T(8,128)S(1)}, u32[]{:S(2)}, u32[]{:S(2)}) %collective-permute-start.3) | collective-permute-done | bytes 24608 | tf_op jit(solution)/shard_map/ppermute | solution.py:586
  4.5 0.0 collective-permute-done.2.lato_ref
  4.5 0.0 collective-permute-done.uno_ref
  4.5 0.0 collective-permute-done.1.upo_ref
  4.5 1.1 %pack.1 = (s16[53,16,128]{2,1,0:T(8,128)(2,1)S(1)}, f32[2,16,256]{2,1,0:T(8,128)S(1)}) custom-call(s32[5]{0:T(128)S(1)} %pad_add_fusion.scal_ref, f32[3,16,16,128]{3,2,1,0:T(8,128)S(1)} %get-tuple-element.19.un_ref, f32[3,16,16,128]{3,2,1,0:T(8,128)S(1)} %get-tuple-element.20.up_ref, f32[16,16,128]{2,1,0:T(8,128)S(1)} %get-tuple-element.21.lat_ref, ...), custom_call_target="tpu_custom_call" | custom-call | tf_op jit(solution)/shard_map/pack/pallas_call | solution.py:665
  5.7 2.8 %collective-permute-start.4 = (s16[53,16,128]{2,1,0:T(8,128)(2,1)S(1)}, s16[53,16,128]{2,1,0:T(8,128)(2,1)S(1)}, u32[]{:S(2)}, u32[]{:S(2)}) collective-permute-start(s16[53,16,128]{2,1,0:T(8,128)(2,1)S(1)} %get-tuple-element.23), channel_id=1, source_target_pairs={{0,2},{1,9},{2,0},{3,5},{4,6},{5,3},{6,4},{7,15},{8,10},{9,1},{10,... | collective-permute-start | bytes 651272 | tf_op jit(solution)/shard_map/ppermute | solution.py:586
  8.5 2.6 %collective-permute-start.5 = (f32[2,16,256]{2,1,0:T(8,128)S(1)}, f32[2,16,256]{2,1,0:T(8,128)S(1)}, u32[]{:S(2)}, u32[]{:S(2)}) collective-permute-start(f32[2,16,256]{2,1,0:T(8,128)S(1)} %get-tuple-element.24.rest_0_), channel_id=1, source_target_pairs={{0,4},{1,7},{2,6},{3,5},{4,0},{5,3},{6,2},{7,1},{8,12},{9,15},{10,... | collective-permute-start | bytes 98312 | tf_op jit(solution)/shard_map/ppermute | solution.py:586
  11.1 3.0 %collective-permute-done.5.rest_1_ = f32[2,16,256]{2,1,0:T(8,128)S(1)} collective-permute-done((f32[2,16,256]{2,1,0:T(8,128)S(1)}, f32[2,16,256]{2,1,0:T(8,128)S(1)}, u32[]{:S(2)}, u32[]{:S(2)}) %collective-permute-start.5) | collective-permute-done | bytes 32800 | tf_op jit(solution)/shard_map/ppermute | solution.py:586
  14.0 0.0 collective-permute-done.4.coded_ref
  14.0 0.0 collective-permute-start.6
  14.1 0.5 %collective-permute-start.7 = (f32[2,16,256]{2,1,0:T(8,128)S(1)}, f32[2,16,256]{2,1,0:T(8,128)S(1)}, u32[]{:S(2)}, u32[]{:S(2)}) collective-permute-start(f32[2,16,256]{2,1,0:T(8,128)S(1)} %collective-permute-done.5.rest_1_), channel_id=1, source_target_pairs={{0,1},{1,0},{2,3},{3,2},{4,5},{5,4},{6,7},{7,6},{8,9},{9,8},{10,11... | collective-permute-start | bytes 98312 | tf_op jit(solution)/shard_map/ppermute | solution.py:586
  14.6 1.0 %collective-permute-done.7.rest_2_ = f32[2,16,256]{2,1,0:T(8,128)S(1)} collective-permute-done((f32[2,16,256]{2,1,0:T(8,128)S(1)}, f32[2,16,256]{2,1,0:T(8,128)S(1)}, u32[]{:S(2)}, u32[]{:S(2)}) %collective-permute-start.7) | collective-permute-done | bytes 32800 | tf_op jit(solution)/shard_map/ppermute | solution.py:586
  15.6 0.0 collective-permute-done.6.codedo_ref
  15.6 1.9 %face.1 = s16[34,16,128]{2,1,0:T(8,128)(2,1)S(1)} custom-call(s32[5]{0:T(128)S(1)} %pad_add_fusion.scal_ref, f32[3,16,16,128]{3,2,1,0:T(8,128)S(1)} %get-tuple-element.19.un_ref, f32[3,16,16,128]{3,2,1,0:T(8,128)S(1)} %get-tuple-element.20.up_ref, f32[16,16,128]{2,1,0:T(8,128)S(1)} %get-tuple-element.21.lat_ref, ...), custom_call_target="tpu_custom_call" | custom-call | tf_op jit(solution)/shard_map/face/pallas_call | solution.py:691
  17.5 1.2 %collective-permute-start.8 = (s16[34,16,128]{2,1,0:T(8,128)(2,1)S(1)}, s16[34,16,128]{2,1,0:T(8,128)(2,1)S(1)}, u32[]{:S(2)}, u32[]{:S(2)}) collective-permute-start(s16[34,16,128]{2,1,0:T(8,128)(2,1)S(1)} %face.1), channel_id=1, source_target_pairs={{0,8},{1,25},{2,10},{3,27},{4,12},{5,29},{6,14},{7,31},{8,0},{9,17... | collective-permute-start | bytes 417800 | tf_op jit(solution)/shard_map/ppermute | solution.py:586
  18.7 6.0 %local.1 = (f32[3,16,16,128]{3,2,1,0:T(8,128)S(1)}, f32[3,16,16,128]{3,2,1,0:T(8,128)S(1)}, f32[2,2,12,24,128]{4,3,2,1,0:T(8,128)S(1)}, f32[2,2,4,24,128]{4,3,2,1,0:T(8,128)S(1)}) custom-call(s32[5]{0:T(128)S(1)} %pad_add_fusion.scal_ref, f32[3,16,16,128]{3,2,1,0:T(8,128)S(1)} %get-tuple-element.19.un_ref, f32[3,16,16,128]{3,2,1,0:T(8,128)S(1)} %get-tuple-element.20.up_ref, ...), custom_call_target="tpu_custom_call" | custom-call | tf_op jit(solution)/shard_map/local/pallas_call | solution.py:701
  24.8 0.0 collective-permute-done.8.coded_ref
  24.8 0.9 %collective-permute-start.9 = (s16[34,16,128]{2,1,0:T(8,128)(2,1)S(1)}, s16[34,16,128]{2,1,0:T(8,128)(2,1)S(1)}, u32[]{:S(2)}, u32[]{:S(2)}) collective-permute-start(s16[34,16,128]{2,1,0:T(8,128)(2,1)S(1)} %collective-permute-done.8.coded_ref), channel_id=1, source_target_pairs={{0,1},{1,0},{2,3},{3,2},{4,5},{5,4},{6,7},{7,6},{8,9},{9,8},{10,11... | collective-permute-start | bytes 417800 | tf_op jit(solution)/shard_map/ppermute | solution.py:586
  25.7 1.0 %collective-permute-done.9.codedo_ref = s16[34,16,128]{2,1,0:T(8,128)(2,1)S(1)} collective-permute-done((s16[34,16,128]{2,1,0:T(8,128)(2,1)S(1)}, s16[34,16,128]{2,1,0:T(8,128)(2,1)S(1)}, u32[]{:S(2)}, u32[]{:S(2)}) %collective-permute-start.9) | collective-permute-done | bytes 139296 | tf_op jit(solution)/shard_map/ppermute | solution.py:586
  26.7 2.8 %join.1 = (f32[3,16,16,128]{3,2,1,0:T(8,128)}, f32[3,16,16,128]{3,2,1,0:T(8,128)}) custom-call(s32[5]{0:T(128)S(1)} %pad_add_fusion.scal_ref, f32[3,16,16,128]{3,2,1,0:T(8,128)S(1)} %get-tuple-element.31.final_in, f32[3,16,16,128]{3,2,1,0:T(8,128)S(1)} %get-tuple-element.32.before_in, f32[2,2,12,24,128]{4,3,2,1,0:T(8,128)S(1)} %get-tuple-element.33.face_ref, ...), custom_call_target="tpu_custom_call" | custom-call | tf_op jit(solution)/shard_map/join/pallas_call | solution.py:725
  (1 shorter events, 0.0 us)
Async XLA Ops:
  0.6 3.9 %collective-permute-start = (f32[3,16,16,128]{3,2,1,0:T(8,128)}, f32[3,16,16,128]{3,2,1,0:T(8,128)S(1)}, u32[]{:S(2)}, u32[]{:S(2)}) collective-permute-start(f32[3,16,16,128]{3,2,1,0:T(8,128)} %un_hbm.1), channel_id=1, source_target_pairs={{0,1},{1,0},{2,3},{3,2},{4,5},{5,4},{6,7},{7,6},{8,9},{9,8},{10,11... | collective-permute-start | bytes 1179656 | tf_op jit(solution)/shard_map/ppermute | solution.py:586
  1.2 3.4 %collective-permute-start.1 = (f32[3,16,16,128]{3,2,1,0:T(8,128)}, f32[3,16,16,128]{3,2,1,0:T(8,128)S(1)}, u32[]{:S(2)}, u32[]{:S(2)}) collective-permute-start(f32[3,16,16,128]{3,2,1,0:T(8,128)} %up_hbm.1), channel_id=1, source_target_pairs={{0,1},{1,0},{2,3},{3,2},{4,5},{5,4},{6,7},{7,6},{8,9},{9,8},{10,11... | collective-permute-start | bytes 1179656 | tf_op jit(solution)/shard_map/ppermute | solution.py:586
  1.2 3.3 %collective-permute-start.2 = (f32[16,16,128]{2,1,0:T(8,128)}, f32[16,16,128]{2,1,0:T(8,128)S(1)}, u32[]{:S(2)}, u32[]{:S(2)}) collective-permute-start(f32[16,16,128]{2,1,0:T(8,128)} %lat_hbm.1), channel_id=1, source_target_pairs={{0,1},{1,0},{2,3},{3,2},{4,5},{5,4},{6,7},{7,6},{8,9},{9,8},{10,11... | collective-permute-start | bytes 393224 | tf_op jit(solution)/shard_map/ppermute | solution.py:586
  3.3 1.3 %collective-permute-start.3 = (f32[24,256]{1,0:T(8,128)S(1)}, f32[24,256]{1,0:T(8,128)S(1)}, u32[]{:S(2)}, u32[]{:S(2)}) collective-permute-start(f32[24,256]{1,0:T(8,128)S(1)} %get-tuple-element.22.ints_ref), channel_id=1, source_target_pairs={{0,1},{1,0},{2,3},{3,2},{4,5},{5,4},{6,7},{7,6},{8,9},{9,8},{10,11... | collective-permute-start | bytes 73736 | tf_op jit(solution)/shard_map/ppermute | solution.py:586
  5.7 8.4 %collective-permute-start.4 = (s16[53,16,128]{2,1,0:T(8,128)(2,1)S(1)}, s16[53,16,128]{2,1,0:T(8,128)(2,1)S(1)}, u32[]{:S(2)}, u32[]{:S(2)}) collective-permute-start(s16[53,16,128]{2,1,0:T(8,128)(2,1)S(1)} %get-tuple-element.23), channel_id=1, source_target_pairs={{0,2},{1,9},{2,0},{3,5},{4,6},{5,3},{6,4},{7,15},{8,10},{9,1},{10,... | collective-permute-start | bytes 651272 | tf_op jit(solution)/shard_map/ppermute | solution.py:586
  8.5 5.6 %collective-permute-start.5 = (f32[2,16,256]{2,1,0:T(8,128)S(1)}, f32[2,16,256]{2,1,0:T(8,128)S(1)}, u32[]{:S(2)}, u32[]{:S(2)}) collective-permute-start(f32[2,16,256]{2,1,0:T(8,128)S(1)} %get-tuple-element.24.rest_0_), channel_id=1, source_target_pairs={{0,4},{1,7},{2,6},{3,5},{4,0},{5,3},{6,2},{7,1},{8,12},{9,15},{10,... | collective-permute-start | bytes 98312 | tf_op jit(solution)/shard_map/ppermute | solution.py:586
  14.0 1.5 %collective-permute-start.6 = (s16[53,16,128]{2,1,0:T(8,128)(2,1)S(1)}, s16[53,16,128]{2,1,0:T(8,128)(2,1)S(1)}, u32[]{:S(2)}, u32[]{:S(2)}) collective-permute-start(s16[53,16,128]{2,1,0:T(8,128)(2,1)S(1)} %collective-permute-done.4.coded_ref), channel_id=1, source_target_pairs={{0,1},{1,0},{2,3},{3,2},{4,5},{5,4},{6,7},{7,6},{8,9},{9,8},{10,11... | collective-permute-start | bytes 651272 | tf_op jit(solution)/shard_map/ppermute | solution.py:586
  14.1 1.5 %collective-permute-start.7 = (f32[2,16,256]{2,1,0:T(8,128)S(1)}, f32[2,16,256]{2,1,0:T(8,128)S(1)}, u32[]{:S(2)}, u32[]{:S(2)}) collective-permute-start(f32[2,16,256]{2,1,0:T(8,128)S(1)} %collective-permute-done.5.rest_1_), channel_id=1, source_target_pairs={{0,1},{1,0},{2,3},{3,2},{4,5},{5,4},{6,7},{7,6},{8,9},{9,8},{10,11... | collective-permute-start | bytes 98312 | tf_op jit(solution)/shard_map/ppermute | solution.py:586
  17.5 7.3 %collective-permute-start.8 = (s16[34,16,128]{2,1,0:T(8,128)(2,1)S(1)}, s16[34,16,128]{2,1,0:T(8,128)(2,1)S(1)}, u32[]{:S(2)}, u32[]{:S(2)}) collective-permute-start(s16[34,16,128]{2,1,0:T(8,128)(2,1)S(1)} %face.1), channel_id=1, source_target_pairs={{0,8},{1,25},{2,10},{3,27},{4,12},{5,29},{6,14},{7,31},{8,0},{9,17... | collective-permute-start | bytes 417800 | tf_op jit(solution)/shard_map/ppermute | solution.py:586
  24.8 1.9 %collective-permute-start.9 = (s16[34,16,128]{2,1,0:T(8,128)(2,1)S(1)}, s16[34,16,128]{2,1,0:T(8,128)(2,1)S(1)}, u32[]{:S(2)}, u32[]{:S(2)}) collective-permute-start(s16[34,16,128]{2,1,0:T(8,128)(2,1)S(1)} %collective-permute-done.8.coded_ref), channel_id=1, source_target_pairs={{0,1},{1,0},{2,3},{3,2},{4,5},{5,4},{6,7},{7,6},{8,9},{9,8},{10,11... | collective-permute-start | bytes 417800 | tf_op jit(solution)/shard_map/ppermute | solution.py:586

commit v4 on v3

--- a/solution.py
+++ b/solution.py
@@ -13,7 +13,7 @@
 HALO = 8
 LANES = 128
 PANELS = 16
-TOP = 32767.0
+TOP = 32000.0
 F32 = jnp.float32
 BF16 = jnp.bfloat16
 
@@ -65,22 +65,20 @@
     return jnp.exp2(exponents) * (1.0 / TOP)
 
 
-def quantize(tiles_ref, out_ref):
-    number = tiles_ref.shape[0]
-    lane = iota(tiles_ref.shape[1:], 1)
-    peak = jnp.zeros(tiles_ref.shape[1:], F32)
-    for t in range(number):
-        peak = jnp.where(lane == t, jnp.max(jnp.abs(tiles_ref[t]), axis=1, keepdims=True), peak)
+def quantize(load, groups, out_ref):
+    shape = (HALO, LANES)
+    lane = iota(shape, 1)
+    peak = jnp.zeros(shape, F32)
+    for group in range(max(groups) + 1):
+        members = [jnp.abs(load(t)) for t, of in enumerate(groups) if of == group]
+        top = functools.reduce(jnp.maximum, members)
+        peak = jnp.where(lane == group, jnp.max(top, axis=1, keepdims=True), peak)
     exponents = jnp.ceil(jnp.log2(jnp.maximum(peak, 1e-30)))
     factor = jnp.exp2(-exponents) * TOP
-
-    def coded(t):
-        scaled = jnp.round(tiles_ref[t] * factor[:, t:t + 1])
-        return jnp.clip(scaled, -TOP, TOP).astype(jnp.int32)
-
-    zero = jnp.zeros(tiles_ref.shape[1:], jnp.int32)
-    parts = [coded(t) for t in range(number)] + [zero] * (number % 2)
-    parts += [exponents.astype(jnp.int32), zero]
+    zero = jnp.zeros(shape, jnp.int32)
+    wide = [jnp.broadcast_to(factor[:, g:g + 1], shape) for g in range(max(groups) + 1)]
+    parts = [jnp.round(load(t) * wide[of]).astype(jnp.int32) for t, of in enumerate(groups)]
+    parts += [zero] * (len(groups) % 2) + [exponents.astype(jnp.int32), zero]
     for i in range(out_ref.shape[0]):
         out_ref[i] = jnp.concatenate(parts[2 * i:2 * i + 2], axis=0).astype(jnp.int16)
 
@@ -89,29 +87,50 @@
     return ((number + 1) // 2 + 1, 2 * HALO, LANES)
 
 
-def scales_of(ref):
-    return row_scales(ref[ref.shape[0] - 1].astype(jnp.int32)[0:HALO].astype(F32))
-
-
-def expand(ref, tiles_ref, blocks):
-    for at, scale in blocks:
-        pair = ref[at].astype(jnp.int32).astype(F32)
-        tiles_ref[2 * at] = pair[0:HALO] * scale[0]
-        tiles_ref[2 * at + 1] = pair[HALO:] * scale[1]
-
-
-def expand_all(ref, tiles_ref):
-    scale = scales_of(ref)
-    expand(ref, tiles_ref, [
-        (i, (scale[:, 2 * i:2 * i + 1], scale[:, 2 * i + 1:2 * i + 2])) for i in range(tiles_ref.shape[0] // 2)
+def side_groups(comps, size_x, rest):
+    near = [c * (size_x // NSTEP) + x // NSTEP for c in range(comps) for x in range(size_x)]
+    return near + [max(near) + 1 + i for i in range(rest)]
+
+
+def scales_of(coded):
+    return row_scales(coded.astype(jnp.int32)[0:HALO].astype(F32))
+
+
+def expand(load, store, scales, blocks):
+    for at, one, two in blocks:
+        pair = load(at).astype(jnp.int32).astype(F32)
+        store(2 * at, pair[0:HALO] * scales[:, one:one + 1])
+        store(2 * at + 1, pair[HALO:] * scales[:, two:two + 1])
+
+
+def expand_all(ref, tiles_ref, groups):
+    def store(t, value):
+        tiles_ref[t] = value
+
+    expand(lambda i: ref[i], store, scales_of(ref[ref.shape[0] - 1]), [
+        (t // 2, groups[t], groups[t + 1]) for t in range(0, len(groups), 2)
     ])
 
 
+def expand_sides(ref, tiles_ref, first, choose):
+    for half in range(2):
+        z = first if half == 0 else 1 - first
+
+        def store(t, value):
+            tiles_ref[z, t] = value
+
+        scales = scales_of(ref[half, ref.shape[1] - 1])
+        for moved, blocks in choose(scales):
+            expand(lambda i: ref[half, i], store, moved, blocks)
+
+
 def prepare_kernel(
-    panels_hbm, coupling_hbm, table_hbm, depth_hbm, owner_hbm, block_hbm, speed_hbm, un_hbm, up_hbm, lat_hbm,
-    out_ref, un_ref, up_ref, lat_ref,
+    scal_ref, panels_hbm, coupling_hbm, table_hbm, depth_hbm, owner_hbm, block_hbm, speed_hbm,
+    un_hbm, up_hbm, lat_hbm, out_ref, state_ref, mine_ref, theirs_ref, tiles_ref,
     panels_ref, coupling_ref, table_ref, depth_ref, owner_ref, block_ref, speed_ref, sems,
 ):
+    comps = un_hbm.shape[0]
+    un_ref, up_ref, lat_ref = state_ref.at[0:comps], state_ref.at[comps:2 * comps], state_ref.at[2 * comps]
     pairs = (
         (panels_hbm, panels_ref), (table_hbm, table_ref), (coupling_hbm, coupling_ref),
         (depth_hbm, depth_ref), (owner_hbm, owner_ref), (block_hbm, block_ref), (speed_hbm, speed_ref),
@@ -123,7 +142,7 @@
     for copy in copies[:7]:
         copy.wait()
     count, rows, spectral = panels_ref.shape
-    comps, block = 3, rows // 3
+    block = rows // comps
     lanes = table_ref.shape[1]
     free = jnp.dot(
         panels_ref[...].reshape(count * rows, spectral), table_ref[...], preferred_element_type=F32
@@ -154,6 +173,27 @@
         out_ref[row:row + 1, at:at + LANES] = piece.astype(F32)
     for copy in copies[7:]:
         copy.wait()
+    comps, size_x, size_y, size_z = un_ref.shape
+    sub = iota((size_x, HALO, size_z), 1)
+    for side in range(2):
+        base = 0 if side else size_y - HALO
+        rate = lat_ref[:, base:base + HALO, :] * speed[None]
+        for c in range(comps):
+            now = un_ref[c, :, base:base + HALO, :]
+            old = spin(up_ref[c, :, base:base + HALO, :], HALO // 2, 1)
+            keep = sub < HALO // 2 if side else sub >= HALO // 2
+            row = c if side else HALO - 1 - c
+            tile = jnp.where(keep, now, old)
+            tile = jnp.where(sub == (HALO - 1 if side else 0), rate[:, row:row + 1, :], tile)
+            tiles_ref[side, c * size_x:(c + 1) * size_x] = tile
+        for part in range(lanes // size_z):
+            for piece in range(count // HALO):
+                at = comps * size_x + part * (count // HALO) + piece
+                tiles_ref[side, at] = out_ref[piece * HALO:(piece + 1) * HALO, part * size_z:(part + 1) * size_z]
+    low = lax.rem(scal_ref[1] + scal_ref[2], 2)
+    groups = side_groups(comps, size_x, tiles_ref.shape[1] - comps * size_x)
+    quantize(lambda t: tiles_ref[low, t], groups, mine_ref)
+    quantize(lambda t: tiles_ref[1 - low, t], groups, theirs_ref)
 
 
 def listed(ref, panels, which):
@@ -167,49 +207,11 @@
     return jnp.concatenate(out, axis=1)
 
 
-def pack_kernel(
-    scal_ref, un_ref, up_ref, lat_ref, uno_ref, upo_ref, lato_ref, ints_ref, intso_ref,
-    coded_ref, pair_ref, out_ref,
-):
-    mine = scal_ref[2]
-    high = lax.rem(scal_ref[1] + mine, 2) == 0
-    comps, size_x, size_y, size_z = un_ref.shape
-    tiles = comps * size_x
-    shape = (size_x, HALO, size_z)
-    sub = iota(shape, 1)
-
-    def fill(side):
-        base = size_y - HALO if side else 0
-        for z_at, un, up, lat, ints in (
-            (mine, un_ref, up_ref, lat_ref, ints_ref),
-            (1 - mine, uno_ref, upo_ref, lato_ref, intso_ref),
-        ):
-            rate = lat[:, base:base + HALO, :] * listed(ints, LANES, 0)[None]
-            for c in range(comps):
-                now = un[c, :, base:base + HALO, :]
-                old = spin(up[c, :, base:base + HALO, :], HALO // 2, 1)
-                keep = sub >= HALO // 2 if side else sub < HALO // 2
-                row = HALO - 1 - c if side else c
-                tile = jnp.where(keep, now, old)
-                tile = jnp.where(sub == (0 if side else HALO - 1), rate[:, row:row + 1, :], tile)
-                out_ref[pl.ds(z_at * tiles + c * size_x, size_x)] = tile
-
-    @pl.when(high)
-    def _():
-        fill(True)
-
-    @pl.when(jnp.logical_not(high))
-    def _():
-        fill(False)
-
-    count, lanes = PANELS, ints_ref.shape[1]
-    for z_at, force in ((mine, ints_ref), (1 - mine, intso_ref)):
-        pair_ref[z_at] = force[0:count]
-        for part in range(lanes // size_z):
-            for piece in range(count // HALO):
-                at = 2 * tiles + (z_at * (lanes // size_z) + part) * (count // HALO) + piece
-                out_ref[at] = force[piece * HALO:(piece + 1) * HALO, part * size_z:(part + 1) * size_z]
-    quantize(out_ref, coded_ref)
+def gather_kernel(mine_ref, theirs_ref, ints_ref, intso_ref, both_ref, pair_ref):
+    both_ref[0] = mine_ref[...]
+    both_ref[1] = theirs_ref[...]
+    pair_ref[0] = ints_ref[0:PANELS]
+    pair_ref[1] = intso_ref[0:PANELS]
 
 
 def place_forces(scal_ref, sets, all_ref):
@@ -220,7 +222,8 @@
     count, lanes = own_ref.shape[1:]
     beside, opposite, mirror = o + 1 - 2 * lax.rem(o, 2), lax.rem(o + 2, 4), 3 - o
     size_z = side_ref.shape[-1]
-    tiles = side_ref.shape[0] - 2 * (lanes // size_z) * (count // HALO)
+    step = count // HALO
+    tiles = side_ref.shape[1] - lanes // size_z * step
     here = mine == 0
 
     def spot(j):
@@ -229,17 +232,15 @@
     for ref, j in ((side_ref, jnp.where(here, beside, mirror)), (sideo_ref, jnp.where(here, mirror, beside))):
         for z in range(2):
             for part in range(lanes // size_z):
-                at = tiles + (z * (lanes // size_z) + part) * (count // HALO)
-                all_ref[z, spot(j), part * size_z:(part + 1) * size_z] = ref[
-                    at:at + count // HALO
-                ].reshape(count, size_z)
-    for ref, j in (
-        (far_ref, jnp.where(here, opposite, mirror)),
-        (faro_ref, jnp.where(here, mirror, opposite)),
-        (own_ref, o),
+                at = tiles + part * step
+                all_ref[z, spot(j), part * size_z:(part + 1) * size_z] = ref[z, at:at + step].reshape(count, size_z)
+    for ref, j, first in (
+        (far_ref, jnp.where(here, opposite, mirror), mine),
+        (faro_ref, jnp.where(here, mirror, opposite), 1 - mine),
+        (own_ref, o, mine),
     ):
-        for z in range(2):
-            all_ref[z, spot(j), :] = ref[z]
+        all_ref[first, spot(j), :] = ref[0]
+        all_ref[1 - first, spot(j), :] = ref[1]
     return all_ref
 
 
@@ -277,6 +278,11 @@
     return jnp.concatenate(out, axis=1)
 
 
+def fields(state_ref):
+    comps = state_ref.shape[0] // 2
+    return state_ref.at[0:comps], state_ref.at[comps:2 * comps], state_ref.at[2 * comps]
+
+
 def halo_tiles(high, low):
     sub = iota(high.shape, high.ndim - 2)
     upper = sub < HALO // 2
@@ -305,27 +311,28 @@
 
 
 def face_kernel(
-    scal_ref, un_ref, up_ref, lat_ref, uno_ref, upo_ref, lato_ref, ints_ref, intso_ref,
+    scal_ref, state_ref, stateo_ref, ints_ref, intso_ref,
     coded_ref, codedo_ref, *rest,
 ):
     *sets, out_ref, all_ref, side_ref, sideo_ref, faces_ref = rest
+    (un_ref, up_ref, lat_ref), (uno_ref, upo_ref, lato_ref) = fields(state_ref), fields(stateo_ref)
     comps, size_x, size_y, size_z = un_ref.shape
     rows = size_y + HALO
     tiles = comps * size_x
     a, o, mine = scal_ref[0], scal_ref[1], scal_ref[2]
     high = lax.rem(a + mine, 2) == 0
     skip = jnp.where(high, size_x - NSTEP, 0)
-    for ref, tiles_ref in ((coded_ref, side_ref), (codedo_ref, sideo_ref)):
-        scale = scales_of(ref)
-        moved = pltpu.roll(scale, lax.rem(LANES - skip, LANES), 1)
-        blocks = []
-        for first in range(0, 2 * tiles, size_x):
-            for i in range(first, first + NSTEP, 2):
-                at = i // 2 + lax.div(skip, 2)
-                blocks.append((at, (moved[:, i:i + 1], moved[:, i + 1:i + 2])))
-        for i in range(2 * tiles, tiles_ref.shape[0], 2):
-            blocks.append((i // 2, (scale[:, i:i + 1], scale[:, i + 1:i + 2])))
-        expand(ref, tiles_ref, blocks)
+
+    groups = side_groups(comps, size_x, side_ref.shape[1] - tiles)
+
+    def choose(scales):
+        moved = pltpu.roll(scales, lax.rem(LANES - lax.div(skip, NSTEP), LANES), 1)
+        near = [first + i for first in range(0, tiles, size_x) for i in range(0, NSTEP, 2)]
+        rest = [(t // 2, groups[t], groups[t + 1]) for t in range(tiles, len(groups), 2)]
+        return (moved, [(t // 2 + lax.div(skip, 2), groups[t], groups[t + 1]) for t in near]), (scales, rest)
+
+    expand_sides(coded_ref, side_ref, mine, choose)
+    expand_sides(codedo_ref, sideo_ref, 1 - mine, choose)
     forces = place_forces(scal_ref, with_sides(sets, side_ref, sideo_ref), all_ref)
     panels = forces.shape[1]
     own = mine == 0
@@ -355,7 +362,7 @@
             x = jnp.where(high, size_x - d, d - 1)
             ups, lows = [], []
             for c in range(comps):
-                upper, lower = sides(scal_ref, side_ref, sideo_ref, z * tiles + c * size_x + x)
+                upper, lower = sides(scal_ref, side_ref, sideo_ref, (z, c * size_x + x))
                 ups.append(upper)
                 lows.append(lower)
                 tile_now, tile_old = halo_tiles(upper, lower)
@@ -399,11 +406,21 @@
                 faces_ref[base + 2 * i + half] = plane[half * HALO:(half + 1) * HALO]
         for i, tail in enumerate(tails):
             faces_ref[base + 2 * len(planes) + i] = tail
-    quantize(faces_ref, out_ref)
+    quantize(lambda t: faces_ref[t], face_groups(comps), out_ref)
 
 
 def face_tiles(comps):
     return 2 * (NSTEP * comps + 2) + comps + 2
+
+
+def face_groups(comps):
+    groups = []
+    for z in range(2):
+        base = z * (2 * NSTEP + 5)
+        groups += [base + 2 * n + half for n in range(NSTEP) for _ in range(comps) for half in range(2)]
+        groups += [base + 2 * NSTEP + half for _ in range(2) for half in range(2)]
+        groups += [base + 2 * NSTEP + 2] * comps + [base + 2 * NSTEP + 3, base + 2 * NSTEP + 4]
+    return groups
 
 
 def face_plane(tiles_ref, z, i, comps):
@@ -442,17 +459,22 @@
 
 
 def local_kernel(
-    scal_ref, un_ref, up_ref, lat_ref, uno_ref, upo_ref, lato_ref, ints_ref, intso_ref,
+    scal_ref, state_ref, stateo_ref, ints_ref, intso_ref,
     coded_ref, codedo_ref, *rest,
 ):
     *sets, final_ref, before_ref, face_ref, ratef_ref, all_ref, side_ref, sideo_ref = rest[:-4]
     now_ref, old_ref, rate_ref, drive_ref = rest[-4:]
+    (un_ref, up_ref, lat_ref), (uno_ref, upo_ref, lato_ref) = fields(state_ref), fields(stateo_ref)
     comps, size_x, size_y, size_z = un_ref.shape
     rows = size_y + HALO
     tiles = comps * size_x
     o, mine = scal_ref[1], scal_ref[2]
-    expand_all(coded_ref, side_ref)
-    expand_all(codedo_ref, sideo_ref)
+    groups = side_groups(comps, size_x, side_ref.shape[1] - comps * size_x)
+    choose = lambda scales: (
+        (scales, [(t // 2, groups[t], groups[t + 1]) for t in range(0, len(groups), 2)]),
+    )
+    expand_sides(coded_ref, side_ref, mine, choose)
+    expand_sides(codedo_ref, sideo_ref, 1 - mine, choose)
     forces = place_forces(scal_ref, with_sides(sets, side_ref, sideo_ref), all_ref)
     panels = forces.shape[1]
     own = mine == 0
@@ -479,7 +501,7 @@
         speed = listed(ints, LANES, 0)
         ups, lows = [], []
         for c in range(comps):
-            upper, lower = sides(scal_ref, side_ref, sideo_ref, pl.ds(z_at * tiles + c * size_x, size_x))
+            upper, lower = sides(scal_ref, side_ref, sideo_ref, (z_at, slice(c * size_x, (c + 1) * size_x)))
             ups.append(upper)
             lows.append(lower)
             tile_now, tile_old = halo_tiles(upper, lower)
@@ -501,44 +523,42 @@
                 for c in range(comps):
                     face_ref[side, z, n * comps + c] = now[z, c, 1 if side else size_x]
 
-        def step(x, carry):
+        def step(x, carry, now=now, old=old, n=n, halves=(0, 1)):
             for c in range(comps):
                 centre = now[0, c, x + 1], now[1, c, x + 1]
                 sums = inplane(*centre)
-                for z in range(2):
+                for z in halves:
                     lap = sums[z] + (now[z, c, x] + now[z, c, x + 2])
-                    old[z, c, x + 1] = (
+                    value = (
                         2.0 * centre[z] - old[z, c, x + 1] + rate_ref[z, x] * lap + drive_ref[n, z, c, x]
                     )
+                    if len(halves) == 2:
+                        old[z, c, x + 1] = value
+                    else:
+                        final_ref[c, x] = value[0:size_y]
+                        before_ref[c, x] = centre[z][0:size_y]
             return carry
 
-        lax.fori_loop(0, size_x, step, 0, unroll=4)
-    now, old = refs[NSTEP % 2], refs[(NSTEP + 1) % 2]
-    for c in range(comps):
-        final_ref[c] = now[mine, c, 1:size_x + 1, 0:size_y]
-        before_ref[c] = old[mine, c, 1:size_x + 1, 0:size_y]
-
-
-def join_kernel(
-    scal_ref, final_in, before_in, face_ref, ratef_ref, coded_ref, codedo_ref, final_ref, before_ref,
-    recv_ref, recvo_ref,
-):
+        if n < NSTEP - 1:
+            lax.fori_loop(0, size_x, step, 0, unroll=size_x)
+        else:
+            for z in range(2):
+                @pl.when(mine == z)
+                def _(step=step, z=z):
+                    lax.fori_loop(0, size_x, functools.partial(step, halves=(z,)), 0, unroll=size_x)
+
+
+def corrected(scal_ref, final_in, before_in, face_ref, ratef_ref, coded_ref, recv_ref, high, edges):
     comps, size_x, size_y, size_z = final_in.shape
     a, mine = scal_ref[0], scal_ref[2]
-    own = mine == 0
-    high = lax.rem(a + mine, 2) == 0
-    expand_all(coded_ref, recv_ref)
-    expand_all(codedo_ref, recvo_ref)
-    final_ref[...] = final_in[...]
-    before_ref[...] = before_in[...]
-    for side in range(2):
-        is_high = side == 0
-        here = high if is_high else jnp.logical_not(high)
-        inside = a < scal_ref[3] - 1 if is_high else a > 0
-
-        def theirs(z, at):
-            return jnp.where(inside, jnp.where(here, face_plane(recv_ref, z, at, comps), face_plane(recvo_ref, z, at, comps)), 0.0)
-
+    side = jnp.where(high, 0, 1)
+    inside = jnp.where(high, a < scal_ref[3] - 1, a > 0)
+    expand_all(coded_ref, recv_ref, face_groups(comps))
+
+    def theirs(z, at):
+        return jnp.where(inside, face_plane(recv_ref, z, at, comps), 0.0)
+
+    def correct(own):
         rate = {}
         for z in range(2):
             for m in range(NSTEP):
@@ -549,32 +569,65 @@
             last, now = {}, {}
             for n in range(NSTEP):
                 later = {}
-                top = min(n + 1, NSTEP - 1 - n)
-                for m in range(-n, top + 1):
+                for m in range(-n, min(n + 1, NSTEP - 1 - n) + 1):
                     centre = [now.get((z, m)) for z in range(2)]
                     sums = inplane(*centre) if centre[0] is not None else (None, None)
-                    for z in range(2):
+                    for z in range(2) if n < NSTEP - 1 else (own,):
                         terms = [sums[z], now.get((z, m - 1)), now.get((z, m + 1))]
                         if m == 0:
                             terms.append(theirs(z, n * comps + c))
                         if m == 1:
                             terms.append(face_ref[side, z, n * comps + c])
-                        terms = [t for t in terms if t is not None]
-                        lap = functools.reduce(lambda p, q: p + q, terms)
-                        value = rate[z, m] * lap
+                        value = functools.reduce(lambda p, q: p + q, [t for t in terms if t is not None])
+                        value = rate[z, m] * value
                         if centre[z] is not None:
                             value = value + 2.0 * centre[z]
                         if (z, m) in last:
                             value = value - last[z, m]
                         later[z, m] = value
                 last, now = now, later
-            for target, values in ((final_ref, now), (before_ref, last)):
-                for m in range(0, -NSTEP, -1):
-                    if (0, m) not in values:
-                        continue
-                    x = size_x - 1 + m if is_high else -m
-                    add = jnp.where(own, values[0, m], values[1, m])[0:size_y]
-                    target[c, x] = target[c, x] + add
+            for values, source, edge in zip((now, last), (final_in, before_in), edges):
+                depth = edge.shape[1]
+                for m in range(1 - depth, 1):
+                    x, at = jnp.where(high, size_x - 1 + m, -m), jnp.where(high, depth - 1 + m, -m)
+                    edge[c, at] = source[c, x] + values[own, m][0:size_y]
+
+    for z in range(2):
+        pl.when(mine == z)(functools.partial(correct, z))
+
+
+def near_kernel(
+    scal_ref, final_in, before_in, face_ref, ratef_ref, coded_ref, final_edge, before_edge, recv_ref
+):
+    high = lax.rem(scal_ref[0] + scal_ref[2], 2) == 0
+    edges = final_edge, before_edge
+    corrected(scal_ref, final_in, before_in, face_ref, ratef_ref, coded_ref, recv_ref, high, edges)
+
+
+def far_kernel(
+    scal_ref, final_in, before_in, face_ref, ratef_ref, coded_ref, final_near, before_near,
+    final_ref, before_ref, recv_ref, final_edge, before_edge, sems,
+):
+    size_x = final_in.shape[1]
+    high = lax.rem(scal_ref[0] + scal_ref[2], 2) == 1
+    copies = []
+
+    def begin(src, target, first, count):
+        copies.append(pltpu.make_async_copy(src, target.at[:, pl.ds(first, count)], sems.at[len(copies)]))
+        copies[-1].start()
+
+    outputs = ((final_in, final_near, final_ref, final_edge), (before_in, before_near, before_ref, before_edge))
+    for source, near, target, edge in outputs:
+        depth = edge.shape[1]
+        begin(near, target, jnp.where(high, 0, size_x - depth), depth)
+        begin(source.at[:, pl.ds(depth, size_x - 2 * depth)], target, depth, size_x - 2 * depth)
+    edges = final_edge, before_edge
+    corrected(scal_ref, final_in, before_in, face_ref, ratef_ref, coded_ref, recv_ref, high, edges)
+    for source, near, target, edge in outputs:
+        depth = edge.shape[1]
+        begin(edge, target, jnp.where(high, size_x - depth, 0), depth)
+    for copy in copies:
+        copy.wait()
 
 
 def send(value, mesh_sizes, route):
@@ -618,26 +671,27 @@
         return i, to, k
 
     assert per_dev == PANELS and size_z == LANES
-    un_o, up_o, lat_o = swap(u_now), swap(u_prev), swap(lateral)
-
     vmem = pl.BlockSpec(memory_space=pltpu.VMEM)
     smem = pl.BlockSpec(memory_space=pltpu.SMEM)
     params = pltpu.CompilerParams(vmem_limit_bytes=48 * 1024 * 1024)
     table = jnp.asarray(wave_table(spectral, panels.shape[3]))
     width = table.shape[1]
-    number = LANES + 4 * npanels
-    extra_rows = -(-(-(-number // width)) // 8) * 8
-    ints, un_v, up_v, lat_v = pl.pallas_call(
+    extra_rows = -(-(LANES + 4 * npanels) // (8 * width)) * 8
+    tiles = comps * size_x
+    number = tiles + width // size_z * (per_dev // HALO)
+    half = jax.ShapeDtypeStruct(coded_shape(number), jnp.int16)
+    ints, fields_own, mine, theirs = pl.pallas_call(
         prepare_kernel,
         out_shape=(
             jax.ShapeDtypeStruct((per_dev + extra_rows, width), F32),
-            jax.ShapeDtypeStruct(u_now.shape, F32),
-            jax.ShapeDtypeStruct(u_prev.shape, F32),
-            jax.ShapeDtypeStruct(lateral.shape, F32),
+            jax.ShapeDtypeStruct((2 * comps + 1,) + u_now.shape[1:], F32),
+            half,
+            half,
         ),
-        in_specs=[pl.BlockSpec(memory_space=pl.ANY)] * 10,
+        in_specs=[smem] + [pl.BlockSpec(memory_space=pl.ANY)] * 10,
         out_specs=(vmem,) * 4,
         scratch_shapes=[
+            pltpu.VMEM((2, number, HALO, size_z), F32),
             pltpu.VMEM((per_dev,) + panels.shape[3:], BF16),
             pltpu.VMEM(coupling.shape, F32),
             pltpu.VMEM(table.shape, BF16),
@@ -649,32 +703,30 @@
         ],
         compiler_params=params,
         name="prepare",
-    )(*(
+    )(scal, *(
         pltpu.with_memory_space_constraint(value, pltpu.HBM)
         for value in (
             panels.reshape((per_dev,) + panels.shape[3:]), coupling, table, layer_depth.reshape(1, -1),
             panel_owner.reshape(1, -1), panel_block.reshape(1, -1), layer_speed, u_now, u_prev, lateral,
         )
     ))
-    ints_o = swap(ints)
-    tiles = comps * size_x
-    extra = 2 * (width // size_z) * (per_dev // HALO)
-    state = (scal, un_v, up_v, lat_v, un_o, up_o, lat_o, ints, ints_o)
-    state_specs = [smem] + [vmem] * 8
-    tiles_scratch = pltpu.VMEM((2 * tiles + extra, HALO, size_z), F32)
-    packed, pair = pl.pallas_call(
-        pack_kernel,
+    theirs, ints_o = swap(theirs), swap(ints)
+    both, pair = pl.pallas_call(
+        gather_kernel,
         out_shape=(
-            jax.ShapeDtypeStruct(coded_shape(2 * tiles + extra), jnp.int16),
+            jax.ShapeDtypeStruct((2,) + half.shape, jnp.int16),
             jax.ShapeDtypeStruct((2, per_dev, width), F32),
         ),
-        in_specs=state_specs,
-        out_specs=(vmem, vmem),
-        scratch_shapes=[tiles_scratch],
+        in_specs=[vmem] * 4,
+        out_specs=(vmem,) * 2,
         compiler_params=params,
-        name="pack",
-    )(*state)
-    side = send(packed, sizes, route_y)
+        name="gather",
+    )(mine, theirs, ints, ints_o)
+    fields_own, both = lax.optimization_barrier((fields_own, both))
+    side = send(both, sizes, route_y)
+    state = (scal, fields_own, swap(fields_own), ints, ints_o)
+    state_specs = [smem] + [vmem] * 4
+    tiles_scratch = pltpu.VMEM((2, number, HALO, size_z), F32)
     if ny == 4:
         far = send(pair, sizes, lambda i, j, k: (i, j ^ 2 if k == 0 else 3 - j, k))
         side, far = lax.optimization_barrier((side, far))
@@ -682,6 +734,7 @@
         sets = (pair, far, far_o)
     else:
         side_o = swap(side)
+        pair = jnp.where(lax.axis_index("gz") == 0, pair, pair[::-1])
         sets = (jnp.moveaxis(lax.all_gather(pair, "gy"), 0, 1).reshape(2, npanels, -1),)
     shared = state + (side, side_o) + sets
     shared_specs = state_specs + [vmem] * (2 + len(sets))
@@ -722,18 +775,35 @@
     )(*shared)
     final, before, face, ratef, recv = lax.optimization_barrier((final, before, face, ratef, recv))
     recv_o = swap(recv)
+    edges = [jax.ShapeDtypeStruct((comps, depth, size_y, size_z), F32) for depth in (NSTEP, NSTEP - 1)]
+    whole = (scal, final, before, face, ratef)
+    near = pl.pallas_call(
+        near_kernel,
+        out_shape=tuple(edges),
+        in_specs=[smem] + [vmem] * 5,
+        out_specs=(vmem, vmem),
+        scratch_shapes=[face_scratch],
+        compiler_params=params,
+        name="near",
+    )(*whole, recv)
+    near, recv_o = lax.optimization_barrier((near, recv_o))
     return pl.pallas_call(
-        join_kernel,
+        far_kernel,
         out_shape=(
             jax.ShapeDtypeStruct(u_now.shape, F32),
             jax.ShapeDtypeStruct(u_now.shape, F32),
         ),
-        in_specs=[smem] + [vmem] * 6,
-        out_specs=(vmem, vmem),
-        scratch_shapes=[face_scratch, face_scratch],
+        in_specs=[smem] + [vmem] * 7,
+        out_specs=(pl.BlockSpec(memory_space=pl.ANY),) * 2,
+        scratch_shapes=[
+            face_scratch,
+            pltpu.VMEM(edges[0].shape, F32),
+            pltpu.VMEM(edges[1].shape, F32),
+            pltpu.SemaphoreType.DMA((6,)),
+        ],
         compiler_params=params,
-        name="join",
-    )(scal, final, before, face, ratef, recv, recv_o)
+        name="far",
+    )(*whole, recv_o, *near)
 
 
 def solution(mesh):

time: 29.6 us -> 26.6 us (0.90)
  Pallas kernels: 13.4 us -> 11.3 us
  starting transfers between devices: 9.23 us -> 8.16 us
    pallas_call x1, Pallas kernels: 6.05 us -> 4.2 us  [per_device(): pl.pallas_call(local_kernel, out_shape=(jax.ShapeDtypeStruct(u_now.shape,...]
    ppermute x10 -> x9, starting transfers between devices: 9.23 us -> 8.16 us  [send(): return lax.ppermute(value, ('gx', 'gy', 'gz'), pairs)]
    pallas_call x2 -> x3, Pallas kernels: 3.88 us -> 2.84 us  [the longest x1 1.77 us: per_device(): pl.pallas_call(far_kernel, out_shape=(jax.ShapeDtypeStruct(u_now.shape, F...]
    pallas_call x1, Pallas kernels: 1.6 us -> 2.53 us  [per_device(): pl.pallas_call(prepare_kernel, out_shape=(jax.ShapeDtypeStruct((per_dev +...]
    ppermute x10 -> x9, waiting for transfers between devices: 6.03 us -> 6.23 us  [send(): return lax.ppermute(value, ('gx', 'gy', 'gz'), pairs)]
  transfers between devices with their start and end apart: 10 -> 9, of which waited for: 4 -> 5; matrix products, arithmetic and copies ran while one was open for 0% -> 0% of each run, Pallas kernels for 26% -> 20%
where the time goes in v4:
time: 26.6 us; the launch traced here: 26.5 us
  Pallas kernels  11.3 us (42%)
  starting transfers between devices  8.16 us (31%)
  waiting for transfers between devices  6.23 us (23%)
  between operations  0.69 us (3%)
    ppermute x9, starting transfers between devices, send(): return lax.ppermute(value, ('gx', 'gy', 'gz'), pairs)  8.16 us
    ppermute x9, waiting for transfers between devices, send(): return lax.ppermute(value, ('gx', 'gy', 'gz'), pairs)  6.23 us
    pallas_call x1, Pallas kernels, per_device(): pl.pallas_call(local_kernel, out_shape=(jax.ShapeDtypeStruct(u_now.shape,...  4.2 us
    pallas_call x1, Pallas kernels, per_device(): pl.pallas_call(prepare_kernel, out_shape=(jax.ShapeDtypeStruct((per_dev +...  2.53 us
    pallas_call x1, Pallas kernels, per_device(): pl.pallas_call(far_kernel, out_shape=(jax.ShapeDtypeStruct(u_now.shape, F...  1.77 us
    pallas_call x1, Pallas kernels, per_device(): pl.pallas_call(face_kernel, out_shape=jax.ShapeDtypeStruct(coded_shape(2...  1.72 us
    pallas_call x1, Pallas kernels, per_device(): pl.pallas_call(near_kernel, out_shape=tuple(edges), in_specs=[smem] + [vm...  1.05 us
  transfers between devices with their start and end apart: 9, of which 5 were waited for; matrix products, arithmetic and copies ran while one was open for 0% of the time, Pallas kernels for 20%

profile of v4, /device:TPU:0, one launch (start us, length us, event | category | flops | bytes accessed | tf_op | source)
XLA Modules:
  0.0 26.5 jit_solution(15928590712474722596)
XLA Ops:
  0.6 0.1 pad_add_fusion.scal_ref
  0.7 2.5 %prepare.1 = (f32[24,256]{1,0:T(8,128)S(1)}, f32[7,16,16,128]{3,2,1,0:T(8,128)S(1)}, s16[27,16,128]{2,1,0:T(8,128)(2,1)S(1)}, s16[27,16,128]{2,1,0:T(8,128)(2,1)S(1)}) custom-call(s32[5]{0:T(128)S(1)} %pad_add_fusion.scal_ref, bf16[16,48,256]{2,1,0:T(8,128)(2,1)} %bitcast.7, f32[3,16,16]{2,1,0:T(8,128)} %coupling_hbm.1, ...), custom_call_target="tpu_custom_call" | custom-call | tf_op jit(solution)/shard_map/prepare/pallas_call | solution.py:683
  3.3 0.5 %collective-permute-start = (s16[27,16,128]{2,1,0:T(8,128)(2,1)S(1)}, s16[27,16,128]{2,1,0:T(8,128)(2,1)S(1)}, u32[]{:S(2)}, u32[]{:S(2)}) collective-permute-start(s16[27,16,128]{2,1,0:T(8,128)(2,1)S(1)} %get-tuple-element.28), channel_id=1, source_target_pairs={{0,1},{1,0},{2,3},{3,2},{4,5},{5,4},{6,7},{7,6},{8,9},{9,8},{10,11... | collective-permute-start | bytes 331784 | tf_op jit(solution)/shard_map/ppermute | solution.py:639
  3.8 0.1 collective-permute-start.1
  3.9 1.1 %collective-permute-done.1.intso_ref = f32[24,256]{1,0:T(8,128)S(1)} collective-permute-done((f32[24,256]{1,0:T(8,128)S(1)}, f32[24,256]{1,0:T(8,128)S(1)}, u32[]{:S(2)}, u32[]{:S(2)}) %collective-permute-start.1) | collective-permute-done | bytes 24608 | tf_op jit(solution)/shard_map/ppermute | solution.py:639
  5.0 0.0 collective-permute-done.theirs_ref
  5.0 0.2 collective-permute-start.2
  5.2 2.9 %collective-permute-start.3 = (s16[2,27,16,128]{3,2,1,0:T(8,128)(2,1)S(1)}, s16[2,27,16,128]{3,2,1,0:T(8,128)(2,1)S(1)}, u32[]{:S(2)}, u32[]{:S(2)}) collective-permute-start(s16[2,27,16,128]{3,2,1,0:T(8,128)(2,1)S(1)} %get-tuple-element.32), channel_id=1, source_target_pairs={{0,2},{1,9},{2,0},{3,5},{4,6},{5,3},{6,4},{7,15},{8,10},{9,1},{10,... | collective-permute-start | bytes 663560 | tf_op jit(solution)/shard_map/ppermute | solution.py:639
  8.2 2.6 %collective-permute-start.4 = (f32[2,16,256]{2,1,0:T(8,128)S(1)}, f32[2,16,256]{2,1,0:T(8,128)S(1)}, u32[]{:S(2)}, u32[]{:S(2)}) collective-permute-start(f32[2,16,256]{2,1,0:T(8,128)S(1)} %get-tuple-element.33.rest_0_), channel_id=1, source_target_pairs={{0,4},{1,7},{2,6},{3,5},{4,0},{5,3},{6,2},{7,1},{8,12},{9,15},{10,... | collective-permute-start | bytes 98312 | tf_op jit(solution)/shard_map/ppermute | solution.py:639
  10.7 2.9 %collective-permute-done.4.rest_1_ = f32[2,16,256]{2,1,0:T(8,128)S(1)} collective-permute-done((f32[2,16,256]{2,1,0:T(8,128)S(1)}, f32[2,16,256]{2,1,0:T(8,128)S(1)}, u32[]{:S(2)}, u32[]{:S(2)}) %collective-permute-start.4) | collective-permute-done | bytes 32800 | tf_op jit(solution)/shard_map/ppermute | solution.py:639
  13.6 0.0 collective-permute-done.3.coded_ref
  13.6 0.0 collective-permute-start.5
  13.6 0.5 %collective-permute-start.6 = (f32[2,16,256]{2,1,0:T(8,128)S(1)}, f32[2,16,256]{2,1,0:T(8,128)S(1)}, u32[]{:S(2)}, u32[]{:S(2)}) collective-permute-start(f32[2,16,256]{2,1,0:T(8,128)S(1)} %collective-permute-done.4.rest_1_), channel_id=1, source_target_pairs={{0,1},{1,0},{2,3},{3,2},{4,5},{5,4},{6,7},{7,6},{8,9},{9,8},{10,11... | collective-permute-start | bytes 98312 | tf_op jit(solution)/shard_map/ppermute | solution.py:639
  14.1 1.0 %collective-permute-done.6.rest_2_ = f32[2,16,256]{2,1,0:T(8,128)S(1)} collective-permute-done((f32[2,16,256]{2,1,0:T(8,128)S(1)}, f32[2,16,256]{2,1,0:T(8,128)S(1)}, u32[]{:S(2)}, u32[]{:S(2)}) %collective-permute-start.6) | collective-permute-done | bytes 32800 | tf_op jit(solution)/shard_map/ppermute | solution.py:639
  15.2 0.0 collective-permute-done.5.codedo_ref
  15.2 0.0 collective-permute-done.2.stateo_ref
  15.2 1.7 %face.1 = s16[34,16,128]{2,1,0:T(8,128)(2,1)S(1)} custom-call(s32[5]{0:T(128)S(1)} %pad_add_fusion.scal_ref, f32[7,16,16,128]{3,2,1,0:T(8,128)S(1)} %get-tuple-element.31.state_ref, f32[7,16,16,128]{3,2,1,0:T(8,128)S(1)} %collective-permute-done.2.stateo_ref, f32[24,256]{1,0:T(8,128)S(1)} %get-tuple-element.29.ints_ref, ...), custom_call_target="tpu_custom_call" | custom-call | tf_op jit(solution)/shard_map/face/pallas_call | solution.py:744
  16.9 1.3 %collective-permute-start.7 = (s16[34,16,128]{2,1,0:T(8,128)(2,1)S(1)}, s16[34,16,128]{2,1,0:T(8,128)(2,1)S(1)}, u32[]{:S(2)}, u32[]{:S(2)}) collective-permute-start(s16[34,16,128]{2,1,0:T(8,128)(2,1)S(1)} %face.1), channel_id=1, source_target_pairs={{0,8},{1,25},{2,10},{3,27},{4,12},{5,29},{6,14},{7,31},{8,0},{9,17... | collective-permute-start | bytes 417800 | tf_op jit(solution)/shard_map/ppermute | solution.py:639
  18.2 4.2 %local.1 = (f32[3,16,16,128]{3,2,1,0:T(8,128)S(1)}, f32[3,16,16,128]{3,2,1,0:T(8,128)S(1)}, f32[2,2,12,24,128]{4,3,2,1,0:T(8,128)S(1)}, f32[2,2,4,24,128]{4,3,2,1,0:T(8,128)S(1)}) custom-call(s32[5]{0:T(128)S(1)} %pad_add_fusion.scal_ref, f32[7,16,16,128]{3,2,1,0:T(8,128)S(1)} %get-tuple-element.31.state_ref, ...), custom_call_target="tpu_custom_call" | custom-call | tf_op jit(solution)/shard_map/local/pallas_call | solution.py:754
  22.4 0.9 %collective-permute-done.7.coded_ref = s16[34,16,128]{2,1,0:T(8,128)(2,1)S(1)} collective-permute-done((s16[34,16,128]{2,1,0:T(8,128)(2,1)S(1)}, s16[34,16,128]{2,1,0:T(8,128)(2,1)S(1)}, u32[]{:S(2)}, u32[]{:S(2)}) %collective-permute-start.7) | collective-permute-done | bytes 139296 | tf_op jit(solution)/shard_map/ppermute | solution.py:639
  23.3 0.0 collective-permute-start.8
  23.3 1.1 %near.1 = (f32[3,4,16,128]{3,2,1,0:T(8,128)S(1)}, f32[3,3,16,128]{3,2,1,0:T(8,128)S(1)}) custom-call(s32[5]{0:T(128)S(1)} %pad_add_fusion.scal_ref, f32[3,16,16,128]{3,2,1,0:T(8,128)S(1)} %get-tuple-element.40.final_in, f32[3,16,16,128]{3,2,1,0:T(8,128)S(1)} %get-tuple-element.41.before_in, f32[2,2,12,24,128]{4,3,2,1,0:T(8,128)S(1)} %get-tuple-element.42.face_ref, ...), custom_call_target="tpu_custom_call" | custom-call | tf_op jit(solution)/shard_map/near/pallas_call | solution.py:780
  24.4 0.3 %collective-permute-done.8.coded_ref = s16[34,16,128]{2,1,0:T(8,128)(2,1)S(1)} collective-permute-done((s16[34,16,128]{2,1,0:T(8,128)(2,1)S(1)}, s16[34,16,128]{2,1,0:T(8,128)(2,1)S(1)}, u32[]{:S(2)}, u32[]{:S(2)}) %collective-permute-start.8) | collective-permute-done | bytes 139296 | tf_op jit(solution)/shard_map/ppermute | solution.py:639
  24.7 1.8 %far.1 = (f32[3,16,16,128]{3,2,1,0:T(8,128)}, f32[3,16,16,128]{3,2,1,0:T(8,128)}) custom-call(s32[5]{0:T(128)S(1)} %pad_add_fusion.scal_ref, f32[3,16,16,128]{3,2,1,0:T(8,128)S(1)} %get-tuple-element.40.final_in, f32[3,16,16,128]{3,2,1,0:T(8,128)S(1)} %get-tuple-element.41.before_in, f32[2,2,12,24,128]{4,3,2,1,0:T(8,128)S(1)} %get-tuple-element.42.face_ref, ...), custom_call_target="tpu_custom_call" | custom-call | tf_op jit(solution)/shard_map/far/pallas_call | solution.py:790
  (2 shorter events, 0.0 us)
Async XLA Ops:
  3.3 1.7 %collective-permute-start = (s16[27,16,128]{2,1,0:T(8,128)(2,1)S(1)}, s16[27,16,128]{2,1,0:T(8,128)(2,1)S(1)}, u32[]{:S(2)}, u32[]{:S(2)}) collective-permute-start(s16[27,16,128]{2,1,0:T(8,128)(2,1)S(1)} %get-tuple-element.28), channel_id=1, source_target_pairs={{0,1},{1,0},{2,3},{3,2},{4,5},{5,4},{6,7},{7,6},{8,9},{9,8},{10,11... | collective-permute-start | bytes 331784 | tf_op jit(solution)/shard_map/ppermute | solution.py:639
  3.8 1.2 %collective-permute-start.1 = (f32[24,256]{1,0:T(8,128)S(1)}, f32[24,256]{1,0:T(8,128)S(1)}, u32[]{:S(2)}, u32[]{:S(2)}) collective-permute-start(f32[24,256]{1,0:T(8,128)S(1)} %get-tuple-element.29.ints_ref), channel_id=1, source_target_pairs={{0,1},{1,0},{2,3},{3,2},{4,5},{5,4},{6,7},{7,6},{8,9},{9,8},{10,11... | collective-permute-start | bytes 73736 | tf_op jit(solution)/shard_map/ppermute | solution.py:639
  5.0 10.2 %collective-permute-start.2 = (f32[7,16,16,128]{3,2,1,0:T(8,128)S(1)}, f32[7,16,16,128]{3,2,1,0:T(8,128)S(1)}, u32[]{:S(2)}, u32[]{:S(2)}) collective-permute-start(f32[7,16,16,128]{3,2,1,0:T(8,128)S(1)} %get-tuple-element.31.state_ref), channel_id=1, source_target_pairs={{0,1},{1,0},{2,3},{3,2},{4,5},{5,4},{6,7},{7,6},{8,9},{9,8},{10,11... | collective-permute-start | bytes 2752520 | tf_op jit(solution)/shard_map/ppermute | solution.py:639
  5.2 8.4 %collective-permute-start.3 = (s16[2,27,16,128]{3,2,1,0:T(8,128)(2,1)S(1)}, s16[2,27,16,128]{3,2,1,0:T(8,128)(2,1)S(1)}, u32[]{:S(2)}, u32[]{:S(2)}) collective-permute-start(s16[2,27,16,128]{3,2,1,0:T(8,128)(2,1)S(1)} %get-tuple-element.32), channel_id=1, source_target_pairs={{0,2},{1,9},{2,0},{3,5},{4,6},{5,3},{6,4},{7,15},{8,10},{9,1},{10,... | collective-permute-start | bytes 663560 | tf_op jit(solution)/shard_map/ppermute | solution.py:639
  8.2 5.5 %collective-permute-start.4 = (f32[2,16,256]{2,1,0:T(8,128)S(1)}, f32[2,16,256]{2,1,0:T(8,128)S(1)}, u32[]{:S(2)}, u32[]{:S(2)}) collective-permute-start(f32[2,16,256]{2,1,0:T(8,128)S(1)} %get-tuple-element.33.rest_0_), channel_id=1, source_target_pairs={{0,4},{1,7},{2,6},{3,5},{4,0},{5,3},{6,2},{7,1},{8,12},{9,15},{10,... | collective-permute-start | bytes 98312 | tf_op jit(solution)/shard_map/ppermute | solution.py:639
  13.6 1.5 %collective-permute-start.5 = (s16[2,27,16,128]{3,2,1,0:T(8,128)(2,1)S(1)}, s16[2,27,16,128]{3,2,1,0:T(8,128)(2,1)S(1)}, u32[]{:S(2)}, u32[]{:S(2)}) collective-permute-start(s16[2,27,16,128]{3,2,1,0:T(8,128)(2,1)S(1)} %collective-permute-done.3.coded_ref), channel_id=1, source_target_pairs={{0,1},{1,0},{2,3},{3,2},{4,5},{5,4},{6,7},{7,6},{8,9},{9,8},{10,11... | collective-permute-start | bytes 663560 | tf_op jit(solution)/shard_map/ppermute | solution.py:639
  13.6 1.5 %collective-permute-start.6 = (f32[2,16,256]{2,1,0:T(8,128)S(1)}, f32[2,16,256]{2,1,0:T(8,128)S(1)}, u32[]{:S(2)}, u32[]{:S(2)}) collective-permute-start(f32[2,16,256]{2,1,0:T(8,128)S(1)} %collective-permute-done.4.rest_1_), channel_id=1, source_target_pairs={{0,1},{1,0},{2,3},{3,2},{4,5},{5,4},{6,7},{7,6},{8,9},{9,8},{10,11... | collective-permute-start | bytes 98312 | tf_op jit(solution)/shard_map/ppermute | solution.py:639
  16.9 6.4 %collective-permute-start.7 = (s16[34,16,128]{2,1,0:T(8,128)(2,1)S(1)}, s16[34,16,128]{2,1,0:T(8,128)(2,1)S(1)}, u32[]{:S(2)}, u32[]{:S(2)}) collective-permute-start(s16[34,16,128]{2,1,0:T(8,128)(2,1)S(1)} %face.1), channel_id=1, source_target_pairs={{0,8},{1,25},{2,10},{3,27},{4,12},{5,29},{6,14},{7,31},{8,0},{9,17... | collective-permute-start | bytes 417800 | tf_op jit(solution)/shard_map/ppermute | solution.py:639
  23.3 1.4 %collective-permute-start.8 = (s16[34,16,128]{2,1,0:T(8,128)(2,1)S(1)}, s16[34,16,128]{2,1,0:T(8,128)(2,1)S(1)}, u32[]{:S(2)}, u32[]{:S(2)}) collective-permute-start(s16[34,16,128]{2,1,0:T(8,128)(2,1)S(1)} %collective-permute-done.7.coded_ref), channel_id=1, source_target_pairs={{0,1},{1,0},{2,3},{3,2},{4,5},{5,4},{6,7},{7,6},{8,9},{9,8},{10,11... | collective-permute-start | bytes 417800 | tf_op jit(solution)/shard_map/ppermute | solution.py:639

commit v5 on v4

--- a/solution.py
+++ b/solution.py
@@ -112,16 +112,25 @@
     ])
 
 
-def expand_sides(ref, tiles_ref, first, choose):
+def expand_sides(ref, tiles_ref, far_ref, first, groups, choose):
+    last = len(groups) // 2
+    forces = len(groups) - far_ref.shape[1]
     for half in range(2):
         z = first if half == 0 else 1 - first
 
         def store(t, value):
             tiles_ref[z, t] = value
 
-        scales = scales_of(ref[half, ref.shape[1] - 1])
+        def store_far(t, value):
+            far_ref[z, t] = value
+
+        scales = scales_of(ref[half, last])
         for moved, blocks in choose(scales):
             expand(lambda i: ref[half, i], store, moved, blocks)
+        if ref.shape[1] > last + 1:
+            expand(lambda i: ref[half, last + 1 + i], store_far, scales_of(ref[half, ref.shape[1] - 1]), [
+                ((t - forces) // 2, groups[t], groups[t + 1]) for t in range(forces, len(groups), 2)
+            ])
 
 
 def prepare_kernel(
@@ -207,41 +216,43 @@
     return jnp.concatenate(out, axis=1)
 
 
-def gather_kernel(mine_ref, theirs_ref, ints_ref, intso_ref, both_ref, pair_ref):
-    both_ref[0] = mine_ref[...]
-    both_ref[1] = theirs_ref[...]
-    pair_ref[0] = ints_ref[0:PANELS]
-    pair_ref[1] = intso_ref[0:PANELS]
-
-
-def place_forces(scal_ref, sets, all_ref):
-    if len(sets) == 1:
-        return sets[0]
-    own_ref, side_ref, sideo_ref, far_ref, faro_ref = sets
+def place_forces(scal_ref, ints_ref, intso_ref, sets, all_ref):
     o, mine = scal_ref[1], scal_ref[2]
-    count, lanes = own_ref.shape[1:]
+    side_ref, sideo_ref, far_ref, faro_ref = sets
+    count, lanes = PANELS, ints_ref.shape[1]
     beside, opposite, mirror = o + 1 - 2 * lax.rem(o, 2), lax.rem(o + 2, 4), 3 - o
     size_z = side_ref.shape[-1]
     step = count // HALO
-    tiles = side_ref.shape[1] - lanes // size_z * step
     here = mine == 0
 
     def spot(j):
         return pl.ds(pl.multiple_of(j * count, count), count)
 
-    for ref, j in ((side_ref, jnp.where(here, beside, mirror)), (sideo_ref, jnp.where(here, mirror, beside))):
+    for ref, j in (
+        (side_ref, jnp.where(here, beside, mirror)),
+        (sideo_ref, jnp.where(here, mirror, beside)),
+        (far_ref, jnp.where(here, opposite, mirror)),
+        (faro_ref, jnp.where(here, mirror, opposite)),
+    ):
+        first = ref.shape[1] - lanes // size_z * step
         for z in range(2):
             for part in range(lanes // size_z):
-                at = tiles + part * step
+                at = first + part * step
                 all_ref[z, spot(j), part * size_z:(part + 1) * size_z] = ref[z, at:at + step].reshape(count, size_z)
-    for ref, j, first in (
-        (far_ref, jnp.where(here, opposite, mirror), mine),
-        (faro_ref, jnp.where(here, mirror, opposite), 1 - mine),
-        (own_ref, o, mine),
-    ):
-        all_ref[first, spot(j), :] = ref[0]
-        all_ref[1 - first, spot(j), :] = ref[1]
+    all_ref[mine, spot(o), :] = ints_ref[0:count]
+    all_ref[1 - mine, spot(o), :] = intso_ref[0:count]
     return all_ref
+
+
+def index_kernel(scal_ref, ints_ref, intso_ref, at_ref, hit_ref, *, sizes, block, panels):
+    size_x, size_y, size_z = sizes
+    rows = size_y + HALO
+    for z, ints in ((scal_ref[2], ints_ref), (1 - scal_ref[2], intso_ref)):
+        keys, depth = panel_keys(ints, scal_ref[1], panels, rows, size_x, size_y, size_z // block)
+        at = (iota((size_z, depth.shape[1]), 0) >> shift_of(block)) == depth
+        at_ref[z] = jnp.transpose(at.astype(F32))
+        hit = iota((size_x * rows, keys.shape[1]), 0) == keys
+        hit_ref[z] = hit.astype(F32).astype(BF16)
 
 
 def panel_keys(ints_ref, o, panels, rows, size_x, size_y, zblocks):
@@ -258,16 +269,14 @@
     return jnp.where(row < 0, -1, key + row), depth
 
 
-def spread_forces(force, depth, size_z, block, steps):
+def spread_forces(force, at, block, steps):
     high = force.astype(BF16).astype(F32)
     both = jnp.concatenate([high, force - high], axis=0)
-    rows = both.shape[0]
+    rows, size_z = at.shape
     lane = iota((rows, size_z), 1) >> shift_of(block)
     base = (
         (iota((size_z, size_z), 0) & (block - 1)) == (iota((size_z, size_z), 1) & (block - 1))
     ).astype(BF16)
-    at = (iota((size_z, rows), 0) >> shift_of(block)) == depth
-    at = jnp.transpose(at.astype(F32))
     per_tile = size_z // block
     out = []
     for q in range(steps * 3):
@@ -310,11 +319,17 @@
     return upper, lower
 
 
+def forces_of(scal_ref, ints_ref, intso_ref, rest, all_ref, scratch):
+    if rest:
+        return rest[0]
+    return place_forces(scal_ref, ints_ref, intso_ref, scratch, all_ref)
+
+
 def face_kernel(
-    scal_ref, state_ref, stateo_ref, ints_ref, intso_ref,
-    coded_ref, codedo_ref, *rest,
+    scal_ref, state_ref, stateo_ref, ints_ref, intso_ref, at_ref, hit_ref, coded_ref, codedo_ref, *rest,
 ):
-    *sets, out_ref, all_ref, side_ref, sideo_ref, faces_ref = rest
+    *rest, out_ref, all_ref, side_ref, sideo_ref, far_ref, faro_ref, faces_ref = rest
+    scratch = side_ref, sideo_ref, far_ref, faro_ref
     (un_ref, up_ref, lat_ref), (uno_ref, upo_ref, lato_ref) = fields(state_ref), fields(stateo_ref)
     comps, size_x, size_y, size_z = un_ref.shape
     rows = size_y + HALO
@@ -331,26 +346,23 @@
         rest = [(t // 2, groups[t], groups[t + 1]) for t in range(tiles, len(groups), 2)]
         return (moved, [(t // 2 + lax.div(skip, 2), groups[t], groups[t + 1]) for t in near]), (scales, rest)
 
-    expand_sides(coded_ref, side_ref, mine, choose)
-    expand_sides(codedo_ref, sideo_ref, 1 - mine, choose)
-    forces = place_forces(scal_ref, with_sides(sets, side_ref, sideo_ref), all_ref)
-    panels = forces.shape[1]
+    expand_sides(coded_ref, side_ref, far_ref, mine, groups, choose)
+    expand_sides(codedo_ref, sideo_ref, faro_ref, 1 - mine, groups, choose)
+    forces = forces_of(scal_ref, ints_ref, intso_ref, rest, all_ref, scratch)
     own = mine == 0
     now, old, rate, drive = {}, {}, {}, {}
     for z in range(2):
-        keys, depth = panel_keys_of(z, own, ints_ref, intso_ref, o, panels, rows, size_x, size_y, size_z)
-        wide = spread_forces(forces[z], depth, size_z, size_z // (size_z // 16), NSTEP - 1)
-        first = jnp.where(high, size_x - NSTEP + 1, 0)
-        node = iota(((NSTEP - 1) * rows, keys.shape[1]), 0) + first * rows
-        hit = (node == keys).astype(F32).astype(BF16)
+        wide = spread_forces(forces[z], at_ref[z], 16, NSTEP - 1)
+        first = pl.multiple_of(jnp.where(high, size_x - NSTEP, 0) * rows, 2 * HALO)
+        hit = hit_ref[z, pl.ds(first, NSTEP * rows)]
         got = jnp.dot(hit, wide, preferred_element_type=F32)
-        got = got.reshape(NSTEP - 1, rows, wide.shape[1])
+        got = got.reshape(NSTEP, rows, wide.shape[1])
         for d in range(1, NSTEP):
             for n in range(NSTEP - d):
                 for c in range(comps):
                     q = (n * comps + c) * size_z
                     drive[z, n, d, c] = jnp.where(
-                        high, got[NSTEP - 1 - d, :, q:q + size_z], got[d - 1, :, q:q + size_z]
+                        high, got[NSTEP - d, :, q:q + size_z], got[d - 1, :, q:q + size_z]
                     )
         speed = jnp.where(
             own if z == 0 else jnp.logical_not(own),
@@ -443,27 +455,13 @@
     return jnp.concatenate(parts, axis=0)
 
 
-def with_sides(sets, side_ref, sideo_ref):
-    if len(sets) == 1:
-        return sets
-    own_ref, far_ref, faro_ref = sets
-    return own_ref, side_ref, sideo_ref, far_ref, faro_ref
-
-
-def panel_keys_of(z, own, ints_ref, intso_ref, o, panels, rows, size_x, size_y, size_z):
-    near = own if z == 0 else jnp.logical_not(own)
-    zblocks = size_z // 16
-    mine = panel_keys(ints_ref, o, panels, rows, size_x, size_y, zblocks)
-    theirs = panel_keys(intso_ref, o, panels, rows, size_x, size_y, zblocks)
-    return tuple(jnp.where(near, one, two) for one, two in zip(mine, theirs))
-
-
 def local_kernel(
-    scal_ref, state_ref, stateo_ref, ints_ref, intso_ref,
-    coded_ref, codedo_ref, *rest,
+    scal_ref, state_ref, stateo_ref, ints_ref, intso_ref, at_ref, hit_ref, coded_ref, codedo_ref, *rest,
 ):
-    *sets, final_ref, before_ref, face_ref, ratef_ref, all_ref, side_ref, sideo_ref = rest[:-4]
     now_ref, old_ref, rate_ref, drive_ref = rest[-4:]
+    all_ref, side_ref, sideo_ref, far_ref, faro_ref = rest[-9:-4]
+    *rest, final_ref, before_ref, face_ref, ratef_ref = rest[:-9]
+    scratch = side_ref, sideo_ref, far_ref, faro_ref
     (un_ref, up_ref, lat_ref), (uno_ref, upo_ref, lato_ref) = fields(state_ref), fields(stateo_ref)
     comps, size_x, size_y, size_z = un_ref.shape
     rows = size_y + HALO
@@ -473,16 +471,13 @@
     choose = lambda scales: (
         (scales, [(t // 2, groups[t], groups[t + 1]) for t in range(0, len(groups), 2)]),
     )
-    expand_sides(coded_ref, side_ref, mine, choose)
-    expand_sides(codedo_ref, sideo_ref, 1 - mine, choose)
-    forces = place_forces(scal_ref, with_sides(sets, side_ref, sideo_ref), all_ref)
-    panels = forces.shape[1]
+    expand_sides(coded_ref, side_ref, far_ref, mine, groups, choose)
+    expand_sides(codedo_ref, sideo_ref, faro_ref, 1 - mine, groups, choose)
+    forces = forces_of(scal_ref, ints_ref, intso_ref, rest, all_ref, scratch)
     own = mine == 0
     for z in range(2):
-        keys, depth = panel_keys_of(z, own, ints_ref, intso_ref, o, panels, rows, size_x, size_y, size_z)
-        wide = spread_forces(forces[z], depth, size_z, 16, NSTEP)
-        node = iota((size_x * rows, keys.shape[1]), 0)
-        hit = (node == keys).astype(F32).astype(BF16)
+        wide = spread_forces(forces[z], at_ref[z], 16, NSTEP)
+        hit = hit_ref[z]
         for n in range(NSTEP):
             span = comps * size_z
             got = jnp.dot(hit, wide[:, n * span:(n + 1) * span], preferred_element_type=F32)
@@ -710,34 +705,37 @@
             panel_owner.reshape(1, -1), panel_block.reshape(1, -1), layer_speed, u_now, u_prev, lateral,
         )
     ))
-    theirs, ints_o = swap(theirs), swap(ints)
-    both, pair = pl.pallas_call(
-        gather_kernel,
+    both = jnp.stack([mine, swap(theirs)])
+    ints, fields_own, both = lax.optimization_barrier((ints, fields_own, both))
+    side = send(both, sizes, route_y)
+    ints_o, fields_o = swap(ints), swap(fields_own)
+    index = pl.pallas_call(
+        functools.partial(
+            index_kernel, sizes=u_now.shape[1:], block=coupling.shape[1], panels=npanels
+        ),
         out_shape=(
-            jax.ShapeDtypeStruct((2,) + half.shape, jnp.int16),
-            jax.ShapeDtypeStruct((2, per_dev, width), F32),
+            jax.ShapeDtypeStruct((2, 2 * npanels, size_z), F32),
+            jax.ShapeDtypeStruct((2, size_x * rows, 2 * npanels), BF16),
         ),
-        in_specs=[vmem] * 4,
+        in_specs=[smem] + [vmem] * 2,
         out_specs=(vmem,) * 2,
         compiler_params=params,
-        name="gather",
-    )(mine, theirs, ints, ints_o)
-    fields_own, both = lax.optimization_barrier((fields_own, both))
-    side = send(both, sizes, route_y)
-    state = (scal, fields_own, swap(fields_own), ints, ints_o)
-    state_specs = [smem] + [vmem] * 4
-    tiles_scratch = pltpu.VMEM((2, number, HALO, size_z), F32)
+        name="index",
+    )(scal, ints, ints_o)
+    sets = ()
     if ny == 4:
-        far = send(pair, sizes, lambda i, j, k: (i, j ^ 2 if k == 0 else 3 - j, k))
-        side, far = lax.optimization_barrier((side, far))
-        side_o, far_o = swap(side), swap(far)
-        sets = (pair, far, far_o)
+        forces = both[:, tiles // 2:]
+        far = send(forces, sizes, lambda i, j, k: (i, j ^ 2 if k == 0 else 3 - j, k))
+        side = jnp.concatenate([side, far], axis=1)
     else:
-        side_o = swap(side)
+        pair = jnp.stack([ints[0:per_dev], ints_o[0:per_dev]])
         pair = jnp.where(lax.axis_index("gz") == 0, pair, pair[::-1])
         sets = (jnp.moveaxis(lax.all_gather(pair, "gy"), 0, 1).reshape(2, npanels, -1),)
-    shared = state + (side, side_o) + sets
-    shared_specs = state_specs + [vmem] * (2 + len(sets))
+    side, index, ints_o, fields_o = lax.optimization_barrier((side, index, ints_o, fields_o))
+    shared = (scal, fields_own, fields_o, ints, ints_o, *index, side, swap(side)) + sets
+    shared_specs = [smem] + [vmem] * (8 + len(sets))
+    tiles_scratch = pltpu.VMEM((2, number, HALO, size_z), F32)
+    far_scratch = pltpu.VMEM((2, number - tiles, HALO, size_z), F32)
     all_scratch = pltpu.VMEM((2, npanels, width), F32)
     planes = NSTEP * comps
     face_scratch = pltpu.VMEM((2 * face_tiles(comps), HALO, size_z), F32)
@@ -746,7 +744,7 @@
         out_shape=jax.ShapeDtypeStruct(coded_shape(2 * face_tiles(comps)), jnp.int16),
         in_specs=shared_specs,
         out_specs=vmem,
-        scratch_shapes=[all_scratch, tiles_scratch, tiles_scratch, face_scratch],
+        scratch_shapes=[all_scratch, tiles_scratch, tiles_scratch, far_scratch, far_scratch, face_scratch],
         compiler_params=params,
         name="face",
     )(*shared)
@@ -765,6 +763,8 @@
             all_scratch,
             tiles_scratch,
             tiles_scratch,
+            far_scratch,
+            far_scratch,
             pltpu.VMEM((2, comps, size_x + 2, rows, size_z), F32),
             pltpu.VMEM((2, comps, size_x + 2, rows, size_z), F32),
             pltpu.VMEM((2, size_x, rows, size_z), F32),

time: 26.6 us -> 26.2 us (0.985)
  waiting for transfers between devices: 6.23 us -> 5.4 us
  Pallas kernels: 11.3 us -> 11.9 us
    ppermute x9 -> x8, waiting for transfers between devices: 6.23 us -> 5.4 us  [send(): return lax.ppermute(value, ('gx', 'gy', 'gz'), pairs)]
    pallas_call x1, Pallas kernels: 0.02 us -> 0.69 us  [per_device(): pl.pallas_call(functools.partial(index_kernel, sizes=u_now.shape[1:], blo...]
    ppermute x9 -> x8, starting transfers between devices: 8.16 us -> 7.97 us  [send(): return lax.ppermute(value, ('gx', 'gy', 'gz'), pairs)]
  transfers between devices with their start and end apart: 9 -> 8, of which waited for: 5 -> 5; matrix products, arithmetic and copies ran while one was open for 0% -> 0% of each run, Pallas kernels for 20% -> 22%
where the time goes in v5:
time: 26.2 us; the launch traced here: 26.1 us
  Pallas kernels  11.9 us (45%)
  starting transfers between devices  7.97 us (30%)
  waiting for transfers between devices  5.4 us (21%)
  between operations  0.7 us (3%)
    ppermute x8, starting transfers between devices, send(): return lax.ppermute(value, ('gx', 'gy', 'gz'), pairs)  7.97 us
    ppermute x8, waiting for transfers between devices, send(): return lax.ppermute(value, ('gx', 'gy', 'gz'), pairs)  5.4 us
    pallas_call x1, Pallas kernels, per_device(): pl.pallas_call(local_kernel, out_shape=(jax.ShapeDtypeStruct(u_now.shape,...  4.12 us
    pallas_call x1, Pallas kernels, per_device(): pl.pallas_call(prepare_kernel, out_shape=(jax.ShapeDtypeStruct((per_dev +...  2.53 us
    pallas_call x1, Pallas kernels, per_device(): pl.pallas_call(far_kernel, out_shape=(jax.ShapeDtypeStruct(u_now.shape, F...  1.77 us
    pallas_call x1, Pallas kernels, per_device(): pl.pallas_call(face_kernel, out_shape=jax.ShapeDtypeStruct(coded_shape(2...  1.7 us
    pallas_call x1, Pallas kernels, per_device(): pl.pallas_call(near_kernel, out_shape=tuple(edges), in_specs=[smem] + [vm...  1.05 us
    pallas_call x1, Pallas kernels, per_device(): pl.pallas_call(functools.partial(index_kernel, sizes=u_now.shape[1:], blo...  0.69 us
  transfers between devices with their start and end apart: 8, of which 5 were waited for; matrix products, arithmetic and copies ran while one was open for 0% of the time, Pallas kernels for 22%

profile of v5, /device:TPU:0, one launch (start us, length us, event | category | flops | bytes accessed | tf_op | source)
XLA Modules:
  0.0 26.1 jit_solution(4682841730270340903)
XLA Ops:
  0.6 0.1 pad_add_fusion.2.scal_ref
  0.7 2.5 %prepare.1 = (f32[24,256]{1,0:T(8,128)S(1)}, f32[7,16,16,128]{3,2,1,0:T(8,128)S(1)}, s16[27,16,128]{2,1,0:T(8,128)(2,1)S(1)}, s16[27,16,128]{2,1,0:T(8,128)(2,1)S(1)}) custom-call(s32[5]{0:T(128)S(1)} %pad_add_fusion.2.scal_ref, bf16[16,48,256]{2,1,0:T(8,128)(2,1)} %bitcast.10, f32[3,16,16]{2,1,0:T(8,128)} %coupling_hbm.1, ...), custom_call_target="tpu_custom_call" | custom-call | tf_op jit(solution)/shard_map/prepare/pallas_call | solution.py:678
  3.3 0.5 %collective-permute-start = (s16[27,16,128]{2,1,0:T(8,128)(2,1)S(1)}, s16[27,16,128]{2,1,0:T(8,128)(2,1)S(1)}, u32[]{:S(2)}, u32[]{:S(2)}) collective-permute-start(s16[27,16,128]{2,1,0:T(8,128)(2,1)S(1)} %get-tuple-element.33), channel_id=1, source_target_pairs={{0,1},{1,0},{2,3},{3,2},{4,5},{5,4},{6,7},{7,6},{8,9},{9,8},{10,11... | collective-permute-start | bytes 331784 | tf_op jit(solution)/shard_map/ppermute | solution.py:634
  3.8 1.0 %collective-permute-done = s16[27,16,128]{2,1,0:T(8,128)(2,1)S(1)} collective-permute-done((s16[27,16,128]{2,1,0:T(8,128)(2,1)S(1)}, s16[27,16,128]{2,1,0:T(8,128)(2,1)S(1)}, u32[]{:S(2)}, u32[]{:S(2)}) %collective-permute-start) | collective-permute-done | bytes 110624 | tf_op jit(solution)/shard_map/ppermute | solution.py:634
  4.8 0.4 %collective-permute-start.4 = (f32[7,16,16,128]{3,2,1,0:T(8,128)S(1)}, f32[7,16,16,128]{3,2,1,0:T(8,128)S(1)}, u32[]{:S(2)}, u32[]{:S(2)}) collective-permute-start(f32[7,16,16,128]{3,2,1,0:T(8,128)S(1)} %get-tuple-element.34.state_ref), channel_id=1, source_target_pairs={{0,1},{1,0},{2,3},{3,2},{4,5},{5,4},{6,7},{7,6},{8,9},{9,8},{10,11... | collective-permute-start | bytes 2752520 | tf_op jit(solution)/shard_map/ppermute | solution.py:634
  5.2 2.7 %collective-permute-start.1 = (s16[2,27,16,128]{3,2,1,0:T(8,128)(2,1)S(1)}, s16[2,27,16,128]{3,2,1,0:T(8,128)(2,1)S(1)}, u32[]{:S(2)}, u32[]{:S(2)}) collective-permute-start(s16[2,27,16,128]{3,2,1,0:T(8,128)(2,1)S(1)} %pad_add_fusion.1), channel_id=1, source_target_pairs={{0,2},{1,9},{2,0},{3,5},{4,6},{5,3},{6,4},{7,15},{8,10},{9,1},{10,... | collective-permute-start | bytes 663560 | tf_op jit(solution)/shard_map/ppermute | solution.py:634
  7.9 0.0 collective-permute-start.3
  7.9 2.6 %collective-permute-start.2 = (s16[2,3,16,128]{3,2,1,0:T(8,128)(2,1)S(1)}, s16[2,3,16,128]{3,2,1,0:T(8,128)(2,1)S(1)}, u32[]{:S(2)}, u32[]{:S(2)}) collective-permute-start(s16[2,3,16,128]{3,2,1,0:T(8,128)(2,1)S(1)} %slice.3), channel_id=1, source_target_pairs={{0,4},{1,7},{2,6},{3,5},{4,0},{5,3},{6,2},{7,1},{8,12},{9,15},{10,... | collective-permute-start | bytes 73736 | tf_op jit(solution)/shard_map/ppermute | solution.py:634
  10.5 0.0 collective-permute-done.3.intso_ref
  10.5 0.7 %index.1 = (f32[2,128,128]{2,1,0:T(8,128)S(1)}, bf16[2,384,128]{2,1,0:T(8,128)(2,1)S(1)}) custom-call(s32[5]{0:T(128)S(1)} %pad_add_fusion.2.scal_ref, f32[24,256]{1,0:T(8,128)S(1)} %get-tuple-element.36.ints_ref, f32[24,256]{1,0:T(8,128)S(1)} %collective-permute-done.3.intso_ref), custom_call_target="tpu_custom_call" | custom-call | tf_op jit(solution)/shard_map/index/pallas_call | solution.py:712
  11.2 1.9 %collective-permute-done.2 = s16[2,3,16,128]{3,2,1,0:T(8,128)(2,1)S(1)} collective-permute-done((s16[2,3,16,128]{3,2,1,0:T(8,128)(2,1)S(1)}, s16[2,3,16,128]{3,2,1,0:T(8,128)(2,1)S(1)}, u32[]{:S(2)}, u32[]{:S(2)}) %collective-permute-start.2) | collective-permute-done | bytes 24608 | tf_op jit(solution)/shard_map/ppermute | solution.py:634
  13.1 0.0 collective-permute-done.1
  13.2 0.0 collective-permute-done.4.stateo_ref
  13.2 0.1 collective-permute-start.5
  13.3 1.5 %collective-permute-done.5.codedo_ref = s16[2,30,16,128]{3,2,1,0:T(8,128)(2,1)S(1)} collective-permute-done((s16[2,30,16,128]{3,2,1,0:T(8,128)(2,1)S(1)}, s16[2,30,16,128]{3,2,1,0:T(8,128)(2,1)S(1)}, u32[]{:S(2)}, u32[]{:S(2)}) %collective-permute-start.5) | collective-permute-done | bytes 245792 | tf_op jit(solution)/shard_map/ppermute | solution.py:634
  14.8 1.7 %face.1 = s16[34,16,128]{2,1,0:T(8,128)(2,1)S(1)} custom-call(s32[5]{0:T(128)S(1)} %pad_add_fusion.2.scal_ref, f32[7,16,16,128]{3,2,1,0:T(8,128)S(1)} %get-tuple-element.34.state_ref, f32[7,16,16,128]{3,2,1,0:T(8,128)S(1)} %collective-permute-done.4.stateo_ref, f32[24,256]{1,0:T(8,128)S(1)} %get-tuple-element.36.ints_ref, ...), custom_call_target="tpu_custom_call" | custom-call | tf_op jit(solution)/shard_map/face/pallas_call | solution.py:742
  16.5 1.6 %collective-permute-start.6 = (s16[34,16,128]{2,1,0:T(8,128)(2,1)S(1)}, s16[34,16,128]{2,1,0:T(8,128)(2,1)S(1)}, u32[]{:S(2)}, u32[]{:S(2)}) collective-permute-start(s16[34,16,128]{2,1,0:T(8,128)(2,1)S(1)} %face.1), channel_id=1, source_target_pairs={{0,8},{1,25},{2,10},{3,27},{4,12},{5,29},{6,14},{7,31},{8,0},{9,17... | collective-permute-start | bytes 417800 | tf_op jit(solution)/shard_map/ppermute | solution.py:634
  18.0 4.1 %local.1 = (f32[3,16,16,128]{3,2,1,0:T(8,128)S(1)}, f32[3,16,16,128]{3,2,1,0:T(8,128)S(1)}, f32[2,2,12,24,128]{4,3,2,1,0:T(8,128)S(1)}, f32[2,2,4,24,128]{4,3,2,1,0:T(8,128)S(1)}) custom-call(s32[5]{0:T(128)S(1)} %pad_add_fusion.2.scal_ref, f32[7,16,16,128]{3,2,1,0:T(8,128)S(1)} %get-tuple-element.34.state_ref, ...), custom_call_target="tpu_custom_call" | custom-call | tf_op jit(solution)/shard_map/local/pallas_call | solution.py:752
  22.2 0.8 %collective-permute-done.6.coded_ref = s16[34,16,128]{2,1,0:T(8,128)(2,1)S(1)} collective-permute-done((s16[34,16,128]{2,1,0:T(8,128)(2,1)S(1)}, s16[34,16,128]{2,1,0:T(8,128)(2,1)S(1)}, u32[]{:S(2)}, u32[]{:S(2)}) %collective-permute-start.6) | collective-permute-done | bytes 139296 | tf_op jit(solution)/shard_map/ppermute | solution.py:634
  22.9 0.1 collective-permute-start.7
  23.0 1.1 %near.1 = (f32[3,4,16,128]{3,2,1,0:T(8,128)S(1)}, f32[3,3,16,128]{3,2,1,0:T(8,128)S(1)}) custom-call(s32[5]{0:T(128)S(1)} %pad_add_fusion.2.scal_ref, f32[3,16,16,128]{3,2,1,0:T(8,128)S(1)} %get-tuple-element.48.final_in, f32[3,16,16,128]{3,2,1,0:T(8,128)S(1)} %get-tuple-element.49.before_in, f32[2,2,12,24,128]{4,3,2,1,0:T(8,128)S(1)} %get-tuple-element.50.face_ref, ...), custom_call_target="tpu_custom_call" | custom-call | tf_op jit(solution)/shard_map/near/pallas_call | solution.py:780
  24.1 0.2 collective-permute-done.7.coded_ref
  24.3 1.8 %far.1 = (f32[3,16,16,128]{3,2,1,0:T(8,128)}, f32[3,16,16,128]{3,2,1,0:T(8,128)}) custom-call(s32[5]{0:T(128)S(1)} %pad_add_fusion.2.scal_ref, f32[3,16,16,128]{3,2,1,0:T(8,128)S(1)} %get-tuple-element.48.final_in, f32[3,16,16,128]{3,2,1,0:T(8,128)S(1)} %get-tuple-element.49.before_in, f32[2,2,12,24,128]{4,3,2,1,0:T(8,128)S(1)} %get-tuple-element.50.face_ref, ...), custom_call_target="tpu_custom_call" | custom-call | tf_op jit(solution)/shard_map/far/pallas_call | solution.py:790
  (4 shorter events, 0.0 us)
Async XLA Ops:
  3.3 1.5 %collective-permute-start = (s16[27,16,128]{2,1,0:T(8,128)(2,1)S(1)}, s16[27,16,128]{2,1,0:T(8,128)(2,1)S(1)}, u32[]{:S(2)}, u32[]{:S(2)}) collective-permute-start(s16[27,16,128]{2,1,0:T(8,128)(2,1)S(1)} %get-tuple-element.33), channel_id=1, source_target_pairs={{0,1},{1,0},{2,3},{3,2},{4,5},{5,4},{6,7},{7,6},{8,9},{9,8},{10,11... | collective-permute-start | bytes 331784 | tf_op jit(solution)/shard_map/ppermute | solution.py:634
  4.8 8.4 %collective-permute-start.4 = (f32[7,16,16,128]{3,2,1,0:T(8,128)S(1)}, f32[7,16,16,128]{3,2,1,0:T(8,128)S(1)}, u32[]{:S(2)}, u32[]{:S(2)}) collective-permute-start(f32[7,16,16,128]{3,2,1,0:T(8,128)S(1)} %get-tuple-element.34.state_ref), channel_id=1, source_target_pairs={{0,1},{1,0},{2,3},{3,2},{4,5},{5,4},{6,7},{7,6},{8,9},{9,8},{10,11... | collective-permute-start | bytes 2752520 | tf_op jit(solution)/shard_map/ppermute | solution.py:634
  5.2 7.9 %collective-permute-start.1 = (s16[2,27,16,128]{3,2,1,0:T(8,128)(2,1)S(1)}, s16[2,27,16,128]{3,2,1,0:T(8,128)(2,1)S(1)}, u32[]{:S(2)}, u32[]{:S(2)}) collective-permute-start(s16[2,27,16,128]{3,2,1,0:T(8,128)(2,1)S(1)} %pad_add_fusion.1), channel_id=1, source_target_pairs={{0,2},{1,9},{2,0},{3,5},{4,6},{5,3},{6,4},{7,15},{8,10},{9,1},{10,... | collective-permute-start | bytes 663560 | tf_op jit(solution)/shard_map/ppermute | solution.py:634
  7.9 2.6 %collective-permute-start.3 = (f32[24,256]{1,0:T(8,128)S(1)}, f32[24,256]{1,0:T(8,128)S(1)}, u32[]{:S(2)}, u32[]{:S(2)}) collective-permute-start(f32[24,256]{1,0:T(8,128)S(1)} %get-tuple-element.36.ints_ref), channel_id=1, source_target_pairs={{0,1},{1,0},{2,3},{3,2},{4,5},{5,4},{6,7},{7,6},{8,9},{9,8},{10,11... | collective-permute-start | bytes 73736 | tf_op jit(solution)/shard_map/ppermute | solution.py:634
  7.9 5.2 %collective-permute-start.2 = (s16[2,3,16,128]{3,2,1,0:T(8,128)(2,1)S(1)}, s16[2,3,16,128]{3,2,1,0:T(8,128)(2,1)S(1)}, u32[]{:S(2)}, u32[]{:S(2)}) collective-permute-start(s16[2,3,16,128]{3,2,1,0:T(8,128)(2,1)S(1)} %slice.3), channel_id=1, source_target_pairs={{0,4},{1,7},{2,6},{3,5},{4,0},{5,3},{6,2},{7,1},{8,12},{9,15},{10,... | collective-permute-start | bytes 73736 | tf_op jit(solution)/shard_map/ppermute | solution.py:634
  13.2 1.6 %collective-permute-start.5 = (s16[2,30,16,128]{3,2,1,0:T(8,128)(2,1)S(1)}, s16[2,30,16,128]{3,2,1,0:T(8,128)(2,1)S(1)}, u32[]{:S(2)}, u32[]{:S(2)}) collective-permute-start(s16[2,30,16,128]{3,2,1,0:T(8,128)(2,1)S(1)} %pad_add_fusion.coded_ref), channel_id=1, source_target_pairs={{0,1},{1,0},{2,3},{3,2},{4,5},{5,4},{6,7},{7,6},{8,9},{9,8},{10,11... | collective-permute-start | bytes 737288 | tf_op jit(solution)/shard_map/ppermute | solution.py:634
  16.5 6.5 %collective-permute-start.6 = (s16[34,16,128]{2,1,0:T(8,128)(2,1)S(1)}, s16[34,16,128]{2,1,0:T(8,128)(2,1)S(1)}, u32[]{:S(2)}, u32[]{:S(2)}) collective-permute-start(s16[34,16,128]{2,1,0:T(8,128)(2,1)S(1)} %face.1), channel_id=1, source_target_pairs={{0,8},{1,25},{2,10},{3,27},{4,12},{5,29},{6,14},{7,31},{8,0},{9,17... | collective-permute-start | bytes 417800 | tf_op jit(solution)/shard_map/ppermute | solution.py:634
  22.9 1.4 %collective-permute-start.7 = (s16[34,16,128]{2,1,0:T(8,128)(2,1)S(1)}, s16[34,16,128]{2,1,0:T(8,128)(2,1)S(1)}, u32[]{:S(2)}, u32[]{:S(2)}) collective-permute-start(s16[34,16,128]{2,1,0:T(8,128)(2,1)S(1)} %collective-permute-done.6.coded_ref), channel_id=1, source_target_pairs={{0,1},{1,0},{2,3},{3,2},{4,5},{5,4},{6,7},{7,6},{8,9},{9,8},{10,11... | collective-permute-start | bytes 417800 | tf_op jit(solution)/shard_map/ppermute | solution.py:634

commit v6 on v5

--- a/solution.py
+++ b/solution.py
@@ -133,11 +133,16 @@
             ])
 
 
+def position():
+    return [lax.axis_index(axis) for axis in ("gx", "gy", "gz")] + [lax.axis_size("gx"), lax.axis_size("gy")]
+
+
 def prepare_kernel(
-    scal_ref, panels_hbm, coupling_hbm, table_hbm, depth_hbm, owner_hbm, block_hbm, speed_hbm,
-    un_hbm, up_hbm, lat_hbm, out_ref, state_ref, mine_ref, theirs_ref, tiles_ref,
+    panels_hbm, coupling_hbm, table_hbm, depth_hbm, owner_hbm, block_hbm, speed_hbm,
+    un_hbm, up_hbm, lat_hbm, out_ref, state_ref, theirs_ref, tiles_ref,
     panels_ref, coupling_ref, table_ref, depth_ref, owner_ref, block_ref, speed_ref, sems,
 ):
+    scal_ref = position()
     comps = un_hbm.shape[0]
     un_ref, up_ref, lat_ref = state_ref.at[0:comps], state_ref.at[comps:2 * comps], state_ref.at[2 * comps]
     pairs = (
@@ -182,9 +187,22 @@
         out_ref[row:row + 1, at:at + LANES] = piece.astype(F32)
     for copy in copies[7:]:
         copy.wait()
+    code_side(state_ref, out_ref, 1 - lax.rem(scal_ref[1] + scal_ref[2], 2), tiles_ref, theirs_ref)
+
+
+def mine_kernel(state_ref, force_ref, mine_ref, tiles_ref):
+    scal_ref = position()
+    code_side(state_ref, force_ref, lax.rem(scal_ref[1] + scal_ref[2], 2), tiles_ref, mine_ref)
+
+
+def code_side(state_ref, force_ref, which, tiles_ref, coded_ref):
+    un_ref, up_ref, lat_ref = fields(state_ref)
     comps, size_x, size_y, size_z = un_ref.shape
+    count, lanes = PANELS, force_ref.shape[1]
+    speed = listed(force_ref, LANES, 0)
     sub = iota((size_x, HALO, size_z), 1)
-    for side in range(2):
+
+    def fill(side):
         base = 0 if side else size_y - HALO
         rate = lat_ref[:, base:base + HALO, :] * speed[None]
         for c in range(comps):
@@ -194,15 +212,16 @@
             row = c if side else HALO - 1 - c
             tile = jnp.where(keep, now, old)
             tile = jnp.where(sub == (HALO - 1 if side else 0), rate[:, row:row + 1, :], tile)
-            tiles_ref[side, c * size_x:(c + 1) * size_x] = tile
-        for part in range(lanes // size_z):
-            for piece in range(count // HALO):
-                at = comps * size_x + part * (count // HALO) + piece
-                tiles_ref[side, at] = out_ref[piece * HALO:(piece + 1) * HALO, part * size_z:(part + 1) * size_z]
-    low = lax.rem(scal_ref[1] + scal_ref[2], 2)
-    groups = side_groups(comps, size_x, tiles_ref.shape[1] - comps * size_x)
-    quantize(lambda t: tiles_ref[low, t], groups, mine_ref)
-    quantize(lambda t: tiles_ref[1 - low, t], groups, theirs_ref)
+            tiles_ref[c * size_x:(c + 1) * size_x] = tile
+
+    for side in range(2):
+        pl.when(which == side)(functools.partial(fill, side))
+    for part in range(lanes // size_z):
+        for piece in range(count // HALO):
+            at = comps * size_x + part * (count // HALO) + piece
+            tiles_ref[at] = force_ref[piece * HALO:(piece + 1) * HALO, part * size_z:(part + 1) * size_z]
+    groups = side_groups(comps, size_x, tiles_ref.shape[0] - comps * size_x)
+    quantize(lambda t: tiles_ref[t], groups, coded_ref)
 
 
 def listed(ref, panels, which):
@@ -244,7 +263,8 @@
     return all_ref
 
 
-def index_kernel(scal_ref, ints_ref, intso_ref, at_ref, hit_ref, *, sizes, block, panels):
+def index_kernel(ints_ref, intso_ref, at_ref, hit_ref, *, sizes, block, panels):
+    scal_ref = position()
     size_x, size_y, size_z = sizes
     rows = size_y + HALO
     for z, ints in ((scal_ref[2], ints_ref), (1 - scal_ref[2], intso_ref)):
@@ -326,8 +346,9 @@
 
 
 def face_kernel(
-    scal_ref, state_ref, stateo_ref, ints_ref, intso_ref, at_ref, hit_ref, coded_ref, codedo_ref, *rest,
+    state_ref, stateo_ref, ints_ref, intso_ref, at_ref, hit_ref, coded_ref, codedo_ref, *rest,
 ):
+    scal_ref = position()
     *rest, out_ref, all_ref, side_ref, sideo_ref, far_ref, faro_ref, faces_ref = rest
     scratch = side_ref, sideo_ref, far_ref, faro_ref
     (un_ref, up_ref, lat_ref), (uno_ref, upo_ref, lato_ref) = fields(state_ref), fields(stateo_ref)
@@ -456,8 +477,9 @@
 
 
 def local_kernel(
-    scal_ref, state_ref, stateo_ref, ints_ref, intso_ref, at_ref, hit_ref, coded_ref, codedo_ref, *rest,
+    state_ref, stateo_ref, ints_ref, intso_ref, at_ref, hit_ref, coded_ref, codedo_ref, *rest,
 ):
+    scal_ref = position()
     now_ref, old_ref, rate_ref, drive_ref = rest[-4:]
     all_ref, side_ref, sideo_ref, far_ref, faro_ref = rest[-9:-4]
     *rest, final_ref, before_ref, face_ref, ratef_ref = rest[:-9]
@@ -592,17 +614,19 @@
 
 
 def near_kernel(
-    scal_ref, final_in, before_in, face_ref, ratef_ref, coded_ref, final_edge, before_edge, recv_ref
+    final_in, before_in, face_ref, ratef_ref, coded_ref, final_edge, before_edge, recv_ref
 ):
+    scal_ref = position()
     high = lax.rem(scal_ref[0] + scal_ref[2], 2) == 0
     edges = final_edge, before_edge
     corrected(scal_ref, final_in, before_in, face_ref, ratef_ref, coded_ref, recv_ref, high, edges)
 
 
 def far_kernel(
-    scal_ref, final_in, before_in, face_ref, ratef_ref, coded_ref, final_near, before_near,
+    final_in, before_in, face_ref, ratef_ref, coded_ref, final_near, before_near,
     final_ref, before_ref, recv_ref, final_edge, before_edge, sems,
 ):
+    scal_ref = position()
     size_x = final_in.shape[1]
     high = lax.rem(scal_ref[0] + scal_ref[2], 2) == 1
     copies = []
@@ -649,9 +673,6 @@
     rows = size_y + HALO
     per_dev, spectral = panels.shape[2], panels.shape[4]
     npanels = ny * per_dev
-    scal = jnp.stack(
-        [lax.axis_index("gx"), lax.axis_index("gy"), lax.axis_index("gz"), jnp.int32(nx), jnp.int32(ny)]
-    ).astype(jnp.int32)
 
     def swap(value):
         return send(value, sizes, lambda i, j, k: (i, j, 1 - k))
@@ -667,7 +688,6 @@
 
     assert per_dev == PANELS and size_z == LANES
     vmem = pl.BlockSpec(memory_space=pltpu.VMEM)
-    smem = pl.BlockSpec(memory_space=pltpu.SMEM)
     params = pltpu.CompilerParams(vmem_limit_bytes=48 * 1024 * 1024)
     table = jnp.asarray(wave_table(spectral, panels.shape[3]))
     width = table.shape[1]
@@ -675,18 +695,17 @@
     tiles = comps * size_x
     number = tiles + width // size_z * (per_dev // HALO)
     half = jax.ShapeDtypeStruct(coded_shape(number), jnp.int16)
-    ints, fields_own, mine, theirs = pl.pallas_call(
+    ints, fields_own, theirs = pl.pallas_call(
         prepare_kernel,
         out_shape=(
             jax.ShapeDtypeStruct((per_dev + extra_rows, width), F32),
             jax.ShapeDtypeStruct((2 * comps + 1,) + u_now.shape[1:], F32),
             half,
-            half,
         ),
-        in_specs=[smem] + [pl.BlockSpec(memory_space=pl.ANY)] * 10,
-        out_specs=(vmem,) * 4,
+        in_specs=[pl.BlockSpec(memory_space=pl.ANY)] * 10,
+        out_specs=(vmem,) * 3,
         scratch_shapes=[
-            pltpu.VMEM((2, number, HALO, size_z), F32),
+            pltpu.VMEM((number, HALO, size_z), F32),
             pltpu.VMEM((per_dev,) + panels.shape[3:], BF16),
             pltpu.VMEM(coupling.shape, F32),
             pltpu.VMEM(table.shape, BF16),
@@ -698,13 +717,22 @@
         ],
         compiler_params=params,
         name="prepare",
-    )(scal, *(
+    )(*(
         pltpu.with_memory_space_constraint(value, pltpu.HBM)
         for value in (
             panels.reshape((per_dev,) + panels.shape[3:]), coupling, table, layer_depth.reshape(1, -1),
             panel_owner.reshape(1, -1), panel_block.reshape(1, -1), layer_speed, u_now, u_prev, lateral,
         )
     ))
+    mine = pl.pallas_call(
+        mine_kernel,
+        out_shape=half,
+        in_specs=[vmem] * 2,
+        out_specs=vmem,
+        scratch_shapes=[pltpu.VMEM((number, HALO, size_z), F32)],
+        compiler_params=params,
+        name="mine",
+    )(fields_own, ints)
     both = jnp.stack([mine, swap(theirs)])
     ints, fields_own, both = lax.optimization_barrier((ints, fields_own, both))
     side = send(both, sizes, route_y)
@@ -717,11 +745,11 @@
             jax.ShapeDtypeStruct((2, 2 * npanels, size_z), F32),
             jax.ShapeDtypeStruct((2, size_x * rows, 2 * npanels), BF16),
         ),
-        in_specs=[smem] + [vmem] * 2,
+        in_specs=[vmem] * 2,
         out_specs=(vmem,) * 2,
         compiler_params=params,
         name="index",
-    )(scal, ints, ints_o)
+    )(ints, ints_o)
     sets = ()
     if ny == 4:
         forces = both[:, tiles // 2:]
@@ -732,8 +760,8 @@
         pair = jnp.where(lax.axis_index("gz") == 0, pair, pair[::-1])
         sets = (jnp.moveaxis(lax.all_gather(pair, "gy"), 0, 1).reshape(2, npanels, -1),)
     side, index, ints_o, fields_o = lax.optimization_barrier((side, index, ints_o, fields_o))
-    shared = (scal, fields_own, fields_o, ints, ints_o, *index, side, swap(side)) + sets
-    shared_specs = [smem] + [vmem] * (8 + len(sets))
+    shared = (fields_own, fields_o, ints, ints_o, *index, side, swap(side)) + sets
+    shared_specs = [vmem] * (8 + len(sets))
     tiles_scratch = pltpu.VMEM((2, number, HALO, size_z), F32)
     far_scratch = pltpu.VMEM((2, number - tiles, HALO, size_z), F32)
     all_scratch = pltpu.VMEM((2, npanels, width), F32)
@@ -776,11 +804,11 @@
     final, before, face, ratef, recv = lax.optimization_barrier((final, before, face, ratef, recv))
     recv_o = swap(recv)
     edges = [jax.ShapeDtypeStruct((comps, depth, size_y, size_z), F32) for depth in (NSTEP, NSTEP - 1)]
-    whole = (scal, final, before, face, ratef)
+    whole = (final, before, face, ratef)
     near = pl.pallas_call(
         near_kernel,
         out_shape=tuple(edges),
-        in_specs=[smem] + [vmem] * 5,
+        in_specs=[vmem] * 5,
         out_specs=(vmem, vmem),
         scratch_shapes=[face_scratch],
         compiler_params=params,
@@ -793,7 +821,7 @@
             jax.ShapeDtypeStruct(u_now.shape, F32),
             jax.ShapeDtypeStruct(u_now.shape, F32),
         ),
-        in_specs=[smem] + [vmem] * 7,
+        in_specs=[vmem] * 7,
         out_specs=(pl.BlockSpec(memory_space=pl.ANY),) * 2,
         scratch_shapes=[
             face_scratch,

time: 26.2 us -> 24.4 us (0.931)
  Pallas kernels: 11.9 us -> 9.1 us
  waiting for transfers between devices: 5.4 us -> 6.56 us
    ppermute x8, waiting for transfers between devices: 5.4 us -> 6.56 us  [send(): return lax.ppermute(value, ('gx', 'gy', 'gz'), pairs)]
    pallas_call x1, Pallas kernels: 2.53 us -> 1.9 us  [per_device(): pl.pallas_call(prepare_kernel, out_shape=(jax.ShapeDtypeStruct((per_dev +...]
    pallas_call x1, Pallas kernels: 0.69 us -> 0.15 us  [per_device(): pl.pallas_call(functools.partial(index_kernel, sizes=u_now.shape[1:], blo...]
    pallas_call x1, Pallas kernels: 1.77 us -> 1.23 us  [per_device(): pl.pallas_call(far_kernel, out_shape=(jax.ShapeDtypeStruct(u_now.shape, F...]
    pallas_call x1, Pallas kernels: 1.7 us -> 1.18 us  [per_device(): pl.pallas_call(face_kernel, out_shape=jax.ShapeDtypeStruct(coded_shape(2...]
    pallas_call x1, Pallas kernels: 4.12 us -> 3.83 us  [per_device(): pl.pallas_call(local_kernel, out_shape=(jax.ShapeDtypeStruct(u_now.shape,...]
    pallas_call x1 -> x2, Pallas kernels: 1.05 us -> 0.81 us  [the longest x1 0.51 us: per_device(): pl.pallas_call(near_kernel, out_shape=tuple(edges), in_specs=[vmem] * 5,...]
  transfers between devices with their start and end apart: 8 -> 8, of which waited for: 5 -> 5; matrix products, arithmetic and copies ran while one was open for 0% -> 0% of each run, Pallas kernels for 22% -> 20%
where the time goes in v6:
time: 24.4 us; the launch traced here: 24.3 us
  Pallas kernels  9.1 us (37%)
  starting transfers between devices  7.89 us (32%)
  waiting for transfers between devices  6.56 us (27%)
  between operations  0.7 us (3%)
    ppermute x8, starting transfers between devices, send(): return lax.ppermute(value, ('gx', 'gy', 'gz'), pairs)  7.89 us
    ppermute x8, waiting for transfers between devices, send(): return lax.ppermute(value, ('gx', 'gy', 'gz'), pairs)  6.56 us
    pallas_call x1, Pallas kernels, per_device(): pl.pallas_call(local_kernel, out_shape=(jax.ShapeDtypeStruct(u_now.shape,...  3.83 us
    pallas_call x1, Pallas kernels, per_device(): pl.pallas_call(prepare_kernel, out_shape=(jax.ShapeDtypeStruct((per_dev +...  1.9 us
    pallas_call x1, Pallas kernels, per_device(): pl.pallas_call(far_kernel, out_shape=(jax.ShapeDtypeStruct(u_now.shape, F...  1.23 us
    pallas_call x1, Pallas kernels, per_device(): pl.pallas_call(face_kernel, out_shape=jax.ShapeDtypeStruct(coded_shape(2...  1.18 us
    pallas_call x1, Pallas kernels, per_device(): pl.pallas_call(near_kernel, out_shape=tuple(edges), in_specs=[vmem] * 5,...  0.51 us
  transfers between devices with their start and end apart: 8, of which 5 were waited for; matrix products, arithmetic and copies ran while one was open for 0% of the time, Pallas kernels for 20%

profile of v6, /device:TPU:0, one launch (start us, length us, event | category | flops | bytes accessed | tf_op | source)
XLA Modules:
  0.0 24.3 jit_solution(209167747304371435)
XLA Ops:
  0.6 1.9 %prepare.1 = (f32[24,256]{1,0:T(8,128)S(1)}, f32[7,16,16,128]{3,2,1,0:T(8,128)S(1)}, s16[27,16,128]{2,1,0:T(8,128)(2,1)S(1)}) custom-call(bf16[16,48,256]{2,1,0:T(8,128)(2,1)} %bitcast.7, f32[3,16,16]{2,1,0:T(8,128)} %coupling_hbm.1, bf16[256,256]{1,0:T(8,128)(2,1)} %constant.2.clone.table_hbm, s32[1,128]{1,0:T(1,128)} %bitcast.9, s32[1,64]{1,0:T(1,128)} %bitcast.10, ...), custom_call_target="tpu_custom_call" | custom-call | tf_op jit(solution)/shard_map/prepare/pallas_call | solution.py:698
  2.5 0.5 %collective-permute-start = (s16[27,16,128]{2,1,0:T(8,128)(2,1)S(1)}, s16[27,16,128]{2,1,0:T(8,128)(2,1)S(1)}, u32[]{:S(2)}, u32[]{:S(2)}) collective-permute-start(s16[27,16,128]{2,1,0:T(8,128)(2,1)S(1)} %get-tuple-element.31), channel_id=1, source_target_pairs={{0,1},{1,0},{2,3},{3,2},{4,5},{5,4},{6,7},{7,6},{8,9},{9,8},{10,11... | collective-permute-start | bytes 331784 | tf_op jit(solution)/shard_map/ppermute | solution.py:658
  3.1 0.3 %mine.1 = s16[27,16,128]{2,1,0:T(8,128)(2,1)S(1)} custom-call(f32[7,16,16,128]{3,2,1,0:T(8,128)S(1)} %get-tuple-element.32.state_ref, f32[24,256]{1,0:T(8,128)S(1)} %get-tuple-element.34.force_ref.ints_ref), custom_call_target="tpu_custom_call" | custom-call | tf_op jit(solution)/shard_map/mine/pallas_call | solution.py:727
  3.4 0.7 %collective-permute-done = s16[27,16,128]{2,1,0:T(8,128)(2,1)S(1)} collective-permute-done((s16[27,16,128]{2,1,0:T(8,128)(2,1)S(1)}, s16[27,16,128]{2,1,0:T(8,128)(2,1)S(1)}, u32[]{:S(2)}, u32[]{:S(2)}) %collective-permute-start) | collective-permute-done | bytes 110624 | tf_op jit(solution)/shard_map/ppermute | solution.py:658
  4.1 0.4 %collective-permute-start.4 = (f32[7,16,16,128]{3,2,1,0:T(8,128)S(1)}, f32[7,16,16,128]{3,2,1,0:T(8,128)S(1)}, u32[]{:S(2)}, u32[]{:S(2)}) collective-permute-start(f32[7,16,16,128]{3,2,1,0:T(8,128)S(1)} %get-tuple-element.32.state_ref), channel_id=1, source_target_pairs={{0,1},{1,0},{2,3},{3,2},{4,5},{5,4},{6,7},{7,6},{8,9},{9,8},{10,11... | collective-permute-start | bytes 2752520 | tf_op jit(solution)/shard_map/ppermute | solution.py:658
  4.5 2.7 %collective-permute-start.1 = (s16[2,27,16,128]{3,2,1,0:T(8,128)(2,1)S(1)}, s16[2,27,16,128]{3,2,1,0:T(8,128)(2,1)S(1)}, u32[]{:S(2)}, u32[]{:S(2)}) collective-permute-start(s16[2,27,16,128]{3,2,1,0:T(8,128)(2,1)S(1)} %pad_add_fusion.1), channel_id=1, source_target_pairs={{0,2},{1,9},{2,0},{3,5},{4,6},{5,3},{6,4},{7,15},{8,10},{9,1},{10,... | collective-permute-start | bytes 663560 | tf_op jit(solution)/shard_map/ppermute | solution.py:658
  7.2 0.0 collective-permute-start.3
  7.2 2.6 %collective-permute-start.2 = (s16[2,3,16,128]{3,2,1,0:T(8,128)(2,1)S(1)}, s16[2,3,16,128]{3,2,1,0:T(8,128)(2,1)S(1)}, u32[]{:S(2)}, u32[]{:S(2)}) collective-permute-start(s16[2,3,16,128]{3,2,1,0:T(8,128)(2,1)S(1)} %slice.3), channel_id=1, source_target_pairs={{0,4},{1,7},{2,6},{3,5},{4,0},{5,3},{6,2},{7,1},{8,12},{9,15},{10,... | collective-permute-start | bytes 73736 | tf_op jit(solution)/shard_map/ppermute | solution.py:658
  9.8 0.0 collective-permute-done.3.intso_ref
  9.8 0.1 index.1
  9.9 2.5 %collective-permute-done.2 = s16[2,3,16,128]{3,2,1,0:T(8,128)(2,1)S(1)} collective-permute-done((s16[2,3,16,128]{3,2,1,0:T(8,128)(2,1)S(1)}, s16[2,3,16,128]{3,2,1,0:T(8,128)(2,1)S(1)}, u32[]{:S(2)}, u32[]{:S(2)}) %collective-permute-start.2) | collective-permute-done | bytes 24608 | tf_op jit(solution)/shard_map/ppermute | solution.py:658
  12.4 0.0 collective-permute-done.1
  12.4 0.0 collective-permute-done.4.stateo_ref
  12.5 0.1 collective-permute-start.5
  12.5 1.5 %collective-permute-done.5.codedo_ref = s16[2,30,16,128]{3,2,1,0:T(8,128)(2,1)S(1)} collective-permute-done((s16[2,30,16,128]{3,2,1,0:T(8,128)(2,1)S(1)}, s16[2,30,16,128]{3,2,1,0:T(8,128)(2,1)S(1)}, u32[]{:S(2)}, u32[]{:S(2)}) %collective-permute-start.5) | collective-permute-done | bytes 245792 | tf_op jit(solution)/shard_map/ppermute | solution.py:658
  14.0 1.2 %face.1 = s16[34,16,128]{2,1,0:T(8,128)(2,1)S(1)} custom-call(f32[7,16,16,128]{3,2,1,0:T(8,128)S(1)} %get-tuple-element.32.state_ref, f32[7,16,16,128]{3,2,1,0:T(8,128)S(1)} %collective-permute-done.4.stateo_ref, f32[24,256]{1,0:T(8,128)S(1)} %get-tuple-element.34.force_ref.ints_ref, f32[24,256]{1,0:T(8,128)S(1)} %collective-permute-done.3.intso_ref, ...), custom_call_target="tpu_custom_call" | custom-call | tf_op jit(solution)/shard_map/face/pallas_call | solution.py:770
  15.2 1.6 %collective-permute-start.6 = (s16[34,16,128]{2,1,0:T(8,128)(2,1)S(1)}, s16[34,16,128]{2,1,0:T(8,128)(2,1)S(1)}, u32[]{:S(2)}, u32[]{:S(2)}) collective-permute-start(s16[34,16,128]{2,1,0:T(8,128)(2,1)S(1)} %face.1), channel_id=1, source_target_pairs={{0,8},{1,25},{2,10},{3,27},{4,12},{5,29},{6,14},{7,31},{8,0},{9,17... | collective-permute-start | bytes 417800 | tf_op jit(solution)/shard_map/ppermute | solution.py:658
  16.8 3.8 %local.1 = (f32[3,16,16,128]{3,2,1,0:T(8,128)S(1)}, f32[3,16,16,128]{3,2,1,0:T(8,128)S(1)}, f32[2,2,12,24,128]{4,3,2,1,0:T(8,128)S(1)}, f32[2,2,4,24,128]{4,3,2,1,0:T(8,128)S(1)}) custom-call(f32[7,16,16,128]{3,2,1,0:T(8,128)S(1)} %get-tuple-element.32.state_ref, f32[7,16,16,128]{3,2,1,0:T(8,128)S(1)} %collective-permute-done.4.stateo_ref, ...), custom_call_target="tpu_custom_call" | custom-call | tf_op jit(solution)/shard_map/local/pallas_call | solution.py:780
  20.6 1.1 %collective-permute-done.6.coded_ref = s16[34,16,128]{2,1,0:T(8,128)(2,1)S(1)} collective-permute-done((s16[34,16,128]{2,1,0:T(8,128)(2,1)S(1)}, s16[34,16,128]{2,1,0:T(8,128)(2,1)S(1)}, u32[]{:S(2)}, u32[]{:S(2)}) %collective-permute-start.6) | collective-permute-done | bytes 139296 | tf_op jit(solution)/shard_map/ppermute | solution.py:658
  21.7 0.0 collective-permute-start.7
  21.7 0.5 %near.1 = (f32[3,4,16,128]{3,2,1,0:T(8,128)S(1)}, f32[3,3,16,128]{3,2,1,0:T(8,128)S(1)}) custom-call(f32[3,16,16,128]{3,2,1,0:T(8,128)S(1)} %get-tuple-element.46.final_in, f32[3,16,16,128]{3,2,1,0:T(8,128)S(1)} %get-tuple-element.47.before_in, f32[2,2,12,24,128]{4,3,2,1,0:T(8,128)S(1)} %get-tuple-element.48.face_ref, ...), custom_call_target="tpu_custom_call" | custom-call | tf_op jit(solution)/shard_map/near/pallas_call | solution.py:808
  22.2 0.8 %collective-permute-done.7.coded_ref = s16[34,16,128]{2,1,0:T(8,128)(2,1)S(1)} collective-permute-done((s16[34,16,128]{2,1,0:T(8,128)(2,1)S(1)}, s16[34,16,128]{2,1,0:T(8,128)(2,1)S(1)}, u32[]{:S(2)}, u32[]{:S(2)}) %collective-permute-start.7) | collective-permute-done | bytes 139296 | tf_op jit(solution)/shard_map/ppermute | solution.py:658
  23.1 1.2 %far.1 = (f32[3,16,16,128]{3,2,1,0:T(8,128)}, f32[3,16,16,128]{3,2,1,0:T(8,128)}) custom-call(f32[3,16,16,128]{3,2,1,0:T(8,128)S(1)} %get-tuple-element.46.final_in, f32[3,16,16,128]{3,2,1,0:T(8,128)S(1)} %get-tuple-element.47.before_in, f32[2,2,12,24,128]{4,3,2,1,0:T(8,128)S(1)} %get-tuple-element.48.face_ref, ...), custom_call_target="tpu_custom_call" | custom-call | tf_op jit(solution)/shard_map/far/pallas_call | solution.py:818
  (3 shorter events, 0.0 us)
Async XLA Ops:
  2.5 1.5 %collective-permute-start = (s16[27,16,128]{2,1,0:T(8,128)(2,1)S(1)}, s16[27,16,128]{2,1,0:T(8,128)(2,1)S(1)}, u32[]{:S(2)}, u32[]{:S(2)}) collective-permute-start(s16[27,16,128]{2,1,0:T(8,128)(2,1)S(1)} %get-tuple-element.31), channel_id=1, source_target_pairs={{0,1},{1,0},{2,3},{3,2},{4,5},{5,4},{6,7},{7,6},{8,9},{9,8},{10,11... | collective-permute-start | bytes 331784 | tf_op jit(solution)/shard_map/ppermute | solution.py:658
  4.1 8.4 %collective-permute-start.4 = (f32[7,16,16,128]{3,2,1,0:T(8,128)S(1)}, f32[7,16,16,128]{3,2,1,0:T(8,128)S(1)}, u32[]{:S(2)}, u32[]{:S(2)}) collective-permute-start(f32[7,16,16,128]{3,2,1,0:T(8,128)S(1)} %get-tuple-element.32.state_ref), channel_id=1, source_target_pairs={{0,1},{1,0},{2,3},{3,2},{4,5},{5,4},{6,7},{7,6},{8,9},{9,8},{10,11... | collective-permute-start | bytes 2752520 | tf_op jit(solution)/shard_map/ppermute | solution.py:658
  4.5 8.0 %collective-permute-start.1 = (s16[2,27,16,128]{3,2,1,0:T(8,128)(2,1)S(1)}, s16[2,27,16,128]{3,2,1,0:T(8,128)(2,1)S(1)}, u32[]{:S(2)}, u32[]{:S(2)}) collective-permute-start(s16[2,27,16,128]{3,2,1,0:T(8,128)(2,1)S(1)} %pad_add_fusion.1), channel_id=1, source_target_pairs={{0,2},{1,9},{2,0},{3,5},{4,6},{5,3},{6,4},{7,15},{8,10},{9,1},{10,... | collective-permute-start | bytes 663560 | tf_op jit(solution)/shard_map/ppermute | solution.py:658
  7.2 2.6 %collective-permute-start.3 = (f32[24,256]{1,0:T(8,128)S(1)}, f32[24,256]{1,0:T(8,128)S(1)}, u32[]{:S(2)}, u32[]{:S(2)}) collective-permute-start(f32[24,256]{1,0:T(8,128)S(1)} %get-tuple-element.34.force_ref.ints_ref), channel_id=1, source_target_pairs={{0,1},{1,0},{2,3},{3,2},{4,5},{5,4},{6,7},{7,6},{8,9},{9,8},{10,11... | collective-permute-start | bytes 73736 | tf_op jit(solution)/shard_map/ppermute | solution.py:658
  7.2 5.2 %collective-permute-start.2 = (s16[2,3,16,128]{3,2,1,0:T(8,128)(2,1)S(1)}, s16[2,3,16,128]{3,2,1,0:T(8,128)(2,1)S(1)}, u32[]{:S(2)}, u32[]{:S(2)}) collective-permute-start(s16[2,3,16,128]{3,2,1,0:T(8,128)(2,1)S(1)} %slice.3), channel_id=1, source_target_pairs={{0,4},{1,7},{2,6},{3,5},{4,0},{5,3},{6,2},{7,1},{8,12},{9,15},{10,... | collective-permute-start | bytes 73736 | tf_op jit(solution)/shard_map/ppermute | solution.py:658
  12.5 1.6 %collective-permute-start.5 = (s16[2,30,16,128]{3,2,1,0:T(8,128)(2,1)S(1)}, s16[2,30,16,128]{3,2,1,0:T(8,128)(2,1)S(1)}, u32[]{:S(2)}, u32[]{:S(2)}) collective-permute-start(s16[2,30,16,128]{3,2,1,0:T(8,128)(2,1)S(1)} %pad_add_fusion.coded_ref), channel_id=1, source_target_pairs={{0,1},{1,0},{2,3},{3,2},{4,5},{5,4},{6,7},{7,6},{8,9},{9,8},{10,11... | collective-permute-start | bytes 737288 | tf_op jit(solution)/shard_map/ppermute | solution.py:658
  15.2 6.5 %collective-permute-start.6 = (s16[34,16,128]{2,1,0:T(8,128)(2,1)S(1)}, s16[34,16,128]{2,1,0:T(8,128)(2,1)S(1)}, u32[]{:S(2)}, u32[]{:S(2)}) collective-permute-start(s16[34,16,128]{2,1,0:T(8,128)(2,1)S(1)} %face.1), channel_id=1, source_target_pairs={{0,8},{1,25},{2,10},{3,27},{4,12},{5,29},{6,14},{7,31},{8,0},{9,17... | collective-permute-start | bytes 417800 | tf_op jit(solution)/shard_map/ppermute | solution.py:658
  21.7 1.4 %collective-permute-start.7 = (s16[34,16,128]{2,1,0:T(8,128)(2,1)S(1)}, s16[34,16,128]{2,1,0:T(8,128)(2,1)S(1)}, u32[]{:S(2)}, u32[]{:S(2)}) collective-permute-start(s16[34,16,128]{2,1,0:T(8,128)(2,1)S(1)} %collective-permute-done.6.coded_ref), channel_id=1, source_target_pairs={{0,1},{1,0},{2,3},{3,2},{4,5},{5,4},{6,7},{7,6},{8,9},{9,8},{10,11... | collective-permute-start | bytes 417800 | tf_op jit(solution)/shard_map/ppermute | solution.py:658

commit v7 on v6

--- a/solution.py
+++ b/solution.py
@@ -65,7 +65,7 @@
     return jnp.exp2(exponents) * (1.0 / TOP)
 
 
-def quantize(load, groups, out_ref):
+def quantize(load, groups, out_ref, spare=None):
     shape = (HALO, LANES)
     lane = iota(shape, 1)
     peak = jnp.zeros(shape, F32)
@@ -78,7 +78,11 @@
     zero = jnp.zeros(shape, jnp.int32)
     wide = [jnp.broadcast_to(factor[:, g:g + 1], shape) for g in range(max(groups) + 1)]
     parts = [jnp.round(load(t) * wide[of]).astype(jnp.int32) for t, of in enumerate(groups)]
-    parts += [zero] * (len(groups) % 2) + [exponents.astype(jnp.int32), zero]
+    if spare is None:
+        parts += [zero] * (len(groups) % 2) + [exponents.astype(jnp.int32), zero]
+    else:
+        moved = pltpu.roll(exponents, LANES // 2, 1).astype(jnp.int32)
+        parts[spare] = jnp.where(lane < LANES // 2, parts[spare], moved)
     for i in range(out_ref.shape[0]):
         out_ref[i] = jnp.concatenate(parts[2 * i:2 * i + 2], axis=0).astype(jnp.int16)
 
@@ -88,7 +92,7 @@
 
 
 def side_groups(comps, size_x, rest):
-    near = [c * (size_x // NSTEP) + x // NSTEP for c in range(comps) for x in range(size_x)]
+    near = [x // NSTEP for c in range(comps) for x in range(size_x)]
     return near + [max(near) + 1 + i for i in range(rest)]
 
 
@@ -124,11 +128,12 @@
         def store_far(t, value):
             far_ref[z, t] = value
 
-        scales = scales_of(ref[half, last])
+        scales = pltpu.roll(scales_of(ref[half, last - 1]), LANES // 2, 1)
         for moved, blocks in choose(scales):
             expand(lambda i: ref[half, i], store, moved, blocks)
-        if ref.shape[1] > last + 1:
-            expand(lambda i: ref[half, last + 1 + i], store_far, scales_of(ref[half, ref.shape[1] - 1]), [
+        if ref.shape[1] > last:
+            scales = pltpu.roll(scales_of(ref[half, ref.shape[1] - 1]), LANES // 2, 1)
+            expand(lambda i: ref[half, last + i], store_far, scales, [
                 ((t - forces) // 2, groups[t], groups[t + 1]) for t in range(forces, len(groups), 2)
             ])
 
@@ -221,7 +226,7 @@
             at = comps * size_x + part * (count // HALO) + piece
             tiles_ref[at] = force_ref[piece * HALO:(piece + 1) * HALO, part * size_z:(part + 1) * size_z]
     groups = side_groups(comps, size_x, tiles_ref.shape[0] - comps * size_x)
-    quantize(lambda t: tiles_ref[t], groups, coded_ref)
+    quantize(lambda t: tiles_ref[t], groups, coded_ref, len(groups) - 2)
 
 
 def listed(ref, panels, which):
@@ -449,10 +454,9 @@
 def face_groups(comps):
     groups = []
     for z in range(2):
-        base = z * (2 * NSTEP + 5)
-        groups += [base + 2 * n + half for n in range(NSTEP) for _ in range(comps) for half in range(2)]
-        groups += [base + 2 * NSTEP + half for _ in range(2) for half in range(2)]
-        groups += [base + 2 * NSTEP + 2] * comps + [base + 2 * NSTEP + 3, base + 2 * NSTEP + 4]
+        base = z * (NSTEP + 3)
+        groups += [base + n for n in range(NSTEP) for _ in range(2 * comps)]
+        groups += [base + NSTEP] * 4 + [base + NSTEP + 1] * comps + [base + NSTEP + 2] * 2
     return groups
 
 
@@ -694,7 +698,8 @@
     extra_rows = -(-(LANES + 4 * npanels) // (8 * width)) * 8
     tiles = comps * size_x
     number = tiles + width // size_z * (per_dev // HALO)
-    half = jax.ShapeDtypeStruct(coded_shape(number), jnp.int16)
+    assert number - tiles == 4 and NSTEP * panels.shape[3] + LANES // 2 <= width
+    half = jax.ShapeDtypeStruct((number // 2, 2 * HALO, LANES), jnp.int16)
     ints, fields_own, theirs = pl.pallas_call(
         prepare_kernel,
         out_shape=(

time: 24.4 us -> 24 us (0.984)
  waiting for transfers between devices: 6.56 us -> 5.94 us
    ppermute x8, waiting for transfers between devices: 6.56 us -> 5.94 us  [send(): return lax.ppermute(value, ('gx', 'gy', 'gz'), pairs)]
where the time goes in v7:
time: 24 us; the launch traced here: 23.8 us
  Pallas kernels  9.09 us (38%)
  starting transfers between devices  8.06 us (34%)
  waiting for transfers between devices  5.94 us (25%)
  between operations  0.7 us (3%)
    ppermute x8, starting transfers between devices, send(): return lax.ppermute(value, ('gx', 'gy', 'gz'), pairs)  8.06 us
    ppermute x8, waiting for transfers between devices, send(): return lax.ppermute(value, ('gx', 'gy', 'gz'), pairs)  5.94 us
    pallas_call x1, Pallas kernels, per_device(): pl.pallas_call(local_kernel, out_shape=(jax.ShapeDtypeStruct(u_now.shape,...  3.96 us
    pallas_call x1, Pallas kernels, per_device(): pl.pallas_call(prepare_kernel, out_shape=(jax.ShapeDtypeStruct((per_dev +...  1.85 us
    pallas_call x1, Pallas kernels, per_device(): pl.pallas_call(far_kernel, out_shape=(jax.ShapeDtypeStruct(u_now.shape, F...  1.21 us
    pallas_call x1, Pallas kernels, per_device(): pl.pallas_call(face_kernel, out_shape=jax.ShapeDtypeStruct(coded_shape(2...  1.19 us
    pallas_call x1, Pallas kernels, per_device(): pl.pallas_call(near_kernel, out_shape=tuple(edges), in_specs=[vmem] * 5,...  0.49 us
  transfers between devices with their start and end apart: 8, of which 5 were waited for; matrix products, arithmetic and copies ran while one was open for 0% of the time, Pallas kernels for 20%

profile of v7, /device:TPU:0, one launch (start us, length us, event | category | flops | bytes accessed | tf_op | source)
XLA Modules:
  0.0 23.8 jit_solution(2956744006381315419)
XLA Ops:
  0.6 1.9 %prepare.1 = (f32[24,256]{1,0:T(8,128)S(1)}, f32[7,16,16,128]{3,2,1,0:T(8,128)S(1)}, s16[26,16,128]{2,1,0:T(8,128)(2,1)S(1)}) custom-call(bf16[16,48,256]{2,1,0:T(8,128)(2,1)} %bitcast.7, f32[3,16,16]{2,1,0:T(8,128)} %coupling_hbm.1, bf16[256,256]{1,0:T(8,128)(2,1)} %constant.2.clone.table_hbm, s32[1,128]{1,0:T(1,128)} %bitcast.9, s32[1,64]{1,0:T(1,128)} %bitcast.10, ...), custom_call_target="tpu_custom_call" | custom-call | tf_op jit(solution)/shard_map/prepare/pallas_call | solution.py:703
  2.5 0.5 %collective-permute-start = (s16[26,16,128]{2,1,0:T(8,128)(2,1)S(1)}, s16[26,16,128]{2,1,0:T(8,128)(2,1)S(1)}, u32[]{:S(2)}, u32[]{:S(2)}) collective-permute-start(s16[26,16,128]{2,1,0:T(8,128)(2,1)S(1)} %get-tuple-element.31), channel_id=1, source_target_pairs={{0,1},{1,0},{2,3},{3,2},{4,5},{5,4},{6,7},{7,6},{8,9},{9,8},{10,11... | collective-permute-start | bytes 319496 | tf_op jit(solution)/shard_map/ppermute | solution.py:662
  3.0 0.2 %mine.1 = s16[26,16,128]{2,1,0:T(8,128)(2,1)S(1)} custom-call(f32[7,16,16,128]{3,2,1,0:T(8,128)S(1)} %get-tuple-element.32.state_ref, f32[24,256]{1,0:T(8,128)S(1)} %get-tuple-element.34.force_ref.ints_ref), custom_call_target="tpu_custom_call" | custom-call | tf_op jit(solution)/shard_map/mine/pallas_call | solution.py:732
  3.3 0.7 %collective-permute-done = s16[26,16,128]{2,1,0:T(8,128)(2,1)S(1)} collective-permute-done((s16[26,16,128]{2,1,0:T(8,128)(2,1)S(1)}, s16[26,16,128]{2,1,0:T(8,128)(2,1)S(1)}, u32[]{:S(2)}, u32[]{:S(2)}) %collective-permute-start) | collective-permute-done | bytes 106528 | tf_op jit(solution)/shard_map/ppermute | solution.py:662
  4.0 0.4 %collective-permute-start.4 = (f32[7,16,16,128]{3,2,1,0:T(8,128)S(1)}, f32[7,16,16,128]{3,2,1,0:T(8,128)S(1)}, u32[]{:S(2)}, u32[]{:S(2)}) collective-permute-start(f32[7,16,16,128]{3,2,1,0:T(8,128)S(1)} %get-tuple-element.32.state_ref), channel_id=1, source_target_pairs={{0,1},{1,0},{2,3},{3,2},{4,5},{5,4},{6,7},{7,6},{8,9},{9,8},{10,11... | collective-permute-start | bytes 2752520 | tf_op jit(solution)/shard_map/ppermute | solution.py:662
  4.4 2.7 %collective-permute-start.1 = (s16[2,26,16,128]{3,2,1,0:T(8,128)(2,1)S(1)}, s16[2,26,16,128]{3,2,1,0:T(8,128)(2,1)S(1)}, u32[]{:S(2)}, u32[]{:S(2)}) collective-permute-start(s16[2,26,16,128]{3,2,1,0:T(8,128)(2,1)S(1)} %pad_add_fusion.1), channel_id=1, source_target_pairs={{0,2},{1,9},{2,0},{3,5},{4,6},{5,3},{6,4},{7,15},{8,10},{9,1},{10,... | collective-permute-start | bytes 638984 | tf_op jit(solution)/shard_map/ppermute | solution.py:662
  7.1 0.0 collective-permute-start.3
  7.1 2.6 %collective-permute-start.2 = (s16[2,2,16,128]{3,2,1,0:T(8,128)(2,1)S(1)}, s16[2,2,16,128]{3,2,1,0:T(8,128)(2,1)S(1)}, u32[]{:S(2)}, u32[]{:S(2)}) collective-permute-start(s16[2,2,16,128]{3,2,1,0:T(8,128)(2,1)S(1)} %slice.3), channel_id=1, source_target_pairs={{0,4},{1,7},{2,6},{3,5},{4,0},{5,3},{6,2},{7,1},{8,12},{9,15},{10,... | collective-permute-start | bytes 49160 | tf_op jit(solution)/shard_map/ppermute | solution.py:662
  9.7 0.0 collective-permute-done.3.intso_ref
  9.7 0.1 index.1
  9.9 2.1 %collective-permute-done.2 = s16[2,2,16,128]{3,2,1,0:T(8,128)(2,1)S(1)} collective-permute-done((s16[2,2,16,128]{3,2,1,0:T(8,128)(2,1)S(1)}, s16[2,2,16,128]{3,2,1,0:T(8,128)(2,1)S(1)}, u32[]{:S(2)}, u32[]{:S(2)}) %collective-permute-start.2) | collective-permute-done | bytes 16416 | tf_op jit(solution)/shard_map/ppermute | solution.py:662
  12.0 0.0 collective-permute-done.1
  12.0 0.0 collective-permute-done.4.stateo_ref
  12.1 0.2 collective-permute-start.5
  12.3 1.3 %collective-permute-done.5.codedo_ref = s16[2,28,16,128]{3,2,1,0:T(8,128)(2,1)S(1)} collective-permute-done((s16[2,28,16,128]{3,2,1,0:T(8,128)(2,1)S(1)}, s16[2,28,16,128]{3,2,1,0:T(8,128)(2,1)S(1)}, u32[]{:S(2)}, u32[]{:S(2)}) %collective-permute-start.5) | collective-permute-done | bytes 229408 | tf_op jit(solution)/shard_map/ppermute | solution.py:662
  13.6 1.2 %face.1 = s16[34,16,128]{2,1,0:T(8,128)(2,1)S(1)} custom-call(f32[7,16,16,128]{3,2,1,0:T(8,128)S(1)} %get-tuple-element.32.state_ref, f32[7,16,16,128]{3,2,1,0:T(8,128)S(1)} %collective-permute-done.4.stateo_ref, f32[24,256]{1,0:T(8,128)S(1)} %get-tuple-element.34.force_ref.ints_ref, f32[24,256]{1,0:T(8,128)S(1)} %collective-permute-done.3.intso_ref, ...), custom_call_target="tpu_custom_call" | custom-call | tf_op jit(solution)/shard_map/face/pallas_call | solution.py:775
  14.8 1.6 %collective-permute-start.6 = (s16[34,16,128]{2,1,0:T(8,128)(2,1)S(1)}, s16[34,16,128]{2,1,0:T(8,128)(2,1)S(1)}, u32[]{:S(2)}, u32[]{:S(2)}) collective-permute-start(s16[34,16,128]{2,1,0:T(8,128)(2,1)S(1)} %face.1), channel_id=1, source_target_pairs={{0,8},{1,25},{2,10},{3,27},{4,12},{5,29},{6,14},{7,31},{8,0},{9,17... | collective-permute-start | bytes 417800 | tf_op jit(solution)/shard_map/ppermute | solution.py:662
  16.4 4.0 %local.1 = (f32[3,16,16,128]{3,2,1,0:T(8,128)S(1)}, f32[3,16,16,128]{3,2,1,0:T(8,128)S(1)}, f32[2,2,12,24,128]{4,3,2,1,0:T(8,128)S(1)}, f32[2,2,4,24,128]{4,3,2,1,0:T(8,128)S(1)}) custom-call(f32[7,16,16,128]{3,2,1,0:T(8,128)S(1)} %get-tuple-element.32.state_ref, f32[7,16,16,128]{3,2,1,0:T(8,128)S(1)} %collective-permute-done.4.stateo_ref, ...), custom_call_target="tpu_custom_call" | custom-call | tf_op jit(solution)/shard_map/local/pallas_call | solution.py:785
  20.3 0.9 %collective-permute-done.6.coded_ref = s16[34,16,128]{2,1,0:T(8,128)(2,1)S(1)} collective-permute-done((s16[34,16,128]{2,1,0:T(8,128)(2,1)S(1)}, s16[34,16,128]{2,1,0:T(8,128)(2,1)S(1)}, u32[]{:S(2)}, u32[]{:S(2)}) %collective-permute-start.6) | collective-permute-done | bytes 139296 | tf_op jit(solution)/shard_map/ppermute | solution.py:662
  21.3 0.0 collective-permute-start.7
  21.3 0.5 %near.1 = (f32[3,4,16,128]{3,2,1,0:T(8,128)S(1)}, f32[3,3,16,128]{3,2,1,0:T(8,128)S(1)}) custom-call(f32[3,16,16,128]{3,2,1,0:T(8,128)S(1)} %get-tuple-element.46.final_in, f32[3,16,16,128]{3,2,1,0:T(8,128)S(1)} %get-tuple-element.47.before_in, f32[2,2,12,24,128]{4,3,2,1,0:T(8,128)S(1)} %get-tuple-element.48.face_ref, ...), custom_call_target="tpu_custom_call" | custom-call | tf_op jit(solution)/shard_map/near/pallas_call | solution.py:813
  21.8 0.9 %collective-permute-done.7.coded_ref = s16[34,16,128]{2,1,0:T(8,128)(2,1)S(1)} collective-permute-done((s16[34,16,128]{2,1,0:T(8,128)(2,1)S(1)}, s16[34,16,128]{2,1,0:T(8,128)(2,1)S(1)}, u32[]{:S(2)}, u32[]{:S(2)}) %collective-permute-start.7) | collective-permute-done | bytes 139296 | tf_op jit(solution)/shard_map/ppermute | solution.py:662
  22.6 1.2 %far.1 = (f32[3,16,16,128]{3,2,1,0:T(8,128)}, f32[3,16,16,128]{3,2,1,0:T(8,128)}) custom-call(f32[3,16,16,128]{3,2,1,0:T(8,128)S(1)} %get-tuple-element.46.final_in, f32[3,16,16,128]{3,2,1,0:T(8,128)S(1)} %get-tuple-element.47.before_in, f32[2,2,12,24,128]{4,3,2,1,0:T(8,128)S(1)} %get-tuple-element.48.face_ref, ...), custom_call_target="tpu_custom_call" | custom-call | tf_op jit(solution)/shard_map/far/pallas_call | solution.py:823
  (3 shorter events, 0.0 us)
Async XLA Ops:
  2.5 1.5 %collective-permute-start = (s16[26,16,128]{2,1,0:T(8,128)(2,1)S(1)}, s16[26,16,128]{2,1,0:T(8,128)(2,1)S(1)}, u32[]{:S(2)}, u32[]{:S(2)}) collective-permute-start(s16[26,16,128]{2,1,0:T(8,128)(2,1)S(1)} %get-tuple-element.31), channel_id=1, source_target_pairs={{0,1},{1,0},{2,3},{3,2},{4,5},{5,4},{6,7},{7,6},{8,9},{9,8},{10,11... | collective-permute-start | bytes 319496 | tf_op jit(solution)/shard_map/ppermute | solution.py:662
  4.0 8.1 %collective-permute-start.4 = (f32[7,16,16,128]{3,2,1,0:T(8,128)S(1)}, f32[7,16,16,128]{3,2,1,0:T(8,128)S(1)}, u32[]{:S(2)}, u32[]{:S(2)}) collective-permute-start(f32[7,16,16,128]{3,2,1,0:T(8,128)S(1)} %get-tuple-element.32.state_ref), channel_id=1, source_target_pairs={{0,1},{1,0},{2,3},{3,2},{4,5},{5,4},{6,7},{7,6},{8,9},{9,8},{10,11... | collective-permute-start | bytes 2752520 | tf_op jit(solution)/shard_map/ppermute | solution.py:662
  4.4 7.6 %collective-permute-start.1 = (s16[2,26,16,128]{3,2,1,0:T(8,128)(2,1)S(1)}, s16[2,26,16,128]{3,2,1,0:T(8,128)(2,1)S(1)}, u32[]{:S(2)}, u32[]{:S(2)}) collective-permute-start(s16[2,26,16,128]{3,2,1,0:T(8,128)(2,1)S(1)} %pad_add_fusion.1), channel_id=1, source_target_pairs={{0,2},{1,9},{2,0},{3,5},{4,6},{5,3},{6,4},{7,15},{8,10},{9,1},{10,... | collective-permute-start | bytes 638984 | tf_op jit(solution)/shard_map/ppermute | solution.py:662
  7.1 2.6 %collective-permute-start.3 = (f32[24,256]{1,0:T(8,128)S(1)}, f32[24,256]{1,0:T(8,128)S(1)}, u32[]{:S(2)}, u32[]{:S(2)}) collective-permute-start(f32[24,256]{1,0:T(8,128)S(1)} %get-tuple-element.34.force_ref.ints_ref), channel_id=1, source_target_pairs={{0,1},{1,0},{2,3},{3,2},{4,5},{5,4},{6,7},{7,6},{8,9},{9,8},{10,11... | collective-permute-start | bytes 73736 | tf_op jit(solution)/shard_map/ppermute | solution.py:662
  7.1 4.9 %collective-permute-start.2 = (s16[2,2,16,128]{3,2,1,0:T(8,128)(2,1)S(1)}, s16[2,2,16,128]{3,2,1,0:T(8,128)(2,1)S(1)}, u32[]{:S(2)}, u32[]{:S(2)}) collective-permute-start(s16[2,2,16,128]{3,2,1,0:T(8,128)(2,1)S(1)} %slice.3), channel_id=1, source_target_pairs={{0,4},{1,7},{2,6},{3,5},{4,0},{5,3},{6,2},{7,1},{8,12},{9,15},{10,... | collective-permute-start | bytes 49160 | tf_op jit(solution)/shard_map/ppermute | solution.py:662
  12.1 1.6 %collective-permute-start.5 = (s16[2,28,16,128]{3,2,1,0:T(8,128)(2,1)S(1)}, s16[2,28,16,128]{3,2,1,0:T(8,128)(2,1)S(1)}, u32[]{:S(2)}, u32[]{:S(2)}) collective-permute-start(s16[2,28,16,128]{3,2,1,0:T(8,128)(2,1)S(1)} %pad_add_fusion.coded_ref), channel_id=1, source_target_pairs={{0,1},{1,0},{2,3},{3,2},{4,5},{5,4},{6,7},{7,6},{8,9},{9,8},{10,11... | collective-permute-start | bytes 688136 | tf_op jit(solution)/shard_map/ppermute | solution.py:662
  14.8 6.4 %collective-permute-start.6 = (s16[34,16,128]{2,1,0:T(8,128)(2,1)S(1)}, s16[34,16,128]{2,1,0:T(8,128)(2,1)S(1)}, u32[]{:S(2)}, u32[]{:S(2)}) collective-permute-start(s16[34,16,128]{2,1,0:T(8,128)(2,1)S(1)} %face.1), channel_id=1, source_target_pairs={{0,8},{1,25},{2,10},{3,27},{4,12},{5,29},{6,14},{7,31},{8,0},{9,17... | collective-permute-start | bytes 417800 | tf_op jit(solution)/shard_map/ppermute | solution.py:662
  21.3 1.4 %collective-permute-start.7 = (s16[34,16,128]{2,1,0:T(8,128)(2,1)S(1)}, s16[34,16,128]{2,1,0:T(8,128)(2,1)S(1)}, u32[]{:S(2)}, u32[]{:S(2)}) collective-permute-start(s16[34,16,128]{2,1,0:T(8,128)(2,1)S(1)} %collective-permute-done.6.coded_ref), channel_id=1, source_target_pairs={{0,1},{1,0},{2,3},{3,2},{4,5},{5,4},{6,7},{7,6},{8,9},{9,8},{10,11... | collective-permute-start | bytes 417800 | tf_op jit(solution)/shard_map/ppermute | solution.py:662
